TPU v7x, 32 devices: a whole 2x2x4 slice. The times are simulated.
32 devices in a mesh: groups: 2 (over x), ctx: 16 (over z, y, core).
Axes of the slice: x: 2, y: 2, z: 4, core: 2. Of those that a mesh axis runs over, the one named last changes fastest.
Arguments:
- query: bfloat16 [8192, 1024], P(('groups', 'ctx')), parts along dimension 0, may hold values from -130 to 130, as said below
- key: bfloat16 [8192, 1024], P(('groups', 'ctx')), parts along dimension 0, may hold values from -4.5 to 4.5
- value: bfloat16 [8192, 1024], P(('groups', 'ctx')), parts along dimension 0, may hold values from -6 to 6
- cotangent: bfloat16 [8192, 1024], P(('groups', 'ctx')), parts along dimension 0, may hold values from -6 to 6
- global_ids: int32 [4], P('groups'), parts along dimension 0, may hold values from 0 to 63
- rand_owner: int32 [128, 6], P('groups'), parts along dimension 0, may hold values from 0 to 15, all different within a row; in each aligned block of 4 rows (0 to 3, 4 to 7, ...) at most 2 rows name the same one
- rand_local: int32 [128, 6], P('groups'), parts along dimension 0, may hold values from 0 to 3
Outputs:
- attended: bfloat16 [8192, 1024], P(('groups', 'ctx')), parts along dimension 0
- grad_query: bfloat16 [8192, 1024], P(('groups', 'ctx')), parts along dimension 0
- grad_key: bfloat16 [8192, 1024], P(('groups', 'ctx')), parts along dimension 0
- grad_value: bfloat16 [8192, 1024], P(('groups', 'ctx')), parts along dimension 0
There are 2 independent parts, one for each index of `groups`. A program takes and returns all parts, laid end to end along the dimension named above; each array names one. Nothing has to cross between parts.
Inputs may be any that keep to these rules, and one draw needn't show every extreme that they name: query and key are drawn together. `rand_owner`: each row names 6 different devices. In the 4 rows of one device no device is named more than 2 times, and in some device's rows some device is named exactly 2 times.
All inputs are finite; a program needn't handle non-finite values.
Results may differ from a plain program's by a relative error of at most 0.017.
Values may be sent and summed in bfloat16 or wider, within the bound.
No kernel may reach another device: no remote copies, remote signals or barrier semaphores. Data moves between devices by JAX's collectives and lax.ppermute only.
A program may use at most 192 MiB of HBM per device.

v0:
```python
import jax
import jax.numpy as jnp
from jax import lax
from jax.sharding import PartitionSpec as P

HEAD_DIM = 64
GROUP_HEADS = 8
BLOCK = 64
GLOBALS = 2
ROUNDS = 3


NEG_FILL = -1e30


def padded_2(block, sides, width):
    for axis, dim in sides:
        count = lax.axis_size(axis)
        forward = [(i, i + 1) for i in range(count - 1)]
        backward = [(target, source) for source, target in forward]
        low = lax.ppermute(
            lax.slice_in_dim(block, block.shape[dim] - width, None, axis=dim), axis, forward
        )
        high = lax.ppermute(lax.slice_in_dim(block, 0, width, axis=dim), axis, backward)
        block = jnp.concatenate([low, block, high], axis=dim)
    return block


def broadcast(array, axis, root):
    mine = lax.axis_index(axis) == root
    return lax.psum(jnp.where(mine, array, jnp.zeros_like(array)), axis)


def request_ranks(owners, device_count):
    onehot = (owners[:, :, None] == jnp.arange(device_count, dtype=jnp.int32)).astype(jnp.int32)
    before = jnp.cumsum(onehot, axis=1) - onehot
    return jnp.sum(before * onehot, axis=2)


def per_device(query, key, value, cotangent, global_ids, rand_owner, rand_local):
    tok_count, features = query.shape
    blocks = tok_count // BLOCK
    head_count = features // HEAD_DIM
    groups = head_count // GROUP_HEADS
    group_width = GROUP_HEADS * HEAD_DIM
    device_count = lax.axis_size("ctx")
    my_index = lax.axis_index("ctx")
    pick_count = groups * ROUNDS
    slot_count = max(2, (pick_count * blocks + device_count - 1) // device_count)
    score_scale = HEAD_DIM ** (-0.5)
    key_kinds = 3 + GLOBALS + ROUNDS
    key_span = key_kinds * BLOCK
    kv_local = jnp.stack(
        (key.reshape(blocks, BLOCK, features), value.reshape(blocks, BLOCK, features)), axis=2
    )
    padded = padded_2(kv_local, (("ctx", 0),), 1)
    glob_list = []
    for glob_index in range(GLOBALS):
        root_dev = global_ids[glob_index] // blocks
        local_block = global_ids[glob_index] % blocks
        block_kv = lax.dynamic_index_in_dim(kv_local, local_block, 0, keepdims=False)
        glob_list.append(broadcast(block_kv, "ctx", root_dev))
    glob_kv = jnp.stack(glob_list)
    owners_all = rand_owner.reshape(device_count, blocks * pick_count)
    locals_all = rand_local.reshape(device_count, blocks * pick_count)
    ranks_all = request_ranks(owners_all, device_count)
    my_owner = lax.dynamic_index_in_dim(owners_all, my_index, 0, keepdims=False)
    my_rank = lax.dynamic_index_in_dim(ranks_all, my_index, 0, keepdims=False)
    fetch_index = my_owner * slot_count + my_rank
    entry_group = jnp.arange(blocks * pick_count, dtype=jnp.int32) % pick_count // ROUNDS
    matched = (
        (owners_all[:, :, None] == my_index)
        & (ranks_all[:, :, None] == jnp.arange(slot_count, dtype=jnp.int32))
    ).astype(jnp.int32)
    send_block = jnp.sum(matched * locals_all[:, :, None], axis=1).reshape(-1)
    send_group = jnp.sum(matched * entry_group[None, :, None], axis=1).reshape(-1)
    send_live = jnp.sum(matched, axis=1).reshape(-1) > 0
    kv_grouped = kv_local.reshape(blocks, BLOCK, 2, groups, group_width)

    def pack_blocks():
        picked = kv_grouped[send_block, :, :, send_group, :]
        picked = jnp.where(send_live[:, None, None, None], picked, jnp.zeros((), picked.dtype))
        return picked.reshape(device_count, slot_count, BLOCK, 2, group_width)

    def unpack_blocks(arrived):
        arrived_flat = arrived.reshape(device_count * slot_count, BLOCK, 2, group_width)
        return arrived_flat[fetch_index].reshape(blocks, groups, ROUNDS, BLOCK, 2, group_width)

    random_kv = unpack_blocks(
        lax.all_to_all(pack_blocks(), "ctx", split_axis=0, concat_axis=0, tiled=True)
    )
    block_ids = jnp.arange(blocks)
    left_ok = jnp.logical_or(my_index > 0, block_ids > 0)
    right_ok = jnp.logical_or(my_index < device_count - 1, block_ids < blocks - 1)
    key_valid = jnp.concatenate(
        (
            jnp.repeat(left_ok[:, None], BLOCK, axis=1),
            jnp.ones((blocks, BLOCK), jnp.bool_),
            jnp.repeat(right_ok[:, None], BLOCK, axis=1),
            jnp.ones((blocks, (GLOBALS + ROUNDS) * BLOCK), jnp.bool_),
        ),
        axis=1,
    )
    valid_four = key_valid[:, None, None, :]

    def assemble(group_idx, source_kv):
        start_col = group_idx * group_width
        window = jnp.stack(
            [
                padded[offset : offset + blocks, :, :, start_col : start_col + group_width]
                for offset in range(3)
            ],
            axis=1,
        )
        global_part = jnp.broadcast_to(
            glob_kv[None, :, :, :, start_col : start_col + group_width],
            (blocks, GLOBALS, BLOCK, 2, group_width),
        )
        random_part = source_kv[:, group_idx]
        joined = jnp.concatenate((window, global_part, random_part), axis=1)
        joined = joined.reshape(blocks, key_span, 2, GROUP_HEADS, HEAD_DIM)
        return (joined[:, :, 0], joined[:, :, 1])

    def score_block(query_group, keys_group):
        scores = (
            jnp.einsum(
                "bqhd,bkhd->bhqk", query_group, keys_group, preferred_element_type=jnp.float32
            )
            * score_scale
        )
        return jnp.where(valid_four, scores, NEG_FILL)

    query_blocks = query.reshape(blocks, BLOCK, groups, GROUP_HEADS, HEAD_DIM)
    cot_blocks = cotangent.reshape(blocks, BLOCK, groups, GROUP_HEADS, HEAD_DIM)
    attended_parts = []
    totals = []
    for group_idx in range(groups):
        keys_group, vals_group = assemble(group_idx, random_kv)
        scores = score_block(query_blocks[:, :, group_idx], keys_group)
        row_max = jnp.max(scores, axis=-1, keepdims=True)
        weights = jnp.where(valid_four, jnp.exp(scores - row_max), 0.0)
        log_total = row_max + jnp.log(jnp.sum(weights, axis=-1, keepdims=True))
        probs_b = jnp.where(valid_four, jnp.exp(scores - log_total), 0.0).astype(jnp.bfloat16)
        attended_parts.append(
            jnp.einsum(
                "bhqk,bkhd->bqhd", probs_b, vals_group, preferred_element_type=jnp.float32
            ).astype(jnp.bfloat16)
        )
        totals.append(log_total)
    back_kv = unpack_blocks(
        lax.all_to_all(pack_blocks(), "ctx", split_axis=0, concat_axis=0, tiled=True)
    )
    win_acc = jnp.zeros((blocks + 2, BLOCK, 2, features), jnp.float32)
    glob_acc = jnp.zeros((GLOBALS, BLOCK, 2, features), jnp.float32)
    grad_query_parts = []
    random_terms = []
    for group_idx in range(groups):
        start_col = group_idx * group_width
        keys_group, vals_group = assemble(group_idx, back_kv)
        query_group = query_blocks[:, :, group_idx]
        cot_group = cot_blocks[:, :, group_idx]
        scores = score_block(query_group, keys_group)
        probs = jnp.where(valid_four, jnp.exp(scores - totals[group_idx]), 0.0)
        probs_b = probs.astype(jnp.bfloat16)
        row_dot = jnp.sum(
            cot_group.astype(jnp.float32) * attended_parts[group_idx].astype(jnp.float32), axis=-1
        )
        row_dot = jnp.transpose(row_dot, (0, 2, 1))[..., None]
        dprob = jnp.einsum(
            "bqhd,bkhd->bhqk", cot_group, vals_group, preferred_element_type=jnp.float32
        )
        dscore = (probs * (dprob - row_dot)).astype(jnp.bfloat16)
        grad_query_parts.append(
            (
                jnp.einsum(
                    "bhqk,bkhd->bqhd", dscore, keys_group, preferred_element_type=jnp.float32
                )
                * score_scale
            ).astype(jnp.bfloat16)
        )
        term_k = (
            jnp.einsum("bhqk,bqhd->bkhd", dscore, query_group, preferred_element_type=jnp.float32)
            * score_scale
        )
        term_v = jnp.einsum(
            "bhqk,bqhd->bkhd", probs_b, cot_group, preferred_element_type=jnp.float32
        )
        term_kv = jnp.stack((term_k, term_v), axis=2).reshape(
            blocks, key_kinds, BLOCK, 2, group_width
        )
        for offset in range(3):
            win_acc = win_acc.at[
                offset : offset + blocks, :, :, start_col : start_col + group_width
            ].add(term_kv[:, offset])
        glob_acc = glob_acc.at[:, :, :, start_col : start_col + group_width].add(
            jnp.sum(term_kv[:, 3 : 3 + GLOBALS], axis=0)
        )
        random_terms.append(term_kv[:, 3 + GLOBALS :].astype(jnp.bfloat16))
    random_flat = jnp.stack(random_terms, axis=1).reshape(
        blocks * pick_count, BLOCK, 2, group_width
    )
    grad_send = (
        jnp.zeros((device_count * slot_count, BLOCK, 2, group_width), jnp.bfloat16)
        .at[fetch_index]
        .set(random_flat)
    )
    grad_back = lax.all_to_all(
        grad_send.reshape(device_count, slot_count, BLOCK, 2, group_width),
        "ctx",
        split_axis=0,
        concat_axis=0,
        tiled=True,
    )
    grad_back = grad_back.reshape(device_count * slot_count, BLOCK, 2, group_width).astype(
        jnp.float32
    )
    grad_back = jnp.where(send_live[:, None, None, None], grad_back, 0.0)
    grad_owned = jnp.zeros((blocks, BLOCK, 2, groups, group_width), jnp.float32)
    grad_owned = grad_owned.at[send_block, :, :, send_group, :].add(grad_back)
    edge_sums = jnp.stack((win_acc[0], win_acc[blocks + 1]))
    edge_ext = padded_2(edge_sums, (("ctx", 0),), 1)
    glob_summed = lax.psum(glob_acc, "ctx")
    grad_total = win_acc[1 : blocks + 1] + grad_owned.reshape(blocks, BLOCK, 2, features)
    grad_total = grad_total.at[0].add(edge_ext[0]).at[blocks - 1].add(edge_ext[3])
    first_id = my_index * blocks + jnp.arange(blocks)
    for glob_index in range(GLOBALS):
        is_owner = global_ids[glob_index] == first_id
        grad_total = grad_total + jnp.where(
            is_owner[:, None, None, None], glob_summed[glob_index][None], 0.0
        )
    attended = jnp.stack(attended_parts, axis=2).reshape(tok_count, features)
    grad_query = jnp.stack(grad_query_parts, axis=2).reshape(tok_count, features)
    grad_key = grad_total[:, :, 0].reshape(tok_count, features).astype(jnp.bfloat16)
    grad_value = grad_total[:, :, 1].reshape(tok_count, features).astype(jnp.bfloat16)
    return (attended, grad_query, grad_key, grad_value)


def solution(mesh):
    return jax.shard_map(
        per_device,
        mesh=mesh,
        in_specs=(
            P(("groups", "ctx"), None),
            P(("groups", "ctx"), None),
            P(("groups", "ctx"), None),
            P(("groups", "ctx"), None),
            P("groups"),
            P("groups", None),
            P("groups", None),
        ),
        out_specs=(
            P(("groups", "ctx"), None),
            P(("groups", "ctx"), None),
            P(("groups", "ctx"), None),
            P(("groups", "ctx"), None),
        ),
        check_vma=False,
    )
```

profile of v0, /device:TPU:9, one launch (start us, length us, event | category | flops | bytes accessed | tf_op | source)
XLA Modules:
  0.0 541.7 jit_solution(3733437625669096891)
XLA Ops:
  15.0 4.5 broadcast_select_fusion
  19.4 6.8 %all-to-all-start = ((bf16[16,2,64,2,512]{4,2,3,1,0:T(8,128)(2,1)}), bf16[16,2,64,2,512]{4,2,3,1,0:T(8,128)(2,1)}, u32[]{:S(2)}, u32[]{:S(2)}) async-start(bf16[16,2,64,2,512]{4,2,3,1,0:T(8,128)(2,1)} %broadcast_select_fusion), calls=%async_computation | async-start | bytes 8388608 | tf_op jit(solution)/shard_map/all_to_all | solution.py:90
  48.4 4.6 collective-permute-done
  55.0 124.8 %all-reduce.7.cloned.1.call-done = (bf16[1,64,2,1024]{3,1,2,0:T(8,128)(2,1)}, bf16[1,64,2,1024]{3,1,2,0:T(8,128)(2,1)}) async-done(((bf16[1,64,2,1024]{3,1,2,0:T(8,128)(2,1)}, bf16[1,64,2,1024]{3,1,2,0:T(8,128)(2,1)}), (bf16[1,64,2,1024]{3,1,2,0:T(8,128)(2,1)}, bf16[1,64,2,1024]{3,1,2,0:T(8,128)(2,1)})) %all-reduce.7.cloned.1.call-update) | async-done | bytes 524304 | tf_op jit(solution)/shard_map/psum | solution.py:31
  191.2 10.0 %copy.236 = bf16[4,8,64,2,512]{2,1,4,0,3:T(8,128)(2,1)} copy(bf16[4,8,64,2,512]{4,2,3,1,0:T(8,128)(2,1)} %get-tuple-element.138) | data formatting | bytes 8388608 | tf_op jit(solution)/shard_map/reshape | solution.py:121
  201.3 11.8 %reshape.691 = bf16[4,512,2,8,64]{1,4,3,0,2:T(8,128)(2,1)} reshape(bf16[4,8,64,2,512]{2,1,4,0,3:T(8,128)(2,1)} %copy.236) | data formatting | bytes 8388608 | tf_op jit(solution)/shard_map/reshape | solution.py:121
  213.1 10.0 %copy.234 = bf16[4,8,64,2,512]{2,1,4,0,3:T(8,128)(2,1)} copy(bf16[4,8,64,2,512]{4,2,3,1,0:T(8,128)(2,1)} %get-tuple-element.137) | data formatting | bytes 8388608 | tf_op jit(solution)/shard_map/reshape | solution.py:121
  223.1 11.8 %reshape.690 = bf16[4,512,2,8,64]{1,4,3,0,2:T(8,128)(2,1)} reshape(bf16[4,8,64,2,512]{2,1,4,0,3:T(8,128)(2,1)} %copy.234) | data formatting | bytes 8388608 | tf_op jit(solution)/shard_map/reshape | solution.py:121
  257.1 7.1 %reshape.688 = f32[4,8,64,1,512]{2,1,4,0,3:T(8,128)} reshape(f32[4,512,8,64]{1,3,2,0:T(8,128)} %convolution_bitcast_fusion) | data formatting | bytes 8388608 | tf_op jit(solution)/shard_map/stack | solution.py:188
  264.2 6.8 %copy.232 = f32[4,8,64,1,512]{4,2,1,0,3:T(8,128)} copy(f32[4,8,64,1,512]{2,1,4,0,3:T(8,128)} %reshape.688) | data formatting | bytes 8388608 | tf_op jit(solution)/shard_map/stack | solution.py:188
  273.7 7.1 %reshape.687 = f32[4,8,64,1,512]{2,1,4,0,3:T(8,128)} reshape(f32[4,512,8,64]{1,3,2,0:T(8,128)} %multiply_bitcast_fusion) | data formatting | bytes 8388608 | tf_op jit(solution)/shard_map/stack | solution.py:188
  280.7 6.8 %copy.231 = f32[4,8,64,1,512]{4,2,1,0,3:T(8,128)} copy(f32[4,8,64,1,512]{2,1,4,0,3:T(8,128)} %reshape.687) | data formatting | bytes 8388608 | tf_op jit(solution)/shard_map/stack | solution.py:188
  287.6 7.1 %reshape.686 = f32[4,8,64,1,512]{2,1,4,0,3:T(8,128)} reshape(f32[4,512,8,64]{1,3,2,0:T(8,128)} %convolution_bitcast_fusion.1) | data formatting | bytes 8388608 | tf_op jit(solution)/shard_map/stack | solution.py:188
  294.6 7.0 %copy.230 = f32[4,8,64,1,512]{4,2,1,0,3:T(8,128)} copy(f32[4,8,64,1,512]{2,1,4,0,3:T(8,128)} %reshape.686) | data formatting | bytes 8388608 | tf_op jit(solution)/shard_map/stack | solution.py:188
  304.3 7.1 %reshape.685 = f32[4,8,64,1,512]{2,1,4,0,3:T(8,128)} reshape(f32[4,512,8,64]{1,3,2,0:T(8,128)} %multiply_bitcast_fusion.1) | data formatting | bytes 8388608 | tf_op jit(solution)/shard_map/stack | solution.py:188
  311.4 6.9 %copy.229 = f32[4,8,64,1,512]{4,2,1,0,3:T(8,128)} copy(f32[4,8,64,1,512]{2,1,4,0,3:T(8,128)} %reshape.685) | data formatting | bytes 8388608 | tf_op jit(solution)/shard_map/stack | solution.py:188
  325.9 7.5 %scatter_fusion = bf16[32,64,2,512]{3,1,2,0:T(8,128)(2,1)} fusion(bf16[32,64,2,512]{3,1,2,0:T(8,128)(2,1)} %broadcast_in_dim.190, s32[24]{0:T(128)S(1)} %fusion.86, bf16[24,64,2,512]{3,1,2,0:T(8,128)(2,1)S(1)} %bitcast.294), kind=kCustom, calls=%fused_computation.2 | custom fusion | bytes 9437280 | tf_op jit(solution)/shard_map/scatter | solution.py:205
  333.4 6.5 %all-to-all-start.1 = ((bf16[16,2,64,2,512]{4,2,3,1,0:T(8,128)(2,1)}), bf16[16,2,64,2,512]{4,2,3,1,0:T(8,128)(2,1)}, u32[]{:S(2)}, u32[]{:S(2)}) async-start(bf16[16,2,64,2,512]{4,2,3,1,0:T(8,128)(2,1)} %bitcast.283), calls=%async_computation.1 | async-start | bytes 8388608 | tf_op jit(solution)/shard_map/all_to_all | solution.py:207
  366.4 5.7 %scatter-add.41 = f32[6,64,2,1024]{3,1,0,2:T(8,128)S(1)} dynamic-update-slice(f32[6,64,2,1024]{3,1,0,2:T(8,128)S(1)} %fusion.58, f32[4,64,2,512]{3,1,0,2:T(8,128)} %add_select_fusion, s32[]{:T(128)} %bitcast.48, s32[]{:T(128)} %constant.374.clone.1, s32[]{:T(128)} %constant.374.clone.1, s32[]{:T(128)} %bitcast.49) | dynamic-update-slice | bytes 2097156 | tf_op jit(solution)/shard_map/scatter-add | solution.py:194
  382.7 3.3 collective-permute-start.2
  388.0 111.8 %all-reduce.5.cloned.1.call-done = f32[2,64,2,1024]{3,1,0,2:T(8,128)} async-done(((f32[2,64,2,1024]{3,1,0,2:T(8,128)}), f32[2,64,2,1024]{3,1,0,2:T(8,128)}) %all-reduce.5.cloned.1.call-update) | async-done | bytes 1048592 | tf_op jit(solution)/shard_map/psum | solution.py:222
  502.1 6.9 %convert_select_fusion = f32[32,64,2,512]{3,1,2,0:T(8,128)} fusion(bf16[16,2,64,2,512]{4,2,3,1,0:T(8,128)(2,1)} %all-to-all-done.1, pred[32]{0:T(512)(128)(4,1)S(1)} %gt.20), kind=kLoop, calls=%fused_computation.20 | loop fusion | flops 4194304 | bytes 12582944 | tf_op jit(solution)/shard_map/jit(_where)/select_n | solution.py:217
  509.3 12.2 %scatter_fusion.1 = f32[4,64,2,2,512]{4,1,3,2,0:T(8,128)S(1)} fusion(f32[4,64,2,2,512]{4,1,3,2,0:T(8,128)S(1)} %broadcast_in_dim.188, s32[32]{0:T(128)S(1)} %get-tuple-element.133, f32[32,64,2,512]{3,1,2,0:T(8,128)} %convert_select_fusion), kind=kCustom, calls=%fused_computation.3 | custom fusion | flops 2097152 | bytes 25166080 | tf_op jit(solution)/shard_map/scatter-add | solution.py:219
  524.4 4.2 reshape.689
  (178 shorter events, 123.4 us)
Async XLA Ops:
  19.4 6.8 %copy-start.30 = (s32[2]{0:T(128)S(1)}, s32[2]{0:T(128)}, u32[]{:S(2)}) copy-start(s32[2]{0:T(128)} %param.31) | copy-start | bytes 28
  19.4 12.6 %copy-start.12 = (bf16[256,1024]{1,0:T(8,128)(2,1)S(1)}, bf16[256,1024]{1,0:T(8,128)(2,1)}, u32[]{:S(2)}) copy-start(bf16[256,1024]{1,0:T(8,128)(2,1)} %param.28) | copy-start | bytes 1572868
  19.4 12.6 %copy-start.13 = (bf16[256,1024]{1,0:T(8,128)(2,1)S(1)}, bf16[256,1024]{1,0:T(8,128)(2,1)}, u32[]{:S(2)}) copy-start(bf16[256,1024]{1,0:T(8,128)(2,1)} %param.29) | copy-start | bytes 1572868
  19.4 19.4 %copy-start.25 = (bf16[256,1024]{1,0:T(8,128)(2,1)S(1)}, bf16[256,1024]{1,0:T(8,128)(2,1)}, u32[]{:S(2)}) copy-start(bf16[256,1024]{1,0:T(8,128)(2,1)} %param.30) | copy-start | bytes 1572868
  19.4 167.0 %all-to-all-start = ((bf16[16,2,64,2,512]{4,2,3,1,0:T(8,128)(2,1)}), bf16[16,2,64,2,512]{4,2,3,1,0:T(8,128)(2,1)}, u32[]{:S(2)}, u32[]{:S(2)}) async-start(bf16[16,2,64,2,512]{4,2,3,1,0:T(8,128)(2,1)} %broadcast_select_fusion), calls=%async_computation | async-start | bytes 8388608 | tf_op jit(solution)/shard_map/all_to_all | solution.py:90
  26.2 153.6 %all-reduce.7.cloned.1.call-start = ((), (), s32[]{:S(2)}) async-start(), calls=%async_computation.3 | async-start | bytes 1048576 | tf_op jit(solution)/shard_map/psum | solution.py:31
  33.0 19.9 %collective-permute-start = (bf16[1,64,2,1024]{3,1,2,0:T(8,128)(2,1)}, bf16[1,64,2,1024]{3,1,2,0:T(8,128)(2,1)}, u32[]{:S(2)}, u32[]{:S(2)}) collective-permute-start(bf16[1,64,2,1024]{3,1,2,0:T(8,128)(2,1)} %get-tuple-element.154), channel_id=1, source_target_pairs={{0,1},{1,2},{2,3},{3,4},{4,5},{5,6},{6,7},{7,8},{8,9},{9,10},{10,1... | collective-permute-start | bytes 786440 | tf_op jit(solution)/shard_map/ppermute | solution.py:21
  36.4 146.4 %collective-permute-start.1 = (bf16[1,64,2,1024]{3,1,2,0:T(8,128)(2,1)S(1)}, bf16[1,64,2,1024]{3,1,2,0:T(8,128)(2,1)}, u32[]{:S(2)}, u32[]{:S(2)}) collective-permute-start(bf16[1,64,2,1024]{3,1,2,0:T(8,128)(2,1)S(1)} %get-tuple-element.155), channel_id=1, source_target_pairs={{1,0},{2,1},{3,2},{4,3},{5,4},{6,5},{7,6},{8,7},{9,8},{10,9},{11,1... | collective-permute-start | bytes 786440 | tf_op jit(solution)/shard_map/ppermute | solution.py:24
  223.1 11.8 %copy-start.18 = (bf16[4,64,1,8,64]{4,3,2,1,0:T(8,128)(2,1)S(1)}, bf16[4,64,1,8,64]{4,3,2,1,0:T(8,128)(2,1)}, u32[]{:S(2)}) copy-start(bf16[4,64,1,8,64]{4,3,2,1,0:T(8,128)(2,1)} %get-tuple-element.150) | copy-start | bytes 786436
  254.4 16.5 %copy-start.21 = (bf16[4,8,64,512]{3,2,1,0:T(8,128)(2,1)}, bf16[4,8,64,512]{3,2,1,0:T(8,128)(2,1)S(1)}, u32[]{:S(2)}) copy-start(bf16[4,8,64,512]{3,2,1,0:T(8,128)(2,1)S(1)} %fusion) | copy-start | bytes 6291460
  294.6 7.0 %copy-start.22 = (bf16[4,8,64,512]{3,2,1,0:T(8,128)(2,1)S(1)}, bf16[4,8,64,512]{3,2,1,0:T(8,128)(2,1)}, u32[]{:S(2)}) copy-start(bf16[4,8,64,512]{3,2,1,0:T(8,128)(2,1)} %fusion.1) | copy-start | bytes 6291460
  318.3 4.4 copy-start.7
  333.4 8.6 %copy-start.31 = (s32[4]{0:T(128)S(1)}, s32[4]{0:T(128)}, u32[]{:S(2)}) copy-start(s32[4]{0:T(128)} %constant.391.clone.1) | copy-start | bytes 52
  333.4 10.6 %copy-start.26 = (bf16[4,8,64,64]{3,2,1,0:T(8,128)(2,1)S(1)}, bf16[4,8,64,64]{3,2,1,0:T(8,128)(2,1)}, u32[]{:S(2)}) copy-start(bf16[4,8,64,64]{3,2,1,0:T(8,128)(2,1)} %get-tuple-element.165) | copy-start | bytes 786436
  333.4 10.6 %copy-start.27 = (bf16[4,8,64,64]{3,2,1,0:T(8,128)(2,1)S(1)}, bf16[4,8,64,64]{3,2,1,0:T(8,128)(2,1)}, u32[]{:S(2)}) copy-start(bf16[4,8,64,64]{3,2,1,0:T(8,128)(2,1)} %get-tuple-element.167) | copy-start | bytes 786436
  333.4 168.7 %all-to-all-start.1 = ((bf16[16,2,64,2,512]{4,2,3,1,0:T(8,128)(2,1)}), bf16[16,2,64,2,512]{4,2,3,1,0:T(8,128)(2,1)}, u32[]{:S(2)}, u32[]{:S(2)}) async-start(bf16[16,2,64,2,512]{4,2,3,1,0:T(8,128)(2,1)} %bitcast.283), calls=%async_computation.1 | async-start | bytes 8388608 | tf_op jit(solution)/shard_map/all_to_all | solution.py:207
  340.0 159.8 %all-reduce.5.cloned.1.call-start = ((), (), s32[]{:S(2)}) async-start(), calls=%async_computation.2 | async-start | bytes 2097152 | tf_op jit(solution)/shard_map/psum | solution.py:222
  372.1 4.1 copy-start.9
  381.6 127.4 %copy-start.10 = (f32[6,64,2,1024]{3,1,0,2:T(8,128)}, f32[6,64,2,1024]{3,1,0,2:T(8,128)S(1)}, u32[]{:S(2)}) copy-start(f32[6,64,2,1024]{3,1,0,2:T(8,128)S(1)} %fusion.48) | copy-start | bytes 9437188
  382.7 148.0 %collective-permute-start.2 = (f32[1,64,2,1024]{3,1,0,2:T(8,128)}, f32[1,64,2,1024]{3,1,0,2:T(8,128)}, u32[]{:S(2)}, u32[]{:S(2)}) collective-permute-start(f32[1,64,2,1024]{3,1,0,2:T(8,128)} %get-tuple-element.136), channel_id=1, source_target_pairs={{0,1},{1,2},{2,3},{3,4},{4,5},{5,6},{6,7},{7,8},{8,9},{9,10},{10,1... | collective-permute-start | bytes 1572872 | tf_op jit(solution)/shard_map/ppermute | solution.py:21
  386.1 145.8 %collective-permute-start.3 = (f32[1,64,2,1024]{3,1,0,2:T(8,128)}, f32[1,64,2,1024]{3,1,0,2:T(8,128)}, u32[]{:S(2)}, u32[]{:S(2)}) collective-permute-start(f32[1,64,2,1024]{3,1,0,2:T(8,128)} %get-tuple-element.135), channel_id=1, source_target_pairs={{1,0},{2,1},{3,2},{4,3},{5,4},{6,5},{7,6},{8,7},{9,8},{10,9},{11,1... | collective-permute-start | bytes 1572872 | tf_op jit(solution)/shard_map/ppermute | solution.py:24
  524.4 4.2 copy-start.11
  528.6 4.5 copy-start.23
  528.6 4.5 copy-start.24
  (16 other events, 47.2 us)
Sparse Core Ops, SparseCore 0:
  39.0 140.7 all-reduce.6
  377.6 122.1 all-reduce.4
where the time goes:
time: 551 us; the launch traced here: 542 us
  waiting for transfers between devices  241 us (44%)
  local copies, waits for them, and re-layouts  171 us (31%)
  other arithmetic  55 us (10%)
  matrix products  30.1 us (5%)
  starting transfers between devices  24.4 us (4%)
  between operations  20.1 us (4%)
    psum x1, waiting for transfers between devices, broadcast(): return lax.psum(jnp.where(mine, array, jnp.zeros_like(array)), axis)  125 us
    psum x1, waiting for transfers between devices, per_device(): glob_summed = lax.psum(glob_acc, 'ctx')  112 us
    another operation x8, local copies, waits for them, and re-layouts, per_device(): jnp.stack((term_k, term_v), axis=2)  55.7 us
    reshape x4, local copies, waits for them, and re-layouts, assemble(): joined = joined.reshape(blocks, key_span, 2, GROUP_HEADS, HEAD_DIM)  43.7 us
    unnamed x70, local copies, waits for them, and re-layouts  19.5 us
    scatter-add x1, other arithmetic, per_device(): grad_owned = grad_owned.at[send_block, :, :, send_group, :].add(grad_back)  12.2 us
  transfers between devices with their start and end apart: 8, of which 3 were waited for; matrix products, arithmetic and copies ran while one was open for 16% of the time, Pallas kernels for 0%

commit v1 on v0

v1 whole, which is shorter than its diff:
```python
import functools
import math

import jax
import jax.numpy as jnp
from jax import lax
from jax.experimental import pallas as pl
from jax.experimental.pallas import tpu as pltpu
from jax.sharding import PartitionSpec as P

HEAD_DIM = 64
GROUP_HEADS = 8
BLOCK = 64
GLOBALS = 2
ROUNDS = 3
KINDS = 3 + GLOBALS + ROUNDS
SPAN = KINDS * BLOCK
NEG_FILL = -1e30
SCALE = HEAD_DIM ** -0.5
EXP_SCALE = SCALE * math.log2(math.e)
VMEM = pl.BlockSpec(memory_space=pltpu.VMEM)
SMEM = pl.BlockSpec(memory_space=pltpu.SMEM)


def head_of(ref, head):
    return ref[:, head * HEAD_DIM : (head + 1) * HEAD_DIM]


def pack_kernel(repeat, q_ref, k_ref, v_ref, c_ref, out_ref):
    for dst in range(out_ref.shape[0]):
        head = dst // repeat
        out_ref[dst, :, 0:128] = jnp.concatenate((head_of(k_ref, head), head_of(v_ref, head)), axis=1)
        out_ref[dst, :, 128:256] = jnp.concatenate((head_of(q_ref, head), head_of(c_ref, head)), axis=1)


def unpack_kernel(repeat, in_ref, att_ref, dq_ref, dk_ref, dv_ref):
    heads = in_ref.shape[0] // repeat
    for out_ref, col in ((dq_ref, 0), (att_ref, 64), (dk_ref, 128), (dv_ref, 192)):
        for pair in range(heads // 2):
            out_ref[:, pair * 128 : (pair + 1) * 128] = jnp.concatenate(
                [in_ref[(2 * pair + half) * repeat, :, col : col + 64] for half in range(2)], axis=1
            )


def attend_kernel(blocks_per_device, repeat, glob_ref, owner_ref, local_ref, in_ref, out_ref, acc_ref):
    blocks = in_ref.shape[0] // BLOCK
    group = lax.axis_index("ctx") // (repeat * GROUP_HEADS)
    acc_ref[...] = jnp.zeros_like(acc_ref)

    def step(i):
        ids = [jnp.maximum(i - 1, 0), i, jnp.minimum(i + 1, blocks - 1)]
        ids += [glob_ref[n] for n in range(GLOBALS)]
        for n in range(ROUNDS):
            col = group * ROUNDS + n
            ids.append(owner_ref[i, col] * blocks_per_device + local_ref[i, col])
        rows = [pl.ds(pl.multiple_of(one * BLOCK, BLOCK), BLOCK) for one in ids]
        kv = jnp.concatenate([in_ref[r, 0:128] for r in rows], axis=0)
        qc = in_ref[rows[1], 128:256]
        zero = jnp.zeros_like(qc)
        low = lax.broadcasted_iota(jnp.int32, qc.shape, 1) < HEAD_DIM
        q_part = jnp.where(low, qc, zero)
        c_part = jnp.where(low, zero, qc)
        both = lax.dot_general(
            jnp.concatenate((q_part, c_part), axis=0),
            kv,
            (((1,), (1,)), ((), ())),
            preferred_element_type=jnp.float32,
        )
        place = lax.broadcasted_iota(jnp.int32, (1, SPAN), 1)
        absent = ((place < BLOCK) & (i == 0)) | (
            (place >= 2 * BLOCK) & (place < 3 * BLOCK) & (i == blocks - 1)
        )
        scores = jnp.where(absent, NEG_FILL, both[:BLOCK])
        dprob = both[BLOCK:]
        row_max = jnp.max(scores, axis=-1, keepdims=True)
        weights = jnp.exp2((scores - row_max) * EXP_SCALE)
        probs = weights * (1.0 / jnp.sum(weights, axis=-1, keepdims=True))
        row_dot = jnp.sum(probs * dprob, axis=-1, keepdims=True)
        dscore = probs * (dprob - row_dot)
        pd = jnp.concatenate((probs.astype(jnp.bfloat16), dscore.astype(jnp.bfloat16)), axis=0)
        res = jnp.dot(pd, kv, preferred_element_type=jnp.float32)
        out_ref[rows[1], 0:128] = jnp.where(low, res[BLOCK:] * SCALE, res[:BLOCK]).astype(jnp.bfloat16)
        terms = lax.dot_general(
            pd,
            jnp.concatenate((c_part, q_part), axis=0),
            (((0,), (0,)), ((), ())),
            preferred_element_type=jnp.float32,
        )
        for n, r in enumerate(rows):
            acc_ref[r, :] += terms[n * BLOCK : (n + 1) * BLOCK]

    pl.loop(0, blocks)(step)

    def finish(i):
        r = pl.ds(pl.multiple_of(i * 256, 256), 256)
        acc = acc_ref[r, :]
        low = lax.broadcasted_iota(jnp.int32, acc.shape, 1) < HEAD_DIM
        out_ref[r, 128:256] = jnp.where(low, acc * SCALE, acc).astype(jnp.bfloat16)

    pl.loop(0, blocks * BLOCK // 256)(finish)


def per_device(query, key, value, cotangent, global_ids, rand_owner, rand_local):
    tokens, features = query.shape
    heads = features // HEAD_DIM
    devices = lax.axis_size("ctx")
    repeat = max(1, devices // heads)
    params = pltpu.CompilerParams(vmem_limit_bytes=48 << 20)
    packed = pl.pallas_call(
        functools.partial(pack_kernel, repeat),
        out_shape=jax.ShapeDtypeStruct((devices, tokens, 256), jnp.bfloat16),
        in_specs=[VMEM] * 4,
        out_specs=VMEM,
        compiler_params=params,
    )(query, key, value, cotangent)
    arrived = lax.all_to_all(packed, "ctx", 0, 0, tiled=True).reshape(devices * tokens, 256)
    grads = pl.pallas_call(
        functools.partial(attend_kernel, tokens // BLOCK, repeat),
        out_shape=jax.ShapeDtypeStruct((devices * tokens, 256), jnp.bfloat16),
        in_specs=[SMEM] * 3 + [VMEM],
        out_specs=VMEM,
        scratch_shapes=[pltpu.VMEM((devices * tokens, 128), jnp.float32)],
        compiler_params=params,
    )(global_ids, rand_owner, rand_local, arrived)
    back = lax.all_to_all(grads.reshape(devices, tokens, 256), "ctx", 0, 0, tiled=True)
    return pl.pallas_call(
        functools.partial(unpack_kernel, repeat),
        out_shape=[jax.ShapeDtypeStruct((tokens, features), jnp.bfloat16)] * 4,
        in_specs=[VMEM],
        out_specs=[VMEM] * 4,
        compiler_params=params,
    )(back)


def solution(mesh):
    split = P(("groups", "ctx"), None)
    return jax.shard_map(
        per_device,
        mesh=mesh,
        in_specs=(split, split, split, split, P("groups"), P("groups", None), P("groups", None)),
        out_specs=(split, split, split, split),
        check_vma=False,
    )
```

time: 551 us -> 163 us (0.30); the launches traced: 542 us -> 162 us
  waiting for transfers between devices: 241 us -> 45.8 us
  local copies, waits for them, and re-layouts: 171 us -> 5.69 us
  other arithmetic: 55 us -> 0 us
  blocking collectives: 0 us -> 54 us
  Pallas kernels: 0 us -> 49.3 us
  matrix products: 30.1 us -> 0 us
  between operations: 20.1 us -> 0.67 us
  starting transfers between devices: 24.4 us -> 6.74 us
    psum x2 -> x0, waiting for transfers between devices: 237 us -> none  [the longest x1 125 us: broadcast(): return lax.psum(jnp.where(mine, array, jnp.zeros_like(array)), axis)]
    another operation x19 -> x0, local copies, waits for them, and re-layouts: 62.8 us -> none  [the longest x8 55.7 us: per_device(): jnp.stack((term_k, term_v), axis=2)]
    reshape x14 -> x0, local copies, waits for them, and re-layouts: 56.6 us -> none  [the longest x4 43.7 us: assemble(): joined = joined.reshape(blocks, key_span, 2, GROUP_HEADS, HEAD_DIM)]
    all_to_all x0 -> x1, blocking collectives: none -> 54 us  [per_device(): lax.all_to_all(grads.reshape(devices, tokens, 256), 'ctx', 0, 0, tiled=True)]
    pallas_call x0 -> x3, Pallas kernels: none -> 49.3 us  [the longest x1 46.8 us: per_device(): pl.pallas_call(functools.partial(attend_kernel, tokens // BLOCK, repeat),...]
    all_to_all x2 -> x1, waiting for transfers between devices: 0.01 us -> 45.8 us  [per_device(): lax.all_to_all(packed, 'ctx', 0, 0, tiled=True)]
    dot_general x12 -> x0, matrix products: 30.1 us -> none  [the longest x2 6.39 us: per_device(): jnp.einsum('bhqk,bqhd->bkhd', probs_b, cot_group, preferred_element_type=...]
    scatter-add x8 -> x0, other arithmetic: 18.2 us -> none  [the longest x1 12.2 us: per_device(): grad_owned = grad_owned.at[send_block, :, :, send_group, :].add(grad_back)]
  transfers between devices with their start and end apart: 8 -> 1, of which waited for: 3 -> 1; matrix products, arithmetic and copies ran while one was open for 16% -> 0% of each run, Pallas kernels for 0% -> 0%
where the time goes in v1:
time: 163 us; the launch traced here: 162 us
  blocking collectives  54 us (33%)
  Pallas kernels  49.3 us (30%)
  waiting for transfers between devices  45.8 us (28%)
  starting transfers between devices  6.74 us (4%)
  local copies, waits for them, and re-layouts  5.69 us (3%)
    all_to_all x1, blocking collectives, per_device(): lax.all_to_all(grads.reshape(devices, tokens, 256), 'ctx', 0, 0, tiled=True)  54 us
    pallas_call x1, Pallas kernels, per_device(): pl.pallas_call(functools.partial(attend_kernel, tokens // BLOCK, repeat),...  46.8 us
    all_to_all x1, waiting for transfers between devices, per_device(): lax.all_to_all(packed, 'ctx', 0, 0, tiled=True)  45.8 us
    all_to_all x1, starting transfers between devices, per_device(): lax.all_to_all(packed, 'ctx', 0, 0, tiled=True)  6.74 us
    unnamed x18, local copies, waits for them, and re-layouts  5.69 us
  transfers between devices with their start and end apart: 1, of which 1 were waited for; matrix products, arithmetic and copies ran while one was open for 0% of the time, Pallas kernels for 0%

profile of v1, /device:TPU:9, one launch (start us, length us, event | category | flops | bytes accessed | tf_op | source)
XLA Modules:
  0.0 162.2 jit_solution(6236200752126726261)
XLA Ops:
  0.6 0.0 copy-start.1
  0.6 1.0 copy-done.1
  1.7 0.0 copy-start.2
  1.7 1.0 copy-done.2
  2.7 0.0 copy-start.3
  2.7 1.0 copy-done.3
  3.8 0.0 copy-start.4
  3.8 1.0 copy-done.4
  4.8 0.6 shard_map.102
  5.4 0.0 copy-start
  5.4 1.3 copy-done
  6.8 0.0 copy-start.6
  6.8 0.0 copy-start.7
  6.8 0.0 copy-start.5
  6.8 6.7 %all-to-all-start = ((bf16[16,256,256]{2,1,0:T(8,128)(2,1)}), bf16[16,256,256]{2,1,0:T(8,128)(2,1)S(1)}, u32[]{:S(2)}, u32[]{:S(2)}) async-start(bf16[16,256,256]{2,1,0:T(8,128)(2,1)} %copy-done), calls=%async_computation | async-start | bytes 4194304 | tf_op jit(solution)/shard_map/all_to_all | solution.py:116
  13.5 0.0 copy-done.6
  13.5 0.1 copy.11.owner_ref
  13.6 0.0 copy-done.7
  13.6 0.1 copy.12.local_ref
  13.7 45.8 %all-to-all-done = bf16[16,256,256]{2,1,0:T(8,128)(2,1)S(1)} async-done(((bf16[16,256,256]{2,1,0:T(8,128)(2,1)}), bf16[16,256,256]{2,1,0:T(8,128)(2,1)S(1)}, u32[]{:S(2)}, u32[]{:S(2)}) %all-to-all-start) | async-done | bytes 2097184 | tf_op jit(solution)/shard_map/all_to_all | solution.py:116
  59.5 0.0 copy-done.5
  59.5 46.8 %shard_map.103 = bf16[4096,256]{1,0:T(8,128)(2,1)S(1)} custom-call(s32[2]{0:T(128)S(1)} %copy-done.5, s32[64,6]{1,0:T(8,128)S(1)} %copy.11.owner_ref, s32[64,6]{1,0:T(8,128)S(1)} %copy.12.local_ref, bf16[4096,256]{1,0:T(8,128)(2,1)S(1)} %bitcast.2), custom_call_target="tpu_custom_call" | custom-call | tf_op jit(solution)/shard_map/pallas_call | solution.py:117
  106.3 54.0 %all_to_all.10.in_ref = bf16[16,256,256]{2,1,0:T(8,128)(2,1)S(1)} all-to-all(bf16[16,256,256]{2,1,0:T(8,128)(2,1)S(1)} %bitcast.3), channel_id=1, replica_groups=mesh['groups'=2,'ctx'=16] {'ctx'}, dimensions={0} | all-to-all | bytes 4194304 | tf_op jit(solution)/shard_map/all_to_all | solution.py:125
  160.3 1.9 %shard_map.104 = (bf16[256,1024]{1,0:T(8,128)(2,1)}, bf16[256,1024]{1,0:T(8,128)(2,1)}, bf16[256,1024]{1,0:T(8,128)(2,1)}, bf16[256,1024]{1,0:T(8,128)(2,1)}) custom-call(bf16[16,256,256]{2,1,0:T(8,128)(2,1)S(1)} %all_to_all.10.in_ref), custom_call_target="tpu_custom_call" | custom-call | tf_op jit(solution)/shard_map/pallas_call | solution.py:126
Async XLA Ops:
  0.6 1.0 copy-start.1
  1.7 1.0 copy-start.2
  2.7 1.0 copy-start.3
  3.8 1.0 copy-start.4
  5.4 1.3 copy-start
  6.8 6.8 %copy-start.6 = (s32[64,6]{0,1:T(8,128)S(1)}, s32[64,6]{0,1:T(8,128)}, u32[]{:S(2)}) copy-start(s32[64,6]{0,1:T(8,128)} %param.12) | copy-start | bytes 4612
  6.8 6.9 %copy-start.7 = (s32[64,6]{0,1:T(8,128)S(1)}, s32[64,6]{0,1:T(8,128)}, u32[]{:S(2)}) copy-start(s32[64,6]{0,1:T(8,128)} %param.13) | copy-start | bytes 4612
  6.8 52.7 %copy-start.5 = (s32[2]{0:T(128)S(1)}, s32[2]{0:T(128)}, u32[]{:S(2)}) copy-start(s32[2]{0:T(128)} %glob_ref.1) | copy-start | bytes 28
  6.8 52.7 %all-to-all-start = ((bf16[16,256,256]{2,1,0:T(8,128)(2,1)}), bf16[16,256,256]{2,1,0:T(8,128)(2,1)S(1)}, u32[]{:S(2)}, u32[]{:S(2)}) async-start(bf16[16,256,256]{2,1,0:T(8,128)(2,1)} %copy-done), calls=%async_computation | async-start | bytes 4194304 | tf_op jit(solution)/shard_map/all_to_all | solution.py:116

commit v2 on v1

--- a/solution.py
+++ b/solution.py
@@ -16,6 +16,7 @@
 KINDS = 3 + GLOBALS + ROUNDS
 SPAN = KINDS * BLOCK
 NEG_FILL = -1e30
+UNROLL = 8
 SCALE = HEAD_DIM ** -0.5
 EXP_SCALE = SCALE * math.log2(math.e)
 VMEM = pl.BlockSpec(memory_space=pltpu.VMEM)
@@ -47,7 +48,10 @@
     group = lax.axis_index("ctx") // (repeat * GROUP_HEADS)
     acc_ref[...] = jnp.zeros_like(acc_ref)
 
-    def step(i):
+    low = lax.broadcasted_iota(jnp.int32, (BLOCK, 128), 1) < HEAD_DIM
+    place = lax.broadcasted_iota(jnp.int32, (1, SPAN), 1)
+
+    def load(i):
         ids = [jnp.maximum(i - 1, 0), i, jnp.minimum(i + 1, blocks - 1)]
         ids += [glob_ref[n] for n in range(GLOBALS)]
         for n in range(ROUNDS):
@@ -57,16 +61,17 @@
         kv = jnp.concatenate([in_ref[r, 0:128] for r in rows], axis=0)
         qc = in_ref[rows[1], 128:256]
         zero = jnp.zeros_like(qc)
-        low = lax.broadcasted_iota(jnp.int32, qc.shape, 1) < HEAD_DIM
-        q_part = jnp.where(low, qc, zero)
-        c_part = jnp.where(low, zero, qc)
-        both = lax.dot_general(
+        return rows, kv, jnp.where(low, qc, zero), jnp.where(low, zero, qc)
+
+    def products(kv, q_part, c_part):
+        return lax.dot_general(
             jnp.concatenate((q_part, c_part), axis=0),
             kv,
             (((1,), (1,)), ((), ())),
             preferred_element_type=jnp.float32,
         )
-        place = lax.broadcasted_iota(jnp.int32, (1, SPAN), 1)
+
+    def softmax(i, both):
         absent = ((place < BLOCK) & (i == 0)) | (
             (place >= 2 * BLOCK) & (place < 3 * BLOCK) & (i == blocks - 1)
         )
@@ -74,28 +79,44 @@
         dprob = both[BLOCK:]
         row_max = jnp.max(scores, axis=-1, keepdims=True)
         weights = jnp.exp2((scores - row_max) * EXP_SCALE)
-        probs = weights * (1.0 / jnp.sum(weights, axis=-1, keepdims=True))
-        row_dot = jnp.sum(probs * dprob, axis=-1, keepdims=True)
+        inverse = 1.0 / jnp.sum(weights, axis=-1, keepdims=True)
+        row_dot = jnp.sum(weights * dprob, axis=-1, keepdims=True) * inverse
+        probs = weights * inverse
         dscore = probs * (dprob - row_dot)
-        pd = jnp.concatenate((probs.astype(jnp.bfloat16), dscore.astype(jnp.bfloat16)), axis=0)
+        return jnp.concatenate((probs.astype(jnp.bfloat16), dscore.astype(jnp.bfloat16)), axis=0)
+
+    def query_side(row, kv, pd):
         res = jnp.dot(pd, kv, preferred_element_type=jnp.float32)
-        out_ref[rows[1], 0:128] = jnp.where(low, res[BLOCK:] * SCALE, res[:BLOCK]).astype(jnp.bfloat16)
-        terms = lax.dot_general(
+        out_ref[row, 0:128] = jnp.where(low, res[BLOCK:] * SCALE, res[:BLOCK]).astype(jnp.bfloat16)
+
+    def key_side(q_part, c_part, pd):
+        return lax.dot_general(
             pd,
             jnp.concatenate((c_part, q_part), axis=0),
             (((0,), (0,)), ((), ())),
             preferred_element_type=jnp.float32,
         )
-        for n, r in enumerate(rows):
-            acc_ref[r, :] += terms[n * BLOCK : (n + 1) * BLOCK]
 
-    pl.loop(0, blocks)(step)
+    def step(j):
+        mine = [j * UNROLL + u for u in range(UNROLL)]
+        loaded = [load(i) for i in mine]
+        both = [products(*one[1:]) for one in loaded]
+        pds = [softmax(i, one) for i, one in zip(mine, both)]
+        terms = []
+        for (rows, kv, q_part, c_part), pd in zip(loaded, pds):
+            query_side(rows[1], kv, pd)
+            terms.append(key_side(q_part, c_part, pd))
+        for one, term in zip(loaded, terms):
+            for n, r in enumerate(one[0]):
+                acc_ref[r, :] += term[n * BLOCK : (n + 1) * BLOCK]
+
+    pl.loop(0, blocks // UNROLL)(step)
 
     def finish(i):
         r = pl.ds(pl.multiple_of(i * 256, 256), 256)
         acc = acc_ref[r, :]
-        low = lax.broadcasted_iota(jnp.int32, acc.shape, 1) < HEAD_DIM
-        out_ref[r, 128:256] = jnp.where(low, acc * SCALE, acc).astype(jnp.bfloat16)
+        left = lax.broadcasted_iota(jnp.int32, acc.shape, 1) < HEAD_DIM
+        out_ref[r, 128:256] = jnp.where(left, acc * SCALE, acc).astype(jnp.bfloat16)
 
     pl.loop(0, blocks * BLOCK // 256)(finish)
 

time: 163 us -> 130 us (0.80)
  Pallas kernels: 49.3 us -> 16 us
    pallas_call x1, Pallas kernels: 46.8 us -> 13.4 us  [per_device(): pl.pallas_call(functools.partial(attend_kernel, tokens // BLOCK, repeat),...]
where the time goes in v2:
time: 130 us; the launch traced here: 129 us
  blocking collectives  54 us (42%)
  waiting for transfers between devices  45.8 us (35%)
  Pallas kernels  16 us (12%)
  starting transfers between devices  6.74 us (5%)
  local copies, waits for them, and re-layouts  5.69 us (4%)
    all_to_all x1, blocking collectives, per_device(): lax.all_to_all(grads.reshape(devices, tokens, 256), 'ctx', 0, 0, tiled=True)  54 us
    all_to_all x1, waiting for transfers between devices, per_device(): lax.all_to_all(packed, 'ctx', 0, 0, tiled=True)  45.8 us
    pallas_call x1, Pallas kernels, per_device(): pl.pallas_call(functools.partial(attend_kernel, tokens // BLOCK, repeat),...  13.4 us
    all_to_all x1, starting transfers between devices, per_device(): lax.all_to_all(packed, 'ctx', 0, 0, tiled=True)  6.74 us
    unnamed x18, local copies, waits for them, and re-layouts  5.69 us
  transfers between devices with their start and end apart: 1, of which 1 were waited for; matrix products, arithmetic and copies ran while one was open for 0% of the time, Pallas kernels for 0%

profile of v2, /device:TPU:9, one launch (start us, length us, event | category | flops | bytes accessed | tf_op | source)
XLA Modules:
  0.0 128.9 jit_solution(3624776104746486091)
XLA Ops:
  0.6 0.0 copy-start.1
  0.6 1.0 copy-done.1
  1.7 0.0 copy-start.2
  1.7 1.0 copy-done.2
  2.7 0.0 copy-start.3
  2.7 1.0 copy-done.3
  3.8 0.0 copy-start.4
  3.8 1.0 copy-done.4
  4.8 0.6 shard_map.102
  5.4 0.0 copy-start
  5.4 1.3 %copy-done = bf16[16,256,256]{2,1,0:T(8,128)(2,1)} copy-done((bf16[16,256,256]{2,1,0:T(8,128)(2,1)}, bf16[16,256,256]{2,1,0:T(8,128)(2,1)S(1)}, u32[]{:S(2)}) %copy-start) | copy-done | bytes 2097176
  6.8 0.0 copy-start.6
  6.8 0.0 copy-start.7
  6.8 0.0 copy-start.5
  6.8 6.7 %all-to-all-start = ((bf16[16,256,256]{2,1,0:T(8,128)(2,1)}), bf16[16,256,256]{2,1,0:T(8,128)(2,1)S(1)}, u32[]{:S(2)}, u32[]{:S(2)}) async-start(bf16[16,256,256]{2,1,0:T(8,128)(2,1)} %copy-done), calls=%async_computation | async-start | bytes 4194304 | tf_op jit(solution)/shard_map/all_to_all | solution.py:137
  13.5 0.0 copy-done.6
  13.5 0.1 copy.11.owner_ref
  13.6 0.0 copy-done.7
  13.6 0.1 copy.12.local_ref
  13.7 45.8 %all-to-all-done = bf16[16,256,256]{2,1,0:T(8,128)(2,1)S(1)} async-done(((bf16[16,256,256]{2,1,0:T(8,128)(2,1)}), bf16[16,256,256]{2,1,0:T(8,128)(2,1)S(1)}, u32[]{:S(2)}, u32[]{:S(2)}) %all-to-all-start) | async-done | bytes 2097184 | tf_op jit(solution)/shard_map/all_to_all | solution.py:137
  59.5 0.0 copy-done.5
  59.5 13.4 %shard_map.103 = bf16[4096,256]{1,0:T(8,128)(2,1)S(1)} custom-call(s32[2]{0:T(128)S(1)} %copy-done.5, s32[64,6]{1,0:T(8,128)S(1)} %copy.11.owner_ref, s32[64,6]{1,0:T(8,128)S(1)} %copy.12.local_ref, bf16[4096,256]{1,0:T(8,128)(2,1)S(1)} %bitcast.2), custom_call_target="tpu_custom_call" | custom-call | tf_op jit(solution)/shard_map/pallas_call | solution.py:138
  72.9 54.0 %all_to_all.10.in_ref = bf16[16,256,256]{2,1,0:T(8,128)(2,1)S(1)} all-to-all(bf16[16,256,256]{2,1,0:T(8,128)(2,1)S(1)} %bitcast.3), channel_id=1, replica_groups=mesh['groups'=2,'ctx'=16] {'ctx'}, dimensions={0} | all-to-all | bytes 4194304 | tf_op jit(solution)/shard_map/all_to_all | solution.py:146
  126.9 1.9 %shard_map.104 = (bf16[256,1024]{1,0:T(8,128)(2,1)}, bf16[256,1024]{1,0:T(8,128)(2,1)}, bf16[256,1024]{1,0:T(8,128)(2,1)}, bf16[256,1024]{1,0:T(8,128)(2,1)}) custom-call(bf16[16,256,256]{2,1,0:T(8,128)(2,1)S(1)} %all_to_all.10.in_ref), custom_call_target="tpu_custom_call" | custom-call | tf_op jit(solution)/shard_map/pallas_call | solution.py:147
Async XLA Ops:
  0.6 1.0 copy-start.1
  1.7 1.0 copy-start.2
  2.7 1.0 copy-start.3
  3.8 1.0 copy-start.4
  5.4 1.3 %copy-start = (bf16[16,256,256]{2,1,0:T(8,128)(2,1)}, bf16[16,256,256]{2,1,0:T(8,128)(2,1)S(1)}, u32[]{:S(2)}) copy-start(bf16[16,256,256]{2,1,0:T(8,128)(2,1)S(1)} %shard_map.102) | copy-start | bytes 6291460
  6.8 6.8 %copy-start.6 = (s32[64,6]{0,1:T(8,128)S(1)}, s32[64,6]{0,1:T(8,128)}, u32[]{:S(2)}) copy-start(s32[64,6]{0,1:T(8,128)} %param.12) | copy-start | bytes 4612
  6.8 6.9 %copy-start.7 = (s32[64,6]{0,1:T(8,128)S(1)}, s32[64,6]{0,1:T(8,128)}, u32[]{:S(2)}) copy-start(s32[64,6]{0,1:T(8,128)} %param.13) | copy-start | bytes 4612
  6.8 52.7 %copy-start.5 = (s32[2]{0:T(128)S(1)}, s32[2]{0:T(128)}, u32[]{:S(2)}) copy-start(s32[2]{0:T(128)} %glob_ref.1) | copy-start | bytes 28
  6.8 52.7 %all-to-all-start = ((bf16[16,256,256]{2,1,0:T(8,128)(2,1)}), bf16[16,256,256]{2,1,0:T(8,128)(2,1)S(1)}, u32[]{:S(2)}, u32[]{:S(2)}) async-start(bf16[16,256,256]{2,1,0:T(8,128)(2,1)} %copy-done), calls=%async_computation | async-start | bytes 4194304 | tf_op jit(solution)/shard_map/all_to_all | solution.py:137

commit v3 on v2

v3 whole, which is shorter than its diff:
```python
import functools
import math

import jax
import jax.numpy as jnp
from jax import lax
from jax.experimental import pallas as pl
from jax.experimental.pallas import tpu as pltpu
from jax.sharding import PartitionSpec as P

HEAD_DIM = 64
GROUP_HEADS = 8
BLOCK = 64
GLOBALS = 2
ROUNDS = 3
KINDS = 3 + GLOBALS + ROUNDS
SPAN = KINDS * BLOCK
PAIR = 2 * HEAD_DIM
NEG_FILL = -1e30
UNROLL = 8
CHUNKS = 4
SCALE = HEAD_DIM ** -0.5
EXP_SCALE = SCALE * math.log2(math.e)
VMEM = pl.BlockSpec(memory_space=pltpu.VMEM)
SMEM = pl.BlockSpec(memory_space=pltpu.SMEM)
HBM = pl.BlockSpec(memory_space=pltpu.HBM)


def pack_kernel(repeat, q_ref, k_ref, v_ref, c_ref, out_ref, buf_ref, tile_ref, sems, out_sems):
    tokens, features = q_ref.shape
    size = tokens // CHUNKS
    copies = []
    for t in range(CHUNKS):
        rows = pl.ds(t * size, size)
        copies.append(
            [
                pltpu.make_async_copy(ref.at[rows], buf_ref.at[n, rows], sems.at[n, t])
                for n, ref in enumerate((k_ref, v_ref, q_ref, c_ref))
            ]
        )
    for one in copies:
        for copy in one:
            copy.start()
    sent = []
    for t in range(CHUNKS):
        for copy in copies[t]:
            copy.wait()
        rows = pl.ds(t * size, size)
        for half in range(2):
            place = pl.ds(half * tokens + t * size, size)
            for pair in range(features // PAIR):
                cols = pl.ds(pair * PAIR, PAIR)
                first = buf_ref[2 * half, rows, cols]
                second = buf_ref[2 * half + 1, rows, cols]
                even = jnp.concatenate((first[:, :HEAD_DIM], second[:, :HEAD_DIM]), axis=1)
                odd = jnp.concatenate((first[:, HEAD_DIM:], second[:, HEAD_DIM:]), axis=1)
                for n in range(repeat):
                    tile_ref[2 * pair * repeat + n, place, :] = even
                    tile_ref[(2 * pair + 1) * repeat + n, place, :] = odd
            sent.append(
                pltpu.make_async_copy(tile_ref.at[:, place], out_ref.at[:, place], out_sems.at[half, t])
            )
            sent[-1].start()
    for copy in sent:
        copy.wait()


def unpack_kernel(repeat, in_ref, att_ref, dq_ref, dk_ref, dv_ref, buf_ref, sems):
    tokens, features = att_ref.shape
    size = tokens // CHUNKS
    copies = []
    for t in range(CHUNKS):
        rows = pl.ds(t * size, size)
        for half in range(2):
            place = pl.ds(half * tokens + t * size, size)
            for pair in range(features // PAIR):
                cols = pl.ds(pair * PAIR, PAIR)
                even = in_ref[2 * pair * repeat, place, :]
                odd = in_ref[(2 * pair + 1) * repeat, place, :]
                buf_ref[2 * half, rows, cols] = jnp.concatenate(
                    (even[:, :HEAD_DIM], odd[:, :HEAD_DIM]), axis=1
                )
                buf_ref[2 * half + 1, rows, cols] = jnp.concatenate(
                    (even[:, HEAD_DIM:], odd[:, HEAD_DIM:]), axis=1
                )
        for n, ref in enumerate((dq_ref, att_ref, dk_ref, dv_ref)):
            copies.append(pltpu.make_async_copy(buf_ref.at[n, rows], ref.at[rows], sems.at[n, t]))
            copies[-1].start()
    for copy in copies:
        copy.wait()


def attend_kernel(tokens, repeat, glob_ref, owner_ref, local_ref, in_ref, out_ref, acc_ref):
    per_device = tokens // BLOCK
    blocks = in_ref.shape[0] // (2 * BLOCK)
    group = lax.axis_index("ctx") // (repeat * GROUP_HEADS)
    acc_ref[...] = jnp.zeros_like(acc_ref)
    low = lax.broadcasted_iota(jnp.int32, (BLOCK, PAIR), 1) < HEAD_DIM
    place = lax.broadcasted_iota(jnp.int32, (1, SPAN), 1)

    def rows_at(owner, local):
        start = owner * (2 * tokens) + local * BLOCK
        return pl.ds(pl.multiple_of(start, BLOCK), BLOCK)

    def rows_of(i):
        return rows_at(lax.div(i, per_device), lax.rem(i, per_device))

    def load(i):
        rows = [rows_of(one) for one in (jnp.maximum(i - 1, 0), i, jnp.minimum(i + 1, blocks - 1))]
        rows += [rows_of(glob_ref[n]) for n in range(GLOBALS)]
        for n in range(ROUNDS):
            entry = group * ROUNDS + n
            rows.append(rows_at(owner_ref[entry, i], local_ref[entry, i]))
        kv = jnp.concatenate([in_ref[r, :] for r in rows], axis=0)
        mine = pl.ds(pl.multiple_of(rows[1].start + tokens, BLOCK), BLOCK)
        qc = in_ref[mine, :]
        zero = jnp.zeros_like(qc)
        return rows, kv, jnp.where(low, qc, zero), jnp.where(low, zero, qc)

    def products(kv, q_part, c_part):
        return lax.dot_general(
            jnp.concatenate((q_part, c_part), axis=0),
            kv,
            (((1,), (1,)), ((), ())),
            preferred_element_type=jnp.float32,
        )

    def softmax(i, both):
        absent = ((place < BLOCK) & (i == 0)) | (
            (place >= 2 * BLOCK) & (place < 3 * BLOCK) & (i == blocks - 1)
        )
        scores = jnp.where(absent, NEG_FILL, both[:BLOCK])
        dprob = both[BLOCK:]
        row_max = jnp.max(scores, axis=-1, keepdims=True)
        weights = jnp.exp2((scores - row_max) * EXP_SCALE)
        inverse = 1.0 / jnp.sum(weights, axis=-1, keepdims=True)
        row_dot = jnp.sum(weights * dprob, axis=-1, keepdims=True) * inverse
        probs = weights * inverse
        dscore = probs * (dprob - row_dot)
        return jnp.concatenate((probs.astype(jnp.bfloat16), dscore.astype(jnp.bfloat16)), axis=0)

    def query_side(row, kv, pd):
        res = jnp.dot(pd, kv, preferred_element_type=jnp.float32)
        out_ref[row, :] = jnp.where(low, res[BLOCK:] * SCALE, res[:BLOCK]).astype(jnp.bfloat16)

    def key_side(q_part, c_part, pd):
        return lax.dot_general(
            pd,
            jnp.concatenate((c_part, q_part), axis=0),
            (((0,), (0,)), ((), ())),
            preferred_element_type=jnp.float32,
        )

    def step(j):
        mine = [j * UNROLL + u for u in range(UNROLL)]
        loaded = [load(i) for i in mine]
        both = [products(*one[1:]) for one in loaded]
        pds = [softmax(i, one) for i, one in zip(mine, both)]
        terms = []
        for (rows, kv, q_part, c_part), pd in zip(loaded, pds):
            query_side(rows[1], kv, pd)
            terms.append(key_side(q_part, c_part, pd))
        for one, term in zip(loaded, terms):
            for n, r in enumerate(one[0]):
                acc_ref[r, :] += term[n * BLOCK : (n + 1) * BLOCK]

    pl.loop(0, blocks // UNROLL)(step)

    def finish(d):
        start = pl.multiple_of(d * (2 * tokens), tokens)
        acc = acc_ref[pl.ds(start, tokens), :]
        left = lax.broadcasted_iota(jnp.int32, acc.shape, 1) < HEAD_DIM
        result = jnp.where(left, acc * SCALE, acc).astype(jnp.bfloat16)
        out_ref[pl.ds(pl.multiple_of(start + tokens, tokens), tokens), :] = result

    pl.loop(0, blocks // per_device)(finish)


def per_device(query, key, value, cotangent, global_ids, rand_owner, rand_local):
    tokens, features = query.shape
    heads = features // HEAD_DIM
    devices = lax.axis_size("ctx")
    repeat = max(1, devices // heads)
    params = pltpu.CompilerParams(vmem_limit_bytes=48 << 20)
    scratch = [
        pltpu.VMEM((4, tokens, features), jnp.bfloat16),
        pltpu.SemaphoreType.DMA((4, CHUNKS)),
    ]
    packed = pl.pallas_call(
        functools.partial(pack_kernel, repeat),
        out_shape=jax.ShapeDtypeStruct((devices, 2 * tokens, PAIR), jnp.bfloat16),
        in_specs=[HBM] * 4,
        out_specs=HBM,
        scratch_shapes=[
            scratch[0],
            pltpu.VMEM((devices, 2 * tokens, PAIR), jnp.bfloat16),
            scratch[1],
            pltpu.SemaphoreType.DMA((2, CHUNKS)),
        ],
        compiler_params=pltpu.CompilerParams(vmem_limit_bytes=60 << 20),
    )(query, key, value, cotangent)
    arrived = lax.all_to_all(packed, "ctx", 0, 0, tiled=True)
    grads = pl.pallas_call(
        functools.partial(attend_kernel, tokens, repeat),
        out_shape=jax.ShapeDtypeStruct((devices * 2 * tokens, PAIR), jnp.bfloat16),
        in_specs=[SMEM] * 3 + [VMEM],
        out_specs=VMEM,
        scratch_shapes=[pltpu.VMEM((devices * 2 * tokens, PAIR), jnp.float32)],
        compiler_params=params,
    )(global_ids, rand_owner.T, rand_local.T, arrived.reshape(devices * 2 * tokens, PAIR))
    back = lax.all_to_all(grads.reshape(devices, 2 * tokens, PAIR), "ctx", 0, 0, tiled=True)
    return pl.pallas_call(
        functools.partial(unpack_kernel, repeat),
        out_shape=[jax.ShapeDtypeStruct((tokens, features), jnp.bfloat16)] * 4,
        in_specs=[VMEM],
        out_specs=[HBM] * 4,
        scratch_shapes=scratch,
        compiler_params=params,
    )(back)


def solution(mesh):
    split = P(("groups", "ctx"), None)
    return jax.shard_map(
        per_device,
        mesh=mesh,
        in_specs=(split, split, split, split, P("groups"), P("groups", None), P("groups", None)),
        out_specs=(split, split, split, split),
        check_vma=False,
    )
```

time: 130 us -> 125 us (0.962)
  blocking collectives: 54 us -> 107 us
  waiting for transfers between devices: 45.8 us -> 0 us
  starting transfers between devices: 6.74 us -> 0 us
  local copies, waits for them, and re-layouts: 5.69 us -> 0.02 us
    all_to_all x1 -> x2, blocking collectives: 54 us -> 107 us  [the longest x1 54.6 us: per_device(): arrived = lax.all_to_all(packed, 'ctx', 0, 0, tiled=True)]
    all_to_all x1 -> x0, waiting for transfers between devices: 45.8 us -> none  [per_device(): lax.all_to_all(packed, 'ctx', 0, 0, tiled=True)]
    all_to_all x1 -> x0, starting transfers between devices: 6.74 us -> none  [per_device(): lax.all_to_all(packed, 'ctx', 0, 0, tiled=True)]
    unnamed x18 -> x6, local copies, waits for them, and re-layouts: 5.69 us -> 0.02 us
    pallas_call x1, Pallas kernels: 0.61 us -> 2.92 us  [per_device(): pl.pallas_call(functools.partial(pack_kernel, repeat), out_shape=jax.Shap...]
  transfers between devices with their start and end apart: 1 -> 0, of which waited for: 1 -> 0; matrix products, arithmetic and copies ran while one was open for 0% -> 0% of each run, Pallas kernels for 0% -> 0%
where the time goes in v3:
time: 125 us
  blocking collectives  107 us (86%)
  Pallas kernels  17.1 us (14%)
    all_to_all x1, blocking collectives, per_device(): arrived = lax.all_to_all(packed, 'ctx', 0, 0, tiled=True)  54.6 us
    all_to_all x1, blocking collectives, per_device(): lax.all_to_all(grads.reshape(devices, 2 * tokens, PAIR), 'ctx', 0, 0, til...  52.2 us
    pallas_call x1, Pallas kernels, per_device(): pl.pallas_call(functools.partial(attend_kernel, tokens, repeat), out_shap...  12.5 us
    pallas_call x1, Pallas kernels, per_device(): pl.pallas_call(functools.partial(pack_kernel, repeat), out_shape=jax.Shap...  2.92 us

profile of v3, /device:TPU:9, one launch (start us, length us, event | category | flops | bytes accessed | tf_op | source)
XLA Modules:
  0.0 124.6 jit_solution(14227678477846784832)
XLA Ops:
  0.6 2.9 %shard_map.102 = bf16[16,512,128]{2,1,0:T(8,128)(2,1)} custom-call(bf16[256,1024]{1,0:T(8,128)(2,1)} %q_ref.1, bf16[256,1024]{1,0:T(8,128)(2,1)} %k_ref.1, bf16[256,1024]{1,0:T(8,128)(2,1)} %v_ref.1, bf16[256,1024]{1,0:T(8,128)(2,1)} %c_ref.1), custom_call_target="tpu_custom_call" | custom-call | tf_op jit(solution)/shard_map/pallas_call | solution.py:189
  3.6 0.0 copy-start
  3.6 0.0 copy-start.1
  3.6 0.0 copy-start.2
  3.6 54.6 %all_to_all.10 = bf16[16,512,128]{2,1,0:T(8,128)(2,1)S(1)} all-to-all(bf16[16,512,128]{2,1,0:T(8,128)(2,1)} %shard_map.102), channel_id=1, replica_groups=mesh['groups'=2,'ctx'=16] {'ctx'}, dimensions={0} | all-to-all | bytes 4194304 | tf_op jit(solution)/shard_map/all_to_all | solution.py:202
  58.2 0.0 copy-done
  58.2 0.0 copy-done.1
  58.2 0.0 copy-done.2
  58.2 12.5 %shard_map.103 = bf16[8192,128]{1,0:T(8,128)(2,1)S(1)} custom-call(s32[2]{0:T(128)S(1)} %copy-done.2, s32[6,64]{1,0:T(8,128)S(1)} %bitcast.6, s32[6,64]{1,0:T(8,128)S(1)} %bitcast.7, bf16[8192,128]{1,0:T(8,128)(2,1)S(1)} %bitcast.4), custom_call_target="tpu_custom_call" | custom-call | tf_op jit(solution)/shard_map/pallas_call | solution.py:203
  70.7 52.2 %all_to_all.11.in_ref = bf16[16,512,128]{2,1,0:T(8,128)(2,1)S(1)} all-to-all(bf16[16,512,128]{2,1,0:T(8,128)(2,1)S(1)} %bitcast.5), channel_id=1, replica_groups=mesh['groups'=2,'ctx'=16] {'ctx'}, dimensions={0} | all-to-all | bytes 4194304 | tf_op jit(solution)/shard_map/all_to_all | solution.py:211
  122.9 1.7 %shard_map.104 = (bf16[256,1024]{1,0:T(8,128)(2,1)}, bf16[256,1024]{1,0:T(8,128)(2,1)}, bf16[256,1024]{1,0:T(8,128)(2,1)}, bf16[256,1024]{1,0:T(8,128)(2,1)}) custom-call(bf16[16,512,128]{2,1,0:T(8,128)(2,1)S(1)} %all_to_all.11.in_ref), custom_call_target="tpu_custom_call" | custom-call | tf_op jit(solution)/shard_map/pallas_call | solution.py:212
Async XLA Ops:
  3.6 54.6 %copy-start = (s32[64,6]{0,1:T(8,128)S(1)}, s32[64,6]{0,1:T(8,128)}, u32[]{:S(2)}) copy-start(s32[64,6]{0,1:T(8,128)} %param.12) | copy-start | bytes 4612
  3.6 54.6 %copy-start.1 = (s32[64,6]{0,1:T(8,128)S(1)}, s32[64,6]{0,1:T(8,128)}, u32[]{:S(2)}) copy-start(s32[64,6]{0,1:T(8,128)} %param.13) | copy-start | bytes 4612
  3.6 54.6 %copy-start.2 = (s32[2]{0:T(128)S(1)}, s32[2]{0:T(128)}, u32[]{:S(2)}) copy-start(s32[2]{0:T(128)} %glob_ref.1) | copy-start | bytes 28

commit v4 on v3

v4 whole, which is shorter than its diff:
```python
import functools
import math

import jax
import jax.numpy as jnp
from jax import lax
from jax.experimental import pallas as pl
from jax.experimental.pallas import tpu as pltpu
from jax.sharding import PartitionSpec as P

HEAD_DIM = 64
GROUP_HEADS = 8
BLOCK = 64
GLOBALS = 2
ROUNDS = 3
KINDS = 3 + GLOBALS + ROUNDS
SPAN = KINDS * BLOCK
PAIR = 2 * HEAD_DIM
NEG_FILL = -1e30
UNROLL = 8
CHUNKS = 4
TOGETHER = 2
SCALE = HEAD_DIM ** -0.5
EXP_SCALE = SCALE * math.log2(math.e)
VMEM = pl.BlockSpec(memory_space=pltpu.VMEM)
SMEM = pl.BlockSpec(memory_space=pltpu.SMEM)
HBM = pl.BlockSpec(memory_space=pltpu.HBM)


def halves(first, second):
    even = jnp.concatenate((first[:, :HEAD_DIM], second[:, :HEAD_DIM]), axis=1)
    odd = jnp.concatenate((first[:, HEAD_DIM:], second[:, HEAD_DIM:]), axis=1)
    return even, odd


def fill_tiles(first_ref, second_ref, tile_ref, place, repeat):
    for pair in range(first_ref.shape[-1] // PAIR):
        cols = pl.ds(pair * PAIR, PAIR)
        even, odd = halves(first_ref[:, cols], second_ref[:, cols])
        for n in range(repeat):
            tile_ref[2 * pair * repeat + n, place, :] = even
            tile_ref[(2 * pair + 1) * repeat + n, place, :] = odd


def send_far(tile_ref, far_refs, sems):
    count = len(far_refs)
    mine = lax.rem(lax.axis_index("ctx"), count)
    copies = []
    for m, ref in enumerate(far_refs):
        copies.append(pltpu.make_async_copy(tile_ref.at[mine ^ m], ref, sems.at[m]))
        copies[-1].start()
    return copies


def sides(refs, count):
    width = refs[0].shape[1] // 2
    upper = lax.div(lax.axis_index("ctx"), count)
    near = pl.ds(pl.multiple_of(upper * width, PAIR), width)
    far = pl.ds(pl.multiple_of((1 - upper) * width, PAIR), width)
    return near, far


def pack_keys_kernel(repeat, k_ref, v_ref, out_ref, buf_ref, tile_ref, sems, out_sems):
    size = k_ref.shape[0] // CHUNKS
    places = [pl.ds(t * size, size) for t in range(CHUNKS)]
    copies = []
    for t, rows in enumerate(places):
        for n, ref in enumerate((k_ref, v_ref)):
            copies.append(pltpu.make_async_copy(ref.at[rows], buf_ref.at[n, rows], sems.at[n, t]))
            copies[-1].start()
    sent = []
    for t, rows in enumerate(places):
        copies[2 * t].wait()
        copies[2 * t + 1].wait()
        fill_tiles(buf_ref.at[0, rows], buf_ref.at[1, rows], tile_ref, rows, repeat)
        sent.append(pltpu.make_async_copy(tile_ref.at[:, rows], out_ref.at[:, rows], out_sems.at[t]))
        sent[-1].start()
    for copy in sent:
        copy.wait()


def pack_queries_kernel(repeat, count, far, waits, q_ref, c_ref, *rest):
    rest = rest[waits:]
    out_refs, (buf_ref, tile_ref, sems, out_sems) = rest[:count], rest[count:]
    cols = sides((q_ref,), count)[far]
    copies = []
    for n, ref in enumerate((q_ref, c_ref)):
        copies.append(pltpu.make_async_copy(ref.at[:, cols], buf_ref.at[n], sems.at[n]))
        copies[-1].start()
    for copy in copies:
        copy.wait()
    fill_tiles(buf_ref.at[0], buf_ref.at[1], tile_ref, pl.ds(0, q_ref.shape[0]), repeat)
    for copy in send_far(tile_ref, out_refs, out_sems):
        copy.wait()


def unpack_kernel(repeat, in_ref, att_ref, dq_ref, dk_ref, dv_ref, buf_ref, sems):
    tokens, features = att_ref.shape
    size = tokens // CHUNKS
    copies = []
    for t in range(CHUNKS):
        rows = pl.ds(t * size, size)
        for half in range(2):
            place = pl.ds(half * tokens + t * size, size)
            for pair in range(features // PAIR):
                cols = pl.ds(pair * PAIR, PAIR)
                even = in_ref[2 * pair * repeat, place, :]
                odd = in_ref[(2 * pair + 1) * repeat, place, :]
                buf_ref[2 * half, rows, cols] = jnp.concatenate(
                    (even[:, :HEAD_DIM], odd[:, :HEAD_DIM]), axis=1
                )
                buf_ref[2 * half + 1, rows, cols] = jnp.concatenate(
                    (even[:, HEAD_DIM:], odd[:, HEAD_DIM:]), axis=1
                )
        for n, ref in enumerate((dq_ref, att_ref, dk_ref, dv_ref)):
            copies.append(pltpu.make_async_copy(buf_ref.at[n, rows], ref.at[rows], sems.at[n, t]))
            copies[-1].start()
    for copy in copies:
        copy.wait()


def attend(tables, kv_ref, acc_ref, blocks, group, items):
    glob_ref, owner_ref, local_ref = tables
    per_device = kv_ref.shape[0] // BLOCK // lax.axis_size("ctx")
    low = lax.broadcasted_iota(jnp.int32, (BLOCK, PAIR), 1) < HEAD_DIM
    place = lax.broadcasted_iota(jnp.int32, (1, SPAN), 1)

    def load(i, qc):
        ids = [jnp.maximum(i - 1, 0), i, jnp.minimum(i + 1, blocks - 1)]
        ids += [glob_ref[n] for n in range(GLOBALS)]
        for n in range(ROUNDS):
            entry = group * ROUNDS + n
            ids.append(owner_ref[entry, i] * per_device + local_ref[entry, i])
        rows = [pl.ds(pl.multiple_of(one * BLOCK, BLOCK), BLOCK) for one in ids]
        kv = jnp.concatenate([kv_ref[r, :] for r in rows], axis=0)
        zero = jnp.zeros_like(qc)
        return rows, kv, jnp.where(low, qc, zero), jnp.where(low, zero, qc)

    def products(kv, q_part, c_part):
        return lax.dot_general(
            jnp.concatenate((q_part, c_part), axis=0),
            kv,
            (((1,), (1,)), ((), ())),
            preferred_element_type=jnp.float32,
        )

    def softmax(i, both):
        absent = ((place < BLOCK) & (i == 0)) | (
            (place >= 2 * BLOCK) & (place < 3 * BLOCK) & (i == blocks - 1)
        )
        scores = jnp.where(absent, NEG_FILL, both[:BLOCK])
        dprob = both[BLOCK:]
        row_max = jnp.max(scores, axis=-1, keepdims=True)
        weights = jnp.exp2((scores - row_max) * EXP_SCALE)
        inverse = 1.0 / jnp.sum(weights, axis=-1, keepdims=True)
        row_dot = jnp.sum(weights * dprob, axis=-1, keepdims=True) * inverse
        probs = weights * inverse
        dscore = probs * (dprob - row_dot)
        return jnp.concatenate((probs.astype(jnp.bfloat16), dscore.astype(jnp.bfloat16)), axis=0)

    def query_side(kv, pd):
        res = jnp.dot(pd, kv, preferred_element_type=jnp.float32)
        return jnp.where(low, res[BLOCK:] * SCALE, res[:BLOCK]).astype(jnp.bfloat16)

    def key_side(q_part, c_part, pd):
        return lax.dot_general(
            pd,
            jnp.concatenate((c_part, q_part), axis=0),
            (((0,), (0,)), ((), ())),
            preferred_element_type=jnp.float32,
        )

    loaded = [load(i, qc) for i, qc, _ in items]
    both = [products(*one[1:]) for one in loaded]
    pds = [softmax(item[0], one) for item, one in zip(items, both)]
    terms = []
    for (_, kv, q_part, c_part), pd, item in zip(loaded, pds, items):
        item[2](query_side(kv, pd))
        terms.append(key_side(q_part, c_part, pd))
    for one, term in zip(loaded, terms):
        for n, r in enumerate(one[0]):
            acc_ref[r, :] += term[n * BLOCK : (n + 1) * BLOCK]


def my_group(repeat):
    return lax.axis_index("ctx") // (repeat * GROUP_HEADS)


def near_kernel(repeat, count, glob_ref, owner_ref, local_ref, kv_ref, *rest):
    qc_refs, (acc_ref, out_ref, near_ref) = rest[:count], rest[count:]
    tokens = qc_refs[0].shape[0]
    mine = lax.rem(lax.axis_index("ctx"), count)
    base = lax.axis_index("ctx") - mine
    blocks = kv_ref.shape[0] // BLOCK
    per_device = tokens // BLOCK
    acc_ref[...] = jnp.zeros_like(acc_ref)
    for m, ref in enumerate(qc_refs):
        near_ref[mine ^ m] = ref[...]

    def step(j):
        items = []
        for u in range(UNROLL):
            place = j * UNROLL + u
            device, local = lax.div(place, per_device), lax.rem(place, per_device)
            rows = pl.ds(pl.multiple_of(local * BLOCK, BLOCK), BLOCK)

            def put(value, device=device, rows=rows):
                out_ref[device, rows, :] = value

            items.append((base * per_device + place, near_ref[device, rows, :], put))
        attend((glob_ref, owner_ref, local_ref), kv_ref, acc_ref, blocks, my_group(repeat), items)

    pl.loop(0, count * per_device // UNROLL)(step)


def far_step(repeat, count, first, tables, kv_ref, qc_refs, acc_ref, out_refs):
    me = lax.axis_index("ctx")
    mine = lax.rem(me, count)
    base = me - mine
    items = []
    for m, (qc_ref, out_ref) in enumerate(zip(qc_refs, out_refs)):
        source = (count - base) + (mine ^ (first + m))
        per_device = qc_ref.shape[0] // BLOCK
        for local in range(per_device):
            rows = pl.ds(local * BLOCK, BLOCK)

            def put(value, out_ref=out_ref, rows=rows):
                out_ref[rows, :] = value

            items.append((source * per_device + local, qc_ref[rows, :], put))
    attend(tables, kv_ref, acc_ref, kv_ref.shape[0] // BLOCK, my_group(repeat), items)


def far_kernel(repeat, count, first, glob_ref, owner_ref, local_ref, kv_ref, acc_in_ref, *rest):
    qc_refs, acc_ref, out_refs = rest[:TOGETHER], rest[TOGETHER], rest[TOGETHER + 1 :]
    acc_ref[...] = acc_in_ref[...]
    far_step(repeat, count, first, (glob_ref, owner_ref, local_ref), kv_ref, qc_refs, acc_ref, out_refs)


def last_kernel(repeat, count, first, glob_ref, owner_ref, local_ref, kv_ref, acc_in_ref, *rest):
    qc_refs, near_ref, done_refs = rest[:TOGETHER], rest[TOGETHER], rest[TOGETHER + 1 : -3]
    out_ref, acc_ref, late_ref = rest[-3:]
    tokens = qc_refs[0].shape[0]
    me = lax.axis_index("ctx")
    mine = lax.rem(me, count)
    base = me - mine
    acc_ref[...] = acc_in_ref[...]
    late = [late_ref.at[m] for m in range(TOGETHER)]
    far_step(repeat, count, first, (glob_ref, owner_ref, local_ref), kv_ref, qc_refs, acc_ref, late)
    for j in range(count):
        out_ref[base + j, :tokens, :] = near_ref[j]
    for m, ref in enumerate(list(done_refs) + late):
        out_ref[(count - base) + (mine ^ m), :tokens, :] = ref[...]

    def finish(d):
        acc = acc_ref[pl.ds(pl.multiple_of(d * tokens, tokens), tokens), :]
        left = lax.broadcasted_iota(jnp.int32, acc.shape, 1) < HEAD_DIM
        out_ref[d, tokens:, :] = jnp.where(left, acc * SCALE, acc).astype(jnp.bfloat16)

    pl.loop(0, 2 * count)(finish)


def per_device(query, key, value, cotangent, global_ids, rand_owner, rand_local):
    tokens, features = query.shape
    heads = features // HEAD_DIM
    devices = lax.axis_size("ctx")
    repeat = max(1, devices // heads)
    count = devices // 2
    params = pltpu.CompilerParams(vmem_limit_bytes=48 << 20)
    roomy = pltpu.CompilerParams(vmem_limit_bytes=60 << 20)
    tile = jax.ShapeDtypeStruct((tokens, PAIR), jnp.bfloat16)

    packed = pl.pallas_call(
        functools.partial(pack_keys_kernel, repeat),
        out_shape=jax.ShapeDtypeStruct((devices, tokens, PAIR), jnp.bfloat16),
        in_specs=[HBM] * 2,
        out_specs=HBM,
        scratch_shapes=[
            pltpu.VMEM((2, tokens, features), jnp.bfloat16),
            pltpu.VMEM((devices, tokens, PAIR), jnp.bfloat16),
            pltpu.SemaphoreType.DMA((2, CHUNKS)),
            pltpu.SemaphoreType.DMA((CHUNKS,)),
        ],
        compiler_params=roomy,
    )(key, value)
    keys = lax.all_to_all(packed, "ctx", 0, 0, tiled=True).reshape(devices * tokens, PAIR)

    def swap(array, mask):
        return lax.ppermute(array, "ctx", [(i, i ^ mask) for i in range(devices)])

    def pack_queries(far, waits):
        return pl.pallas_call(
            functools.partial(pack_queries_kernel, repeat, count, far, len(waits)),
            out_shape=[tile] * count,
            in_specs=[HBM] * 2 + [pl.BlockSpec(memory_space=pl.ANY)] * len(waits),
            out_specs=[HBM] * count,
            scratch_shapes=[
                pltpu.VMEM((2, tokens, features // 2), jnp.bfloat16),
                pltpu.VMEM((count, tokens, PAIR), jnp.bfloat16),
                pltpu.SemaphoreType.DMA((2,)),
                pltpu.SemaphoreType.DMA((count,)),
            ],
            compiler_params=pltpu.CompilerParams(vmem_limit_bytes=16 << 20),
        )(query, cotangent, *waits)

    near_qc = pack_queries(0, [])
    near_qc = [one if m == 0 else swap(one, m) for m, one in enumerate(near_qc)]
    far_qc = pack_queries(1, [])
    far_qc = [swap(one, count + m) for m, one in enumerate(far_qc)]

    tables = (global_ids, rand_owner.T, rand_local.T)
    total = jax.ShapeDtypeStruct((devices * tokens, PAIR), jnp.float32)
    acc, near_out = pl.pallas_call(
        functools.partial(near_kernel, repeat, count),
        out_shape=[total, jax.ShapeDtypeStruct((count, tokens, PAIR), jnp.bfloat16)],
        in_specs=[SMEM] * 3 + [VMEM] * (1 + count),
        out_specs=[VMEM] * 2,
        scratch_shapes=[pltpu.VMEM((count, tokens, PAIR), jnp.bfloat16)],
        compiler_params=params,
        cost_estimate=pl.CostEstimate(flops=7 * 10**9, bytes_accessed=4 << 20, transcendentals=0),
    )(*tables, keys, *near_qc)
    done = []
    for first in range(0, count - TOGETHER, TOGETHER):
        acc, *outs = pl.pallas_call(
            functools.partial(far_kernel, repeat, count, first),
            out_shape=[total] + [tile] * TOGETHER,
            in_specs=[SMEM] * 3 + [VMEM] * (2 + TOGETHER),
            out_specs=[VMEM] * (1 + TOGETHER),
            compiler_params=params,
            cost_estimate=pl.CostEstimate(flops=2 * 10**9, bytes_accessed=4 << 20, transcendentals=0),
        )(*tables, keys, acc, *far_qc[first : first + TOGETHER])
        done += outs
    first = count - TOGETHER
    grads = pl.pallas_call(
        functools.partial(last_kernel, repeat, count, first),
        out_shape=jax.ShapeDtypeStruct((devices, 2 * tokens, PAIR), jnp.bfloat16),
        in_specs=[SMEM] * 3 + [VMEM] * (3 + count),
        out_specs=VMEM,
        scratch_shapes=[
            pltpu.VMEM((devices * tokens, PAIR), jnp.float32),
            pltpu.VMEM((TOGETHER, tokens, PAIR), jnp.bfloat16),
        ],
        compiler_params=params,
    )(*tables, keys, acc, *far_qc[first:], near_out, *done)
    back = lax.all_to_all(grads, "ctx", 0, 0, tiled=True)
    return pl.pallas_call(
        functools.partial(unpack_kernel, repeat),
        out_shape=[jax.ShapeDtypeStruct((tokens, features), jnp.bfloat16)] * 4,
        in_specs=[VMEM],
        out_specs=[HBM] * 4,
        scratch_shapes=[
            pltpu.VMEM((4, tokens, features), jnp.bfloat16),
            pltpu.SemaphoreType.DMA((4, CHUNKS)),
        ],
        compiler_params=params,
    )(back)


def solution(mesh):
    split = P(("groups", "ctx"), None)
    return jax.shard_map(
        per_device,
        mesh=mesh,
        in_specs=(split, split, split, split, P("groups"), P("groups", None), P("groups", None)),
        out_specs=(split, split, split, split),
        check_vma=False,
    )
```

time: 125 us -> 118 us (0.944)
  blocking collectives: 107 us -> 53.9 us
  starting transfers between devices: 0 us -> 30 us
  waiting for transfers between devices: 0 us -> 8.2 us
  Pallas kernels: 17.1 us -> 23 us
  local copies, waits for them, and re-layouts: 0.02 us -> 1.36 us
    all_to_all x2 -> x1, blocking collectives: 107 us -> 53.9 us  [per_device(): back = lax.all_to_all(grads, 'ctx', 0, 0, tiled=True)]
    ppermute x0 -> x15, starting transfers between devices: none -> 23.2 us  [swap(): return lax.ppermute(array, 'ctx', [(i, i ^ mask) for i in range(devices)])]
    ppermute x0 -> x15, waiting for transfers between devices: none -> 8.2 us  [swap(): return lax.ppermute(array, 'ctx', [(i, i ^ mask) for i in range(devices)])]
    all_to_all x0 -> x1, starting transfers between devices: none -> 6.75 us  [per_device(): lax.all_to_all(packed, 'ctx', 0, 0, tiled=True)]
    pallas_call x2 -> x8, Pallas kernels: 15.4 us -> 21.3 us  [the longest x1 6.71 us: per_device(): pl.pallas_call(functools.partial(near_kernel, repeat, count), out_shape=[...]
    unnamed x6 -> x12, local copies, waits for them, and re-layouts: 0.02 us -> 1.36 us
  transfers between devices with their start and end apart: 0 -> 16, of which waited for: 0 -> 5; matrix products, arithmetic and copies ran while one was open for 0% -> 0% of each run, Pallas kernels for 0% -> 13%
where the time goes in v4:
time: 118 us; the launch traced here: 117 us
  blocking collectives  53.9 us (46%)
  starting transfers between devices  30 us (25%)
  Pallas kernels  23 us (19%)
  waiting for transfers between devices  8.2 us (7%)
  local copies, waits for them, and re-layouts  1.36 us (1%)
    all_to_all x1, blocking collectives, per_device(): back = lax.all_to_all(grads, 'ctx', 0, 0, tiled=True)  53.9 us
    ppermute x15, starting transfers between devices, swap(): return lax.ppermute(array, 'ctx', [(i, i ^ mask) for i in range(devices)])  23.2 us
    ppermute x15, waiting for transfers between devices, swap(): return lax.ppermute(array, 'ctx', [(i, i ^ mask) for i in range(devices)])  8.2 us
    all_to_all x1, starting transfers between devices, per_device(): lax.all_to_all(packed, 'ctx', 0, 0, tiled=True)  6.75 us
    pallas_call x1, Pallas kernels, per_device(): pl.pallas_call(functools.partial(near_kernel, repeat, count), out_shape=[...  6.71 us
    pallas_call x3, Pallas kernels, per_device(): pl.pallas_call(functools.partial(far_kernel, repeat, count, first), out_s...  6.66 us
    pallas_call x1, Pallas kernels, per_device(): pl.pallas_call(functools.partial(last_kernel, repeat, count, first), out_...  3.48 us
    pallas_call x1, Pallas kernels, per_device(): pl.pallas_call(functools.partial(pack_keys_kernel, repeat), out_shape=jax...  2.44 us
  transfers between devices with their start and end apart: 16, of which 5 were waited for; matrix products, arithmetic and copies ran while one was open for 0% of the time, Pallas kernels for 13%

profile of v4, /device:TPU:9, one launch (start us, length us, event | category | flops | bytes accessed | tf_op | source)
XLA Modules:
  0.0 117.2 jit_solution(297098446092830812)
XLA Ops:
  0.7 2.4 %shard_map.102 = bf16[16,256,128]{2,1,0:T(8,128)(2,1)} custom-call(bf16[256,1024]{1,0:T(8,128)(2,1)} %k_ref.1, bf16[256,1024]{1,0:T(8,128)(2,1)} %v_ref.1), custom_call_target="tpu_custom_call" | custom-call | tf_op jit(solution)/shard_map/pallas_call | solution.py:273
  3.1 6.8 %all-to-all-start = ((bf16[16,256,128]{2,1,0:T(8,128)(2,1)}), bf16[16,256,128]{2,1,0:T(8,128)(2,1)S(1)}, u32[]{:S(2)}, u32[]{:S(2)}) async-start(bf16[16,256,128]{2,1,0:T(8,128)(2,1)} %shard_map.102), calls=%async_computation | async-start | bytes 2097152 | tf_op jit(solution)/shard_map/all_to_all | solution.py:286
  11.4 1.2 %collective-permute-start.1 = (bf16[256,128]{1,0:T(8,128)(2,1)S(1)}, bf16[256,128]{1,0:T(8,128)(2,1)S(1)}, u32[]{:S(2)}, u32[]{:S(2)}) collective-permute-start(bf16[256,128]{1,0:T(8,128)(2,1)S(1)} %get-tuple-element.33), channel_id=1, source_target_pairs={{0,2},{1,3},{2,0},{3,1},{4,6},{5,7},{6,4},{7,5},{8,10},{9,11},{10,... | collective-permute-start | bytes 196616 | tf_op jit(solution)/shard_map/ppermute | solution.py:289
  13.2 1.6 %collective-permute-start.4 = (bf16[256,128]{1,0:T(8,128)(2,1)S(1)}, bf16[256,128]{1,0:T(8,128)(2,1)S(1)}, u32[]{:S(2)}, u32[]{:S(2)}) collective-permute-start(bf16[256,128]{1,0:T(8,128)(2,1)S(1)} %get-tuple-element.36), channel_id=1, source_target_pairs={{0,5},{1,4},{2,7},{3,6},{4,1},{5,0},{6,3},{7,2},{8,13},{9,12},{10,... | collective-permute-start | bytes 196616 | tf_op jit(solution)/shard_map/ppermute | solution.py:289
  14.9 1.2 %collective-permute-start.5 = (bf16[256,128]{1,0:T(8,128)(2,1)S(1)}, bf16[256,128]{1,0:T(8,128)(2,1)S(1)}, u32[]{:S(2)}, u32[]{:S(2)}) collective-permute-start(bf16[256,128]{1,0:T(8,128)(2,1)S(1)} %get-tuple-element.37), channel_id=1, source_target_pairs={{0,6},{1,7},{2,4},{3,5},{4,2},{5,3},{6,0},{7,1},{8,14},{9,15},{10,... | collective-permute-start | bytes 196616 | tf_op jit(solution)/shard_map/ppermute | solution.py:289
  16.1 1.5 %collective-permute-done.1.rest_2_ = bf16[256,128]{1,0:T(8,128)(2,1)S(1)} collective-permute-done((bf16[256,128]{1,0:T(8,128)(2,1)S(1)}, bf16[256,128]{1,0:T(8,128)(2,1)S(1)}, u32[]{:S(2)}, u32[]{:S(2)}) %collective-permute-start.1) | collective-permute-done | bytes 65568 | tf_op jit(solution)/shard_map/ppermute | solution.py:289
  17.5 2.9 %collective-permute-start.6 = (bf16[256,128]{1,0:T(8,128)(2,1)S(1)}, bf16[256,128]{1,0:T(8,128)(2,1)S(1)}, u32[]{:S(2)}, u32[]{:S(2)}) collective-permute-start(bf16[256,128]{1,0:T(8,128)(2,1)S(1)} %get-tuple-element.38), channel_id=1, source_target_pairs={{0,7},{1,6},{2,5},{3,4},{4,3},{5,2},{6,1},{7,0},{8,15},{9,14},{10,... | collective-permute-start | bytes 196616 | tf_op jit(solution)/shard_map/ppermute | solution.py:289
  21.4 4.1 %collective-permute-start.7 = (bf16[256,128]{1,0:T(8,128)(2,1)S(1)}, bf16[256,128]{1,0:T(8,128)(2,1)S(1)}, u32[]{:S(2)}, u32[]{:S(2)}) collective-permute-start(bf16[256,128]{1,0:T(8,128)(2,1)S(1)} %get-tuple-element.40), channel_id=1, source_target_pairs={{0,8},{1,9},{2,10},{3,11},{4,12},{5,13},{6,14},{7,15},{8,0},{9,1},... | collective-permute-start | bytes 196616 | tf_op jit(solution)/shard_map/ppermute | solution.py:289
  25.6 4.2 %collective-permute-done.3.rest_4_ = bf16[256,128]{1,0:T(8,128)(2,1)S(1)} collective-permute-done((bf16[256,128]{1,0:T(8,128)(2,1)S(1)}, bf16[256,128]{1,0:T(8,128)(2,1)S(1)}, u32[]{:S(2)}, u32[]{:S(2)}) %collective-permute-start.3) | collective-permute-done | bytes 65568 | tf_op jit(solution)/shard_map/ppermute | solution.py:289
  29.8 2.1 %collective-permute-start.8 = (bf16[256,128]{1,0:T(8,128)(2,1)S(1)}, bf16[256,128]{1,0:T(8,128)(2,1)S(1)}, u32[]{:S(2)}, u32[]{:S(2)}) collective-permute-start(bf16[256,128]{1,0:T(8,128)(2,1)S(1)} %get-tuple-element.41), channel_id=1, source_target_pairs={{0,9},{1,8},{2,11},{3,10},{4,13},{5,12},{6,15},{7,14},{8,1},{9,0},... | collective-permute-start | bytes 196616 | tf_op jit(solution)/shard_map/ppermute | solution.py:289
  31.8 2.1 %collective-permute-start.9 = (bf16[256,128]{1,0:T(8,128)(2,1)S(1)}, bf16[256,128]{1,0:T(8,128)(2,1)S(1)}, u32[]{:S(2)}, u32[]{:S(2)}) collective-permute-start(bf16[256,128]{1,0:T(8,128)(2,1)S(1)} %get-tuple-element.43), channel_id=1, source_target_pairs={{0,10},{1,11},{2,8},{3,9},{4,14},{5,15},{6,12},{7,13},{8,2},{9,3},... | collective-permute-start | bytes 196616 | tf_op jit(solution)/shard_map/ppermute | solution.py:289
  34.0 1.7 %collective-permute-start.10 = (bf16[256,128]{1,0:T(8,128)(2,1)S(1)}, bf16[256,128]{1,0:T(8,128)(2,1)S(1)}, u32[]{:S(2)}, u32[]{:S(2)}) collective-permute-start(bf16[256,128]{1,0:T(8,128)(2,1)S(1)} %get-tuple-element.44), channel_id=1, source_target_pairs={{0,11},{1,10},{2,9},{3,8},{4,15},{5,14},{6,13},{7,12},{8,3},{9,2},... | collective-permute-start | bytes 196616 | tf_op jit(solution)/shard_map/ppermute | solution.py:289
  36.2 1.9 %collective-permute-start.11 = (bf16[256,128]{1,0:T(8,128)(2,1)S(1)}, bf16[256,128]{1,0:T(8,128)(2,1)S(1)}, u32[]{:S(2)}, u32[]{:S(2)}) collective-permute-start(bf16[256,128]{1,0:T(8,128)(2,1)S(1)} %get-tuple-element.46), channel_id=1, source_target_pairs={{0,12},{1,13},{2,14},{3,15},{4,8},{5,9},{6,10},{7,11},{8,4},{9,5},... | collective-permute-start | bytes 196616 | tf_op jit(solution)/shard_map/ppermute | solution.py:289
  38.1 6.7 %shard_map.104 = (f32[4096,128]{1,0:T(8,128)S(1)}, bf16[8,256,128]{2,1,0:T(8,128)(2,1)S(1)}) custom-call(s32[2]{0:T(128)S(1)} %copy-done.5, s32[6,64]{1,0:T(8,128)S(1)} %bitcast.8, s32[6,64]{1,0:T(8,128)S(1)} %bitcast.13, bf16[4096,128]{1,0:T(8,128)(2,1)S(1)} %bitcast.3, bf16[256,128]{1,0:T(8,128)(2,1)S(1)} %get-tuple-element.31.rest_0_, ...), custom_call_target="tpu_custom_call" | custom-call | flops 7000000000 | bytes 4194304 | tf_op jit(solution)/shard_map/pallas_call | solution.py:313
  45.0 2.0 %collective-permute-start.13 = (bf16[256,128]{1,0:T(8,128)(2,1)S(1)}, bf16[256,128]{1,0:T(8,128)(2,1)S(1)}, u32[]{:S(2)}, u32[]{:S(2)}) collective-permute-start(bf16[256,128]{1,0:T(8,128)(2,1)S(1)} %get-tuple-element.49), channel_id=1, source_target_pairs={{0,14},{1,15},{2,12},{3,13},{4,10},{5,11},{6,8},{7,9},{8,6},{9,7},... | collective-permute-start | bytes 196616 | tf_op jit(solution)/shard_map/ppermute | solution.py:289
  47.0 2.2 %shard_map.106 = (f32[4096,128]{1,0:T(8,128)S(1)}, bf16[256,128]{1,0:T(8,128)(2,1)S(1)}, bf16[256,128]{1,0:T(8,128)(2,1)S(1)}) custom-call(s32[2]{0:T(128)S(1)} %copy-done.5, s32[6,64]{1,0:T(8,128)S(1)} %bitcast.9, s32[6,64]{1,0:T(8,128)S(1)} %bitcast.14, bf16[4096,128]{1,0:T(8,128)(2,1)S(1)} %bitcast.4, f32[4096,128]{1,0:T(8,128)S(1)} %get-tuple-element.39.acc_in_ref, ...), custom_call_target="tpu_custom_call" | custom-call | flops 2000000000 | bytes 4194304 | tf_op jit(solution)/shard_map/pallas_call | solution.py:324
  49.3 1.1 collective-permute-start.14
  50.3 2.2 %shard_map.107 = (f32[4096,128]{1,0:T(8,128)S(1)}, bf16[256,128]{1,0:T(8,128)(2,1)S(1)}, bf16[256,128]{1,0:T(8,128)(2,1)S(1)}) custom-call(s32[2]{0:T(128)S(1)} %copy-done.5, s32[6,64]{1,0:T(8,128)S(1)} %bitcast.10, s32[6,64]{1,0:T(8,128)S(1)} %bitcast.15, bf16[4096,128]{1,0:T(8,128)(2,1)S(1)} %bitcast.5, f32[4096,128]{1,0:T(8,128)S(1)} %get-tuple-element.42.acc_in_ref, ...), custom_call_target="tpu_custom_call" | custom-call | flops 2000000000 | bytes 4194304 | tf_op jit(solution)/shard_map/pallas_call | solution.py:324
  52.8 2.2 %shard_map.108 = (f32[4096,128]{1,0:T(8,128)S(1)}, bf16[256,128]{1,0:T(8,128)(2,1)S(1)}, bf16[256,128]{1,0:T(8,128)(2,1)S(1)}) custom-call(s32[2]{0:T(128)S(1)} %copy-done.5, s32[6,64]{1,0:T(8,128)S(1)} %bitcast.11, s32[6,64]{1,0:T(8,128)S(1)} %bitcast.16, bf16[4096,128]{1,0:T(8,128)(2,1)S(1)} %bitcast.6, f32[4096,128]{1,0:T(8,128)S(1)} %get-tuple-element.45.acc_in_ref, ...), custom_call_target="tpu_custom_call" | custom-call | flops 2000000000 | bytes 4194304 | tf_op jit(solution)/shard_map/pallas_call | solution.py:324
  55.1 1.3 %copy-done = f32[4096,128]{1,0:T(8,128)} copy-done((f32[4096,128]{1,0:T(8,128)}, f32[4096,128]{1,0:T(8,128)S(1)}, u32[]{:S(2)}) %copy-start) | copy-done | bytes 2097176
  56.4 1.8 %collective-permute-done.14.rest_1_ = bf16[256,128]{1,0:T(8,128)(2,1)S(1)} collective-permute-done((bf16[256,128]{1,0:T(8,128)(2,1)S(1)}, bf16[256,128]{1,0:T(8,128)(2,1)S(1)}, u32[]{:S(2)}, u32[]{:S(2)}) %collective-permute-start.14) | collective-permute-done | bytes 65568 | tf_op jit(solution)/shard_map/ppermute | solution.py:289
  58.2 3.5 %shard_map.109 = bf16[16,512,128]{2,1,0:T(8,128)(2,1)S(1)} custom-call(s32[2]{0:T(128)S(1)} %copy-done.5, s32[6,64]{1,0:T(8,128)S(1)} %bitcast.12, s32[6,64]{1,0:T(8,128)S(1)} %bitcast.17, bf16[4096,128]{1,0:T(8,128)(2,1)S(1)} %bitcast.7, f32[4096,128]{1,0:T(8,128)} %copy-done, bf16[256,128]{1,0:T(8,128)(2,1)S(1)} %collective-permute-done.13.rest_0_, ...), custom_call_target="tpu_custom_call" | custom-call | tf_op jit(solution)/shard_map/pallas_call | solution.py:334
  61.7 53.9 %all_to_all.10.in_ref = bf16[16,512,128]{2,1,0:T(8,128)(2,1)S(1)} all-to-all(bf16[16,512,128]{2,1,0:T(8,128)(2,1)S(1)} %shard_map.109), channel_id=1, replica_groups=mesh['groups'=2,'ctx'=16] {'ctx'}, dimensions={0} | all-to-all | bytes 4194304 | tf_op jit(solution)/shard_map/all_to_all | solution.py:345
  115.6 1.7 %shard_map.110 = (bf16[256,1024]{1,0:T(8,128)(2,1)}, bf16[256,1024]{1,0:T(8,128)(2,1)}, bf16[256,1024]{1,0:T(8,128)(2,1)}, bf16[256,1024]{1,0:T(8,128)(2,1)}) custom-call(bf16[16,512,128]{2,1,0:T(8,128)(2,1)S(1)} %all_to_all.10.in_ref), custom_call_target="tpu_custom_call" | custom-call | tf_op jit(solution)/shard_map/pallas_call | solution.py:346
  (30 shorter events, 4.1 us)
Async XLA Ops:
  0.6 9.3 %copy-start.2 = (bf16[256,1024]{1,0:T(8,128)(2,1)S(1)}, bf16[256,1024]{1,0:T(8,128)(2,1)}, u32[]{:S(2)}) copy-start(bf16[256,1024]{1,0:T(8,128)(2,1)} %c_ref.3) | copy-start | bytes 1572868
  0.6 9.3 %copy-start.1 = (bf16[256,1024]{1,0:T(8,128)(2,1)S(1)}, bf16[256,1024]{1,0:T(8,128)(2,1)}, u32[]{:S(2)}) copy-start(bf16[256,1024]{1,0:T(8,128)(2,1)} %q_ref.3) | copy-start | bytes 1572868
  3.1 35.0 %copy-start.3 = (s32[64,6]{0,1:T(8,128)S(1)}, s32[64,6]{0,1:T(8,128)}, u32[]{:S(2)}) copy-start(s32[64,6]{0,1:T(8,128)} %param.12) | copy-start | bytes 4612
  3.1 35.0 %copy-start.4 = (s32[64,6]{0,1:T(8,128)S(1)}, s32[64,6]{0,1:T(8,128)}, u32[]{:S(2)}) copy-start(s32[64,6]{0,1:T(8,128)} %param.13) | copy-start | bytes 4612
  3.1 35.0 %copy-start.5 = (s32[2]{0:T(128)S(1)}, s32[2]{0:T(128)}, u32[]{:S(2)}) copy-start(s32[2]{0:T(128)} %glob_ref.9) | copy-start | bytes 28
  3.1 35.0 %all-to-all-start = ((bf16[16,256,128]{2,1,0:T(8,128)(2,1)}), bf16[16,256,128]{2,1,0:T(8,128)(2,1)S(1)}, u32[]{:S(2)}, u32[]{:S(2)}) async-start(bf16[16,256,128]{2,1,0:T(8,128)(2,1)} %shard_map.102), calls=%async_computation | async-start | bytes 2097152 | tf_op jit(solution)/shard_map/all_to_all | solution.py:286
  10.9 3.9 %collective-permute-start = (bf16[256,128]{1,0:T(8,128)(2,1)S(1)}, bf16[256,128]{1,0:T(8,128)(2,1)S(1)}, u32[]{:S(2)}, u32[]{:S(2)}) collective-permute-start(bf16[256,128]{1,0:T(8,128)(2,1)S(1)} %get-tuple-element.32), channel_id=1, source_target_pairs={{0,1},{1,0},{2,3},{3,2},{4,5},{5,4},{6,7},{7,6},{8,9},{9,8},{10,11... | collective-permute-start | bytes 196616 | tf_op jit(solution)/shard_map/ppermute | solution.py:289
  11.4 6.2 %collective-permute-start.1 = (bf16[256,128]{1,0:T(8,128)(2,1)S(1)}, bf16[256,128]{1,0:T(8,128)(2,1)S(1)}, u32[]{:S(2)}, u32[]{:S(2)}) collective-permute-start(bf16[256,128]{1,0:T(8,128)(2,1)S(1)} %get-tuple-element.33), channel_id=1, source_target_pairs={{0,2},{1,3},{2,0},{3,1},{4,6},{5,7},{6,4},{7,5},{8,10},{9,11},{10,... | collective-permute-start | bytes 196616 | tf_op jit(solution)/shard_map/ppermute | solution.py:289
  12.6 8.9 %collective-permute-start.2 = (bf16[256,128]{1,0:T(8,128)(2,1)S(1)}, bf16[256,128]{1,0:T(8,128)(2,1)S(1)}, u32[]{:S(2)}, u32[]{:S(2)}) collective-permute-start(bf16[256,128]{1,0:T(8,128)(2,1)S(1)} %get-tuple-element.34), channel_id=1, source_target_pairs={{0,3},{1,2},{2,1},{3,0},{4,7},{5,6},{6,5},{7,4},{8,11},{9,10},{10,... | collective-permute-start | bytes 196616 | tf_op jit(solution)/shard_map/ppermute | solution.py:289
  13.2 16.6 %collective-permute-start.3 = (bf16[256,128]{1,0:T(8,128)(2,1)S(1)}, bf16[256,128]{1,0:T(8,128)(2,1)S(1)}, u32[]{:S(2)}, u32[]{:S(2)}) collective-permute-start(bf16[256,128]{1,0:T(8,128)(2,1)S(1)} %get-tuple-element.35), channel_id=1, source_target_pairs={{0,4},{1,5},{2,6},{3,7},{4,0},{5,1},{6,2},{7,3},{8,12},{9,13},{10,... | collective-permute-start | bytes 196616 | tf_op jit(solution)/shard_map/ppermute | solution.py:289
  13.2 18.6 %collective-permute-start.4 = (bf16[256,128]{1,0:T(8,128)(2,1)S(1)}, bf16[256,128]{1,0:T(8,128)(2,1)S(1)}, u32[]{:S(2)}, u32[]{:S(2)}) collective-permute-start(bf16[256,128]{1,0:T(8,128)(2,1)S(1)} %get-tuple-element.36), channel_id=1, source_target_pairs={{0,5},{1,4},{2,7},{3,6},{4,1},{5,0},{6,3},{7,2},{8,13},{9,12},{10,... | collective-permute-start | bytes 196616 | tf_op jit(solution)/shard_map/ppermute | solution.py:289
  14.9 19.1 %collective-permute-start.5 = (bf16[256,128]{1,0:T(8,128)(2,1)S(1)}, bf16[256,128]{1,0:T(8,128)(2,1)S(1)}, u32[]{:S(2)}, u32[]{:S(2)}) collective-permute-start(bf16[256,128]{1,0:T(8,128)(2,1)S(1)} %get-tuple-element.37), channel_id=1, source_target_pairs={{0,6},{1,7},{2,4},{3,5},{4,2},{5,3},{6,0},{7,1},{8,14},{9,15},{10,... | collective-permute-start | bytes 196616 | tf_op jit(solution)/shard_map/ppermute | solution.py:289
  17.5 18.6 %collective-permute-start.6 = (bf16[256,128]{1,0:T(8,128)(2,1)S(1)}, bf16[256,128]{1,0:T(8,128)(2,1)S(1)}, u32[]{:S(2)}, u32[]{:S(2)}) collective-permute-start(bf16[256,128]{1,0:T(8,128)(2,1)S(1)} %get-tuple-element.38), channel_id=1, source_target_pairs={{0,7},{1,6},{2,5},{3,4},{4,3},{5,2},{6,1},{7,0},{8,15},{9,14},{10,... | collective-permute-start | bytes 196616 | tf_op jit(solution)/shard_map/ppermute | solution.py:289
  21.4 23.4 %collective-permute-start.7 = (bf16[256,128]{1,0:T(8,128)(2,1)S(1)}, bf16[256,128]{1,0:T(8,128)(2,1)S(1)}, u32[]{:S(2)}, u32[]{:S(2)}) collective-permute-start(bf16[256,128]{1,0:T(8,128)(2,1)S(1)} %get-tuple-element.40), channel_id=1, source_target_pairs={{0,8},{1,9},{2,10},{3,11},{4,12},{5,13},{6,14},{7,15},{8,0},{9,1},... | collective-permute-start | bytes 196616 | tf_op jit(solution)/shard_map/ppermute | solution.py:289
  29.8 15.3 %collective-permute-start.8 = (bf16[256,128]{1,0:T(8,128)(2,1)S(1)}, bf16[256,128]{1,0:T(8,128)(2,1)S(1)}, u32[]{:S(2)}, u32[]{:S(2)}) collective-permute-start(bf16[256,128]{1,0:T(8,128)(2,1)S(1)} %get-tuple-element.41), channel_id=1, source_target_pairs={{0,9},{1,8},{2,11},{3,10},{4,13},{5,12},{6,15},{7,14},{8,1},{9,0},... | collective-permute-start | bytes 196616 | tf_op jit(solution)/shard_map/ppermute | solution.py:289
  31.8 17.4 %collective-permute-start.9 = (bf16[256,128]{1,0:T(8,128)(2,1)S(1)}, bf16[256,128]{1,0:T(8,128)(2,1)S(1)}, u32[]{:S(2)}, u32[]{:S(2)}) collective-permute-start(bf16[256,128]{1,0:T(8,128)(2,1)S(1)} %get-tuple-element.43), channel_id=1, source_target_pairs={{0,10},{1,11},{2,8},{3,9},{4,14},{5,15},{6,12},{7,13},{8,2},{9,3},... | collective-permute-start | bytes 196616 | tf_op jit(solution)/shard_map/ppermute | solution.py:289
  34.0 16.3 %collective-permute-start.10 = (bf16[256,128]{1,0:T(8,128)(2,1)S(1)}, bf16[256,128]{1,0:T(8,128)(2,1)S(1)}, u32[]{:S(2)}, u32[]{:S(2)}) collective-permute-start(bf16[256,128]{1,0:T(8,128)(2,1)S(1)} %get-tuple-element.44), channel_id=1, source_target_pairs={{0,11},{1,10},{2,9},{3,8},{4,15},{5,14},{6,13},{7,12},{8,3},{9,2},... | collective-permute-start | bytes 196616 | tf_op jit(solution)/shard_map/ppermute | solution.py:289
  36.2 16.4 %collective-permute-start.11 = (bf16[256,128]{1,0:T(8,128)(2,1)S(1)}, bf16[256,128]{1,0:T(8,128)(2,1)S(1)}, u32[]{:S(2)}, u32[]{:S(2)}) collective-permute-start(bf16[256,128]{1,0:T(8,128)(2,1)S(1)} %get-tuple-element.46), channel_id=1, source_target_pairs={{0,12},{1,13},{2,14},{3,15},{4,8},{5,9},{6,10},{7,11},{8,4},{9,5},... | collective-permute-start | bytes 196616 | tf_op jit(solution)/shard_map/ppermute | solution.py:289
  44.9 8.0 %collective-permute-start.12 = (bf16[256,128]{1,0:T(8,128)(2,1)S(1)}, bf16[256,128]{1,0:T(8,128)(2,1)S(1)}, u32[]{:S(2)}, u32[]{:S(2)}) collective-permute-start(bf16[256,128]{1,0:T(8,128)(2,1)S(1)} %get-tuple-element.47), channel_id=1, source_target_pairs={{0,13},{1,12},{2,15},{3,14},{4,9},{5,8},{6,11},{7,10},{8,5},{9,4},... | collective-permute-start | bytes 196616 | tf_op jit(solution)/shard_map/ppermute | solution.py:289
  45.0 11.4 %collective-permute-start.13 = (bf16[256,128]{1,0:T(8,128)(2,1)S(1)}, bf16[256,128]{1,0:T(8,128)(2,1)S(1)}, u32[]{:S(2)}, u32[]{:S(2)}) collective-permute-start(bf16[256,128]{1,0:T(8,128)(2,1)S(1)} %get-tuple-element.49), channel_id=1, source_target_pairs={{0,14},{1,15},{2,12},{3,13},{4,10},{5,11},{6,8},{7,9},{8,6},{9,7},... | collective-permute-start | bytes 196616 | tf_op jit(solution)/shard_map/ppermute | solution.py:289
  49.3 8.9 %collective-permute-start.14 = (bf16[256,128]{1,0:T(8,128)(2,1)S(1)}, bf16[256,128]{1,0:T(8,128)(2,1)S(1)}, u32[]{:S(2)}, u32[]{:S(2)}) collective-permute-start(bf16[256,128]{1,0:T(8,128)(2,1)S(1)} %get-tuple-element.50), channel_id=1, source_target_pairs={{0,15},{1,14},{2,13},{3,12},{4,11},{5,10},{6,9},{7,8},{8,7},{9,6},... | collective-permute-start | bytes 196616 | tf_op jit(solution)/shard_map/ppermute | solution.py:289
  55.0 1.3 %copy-start = (f32[4096,128]{1,0:T(8,128)}, f32[4096,128]{1,0:T(8,128)S(1)}, u32[]{:S(2)}) copy-start(f32[4096,128]{1,0:T(8,128)S(1)} %get-tuple-element.48.acc_in_ref) | copy-start | bytes 6291460

commit v5 on v4

--- a/solution.py
+++ b/solution.py
@@ -19,7 +19,7 @@
 NEG_FILL = -1e30
 UNROLL = 8
 CHUNKS = 4
-TOGETHER = 2
+PARTS = (4, 2, 2)
 SCALE = HEAD_DIM ** -0.5
 EXP_SCALE = SCALE * math.log2(math.e)
 VMEM = pl.BlockSpec(memory_space=pltpu.VMEM)
@@ -227,25 +227,27 @@
             def put(value, out_ref=out_ref, rows=rows):
                 out_ref[rows, :] = value
 
-            items.append((source * per_device + local, qc_ref[rows, :], put))
-    attend(tables, kv_ref, acc_ref, kv_ref.shape[0] // BLOCK, my_group(repeat), items)
-
-
-def far_kernel(repeat, count, first, glob_ref, owner_ref, local_ref, kv_ref, acc_in_ref, *rest):
-    qc_refs, acc_ref, out_refs = rest[:TOGETHER], rest[TOGETHER], rest[TOGETHER + 1 :]
+            items.append((source * per_device + local, qc_ref, rows, put))
+    for start in range(0, len(items), UNROLL):
+        now = [(i, ref[rows, :], put) for i, ref, rows, put in items[start : start + UNROLL]]
+        attend(tables, kv_ref, acc_ref, kv_ref.shape[0] // BLOCK, my_group(repeat), now)
+
+
+def far_kernel(repeat, count, first, size, glob_ref, owner_ref, local_ref, kv_ref, acc_in_ref, *rest):
+    qc_refs, acc_ref, out_refs = rest[:size], rest[size], rest[size + 1 :]
     acc_ref[...] = acc_in_ref[...]
     far_step(repeat, count, first, (glob_ref, owner_ref, local_ref), kv_ref, qc_refs, acc_ref, out_refs)
 
 
-def last_kernel(repeat, count, first, glob_ref, owner_ref, local_ref, kv_ref, acc_in_ref, *rest):
-    qc_refs, near_ref, done_refs = rest[:TOGETHER], rest[TOGETHER], rest[TOGETHER + 1 : -3]
+def last_kernel(repeat, count, first, size, glob_ref, owner_ref, local_ref, kv_ref, acc_in_ref, *rest):
+    qc_refs, near_ref, done_refs = rest[:size], rest[size], rest[size + 1 : -3]
     out_ref, acc_ref, late_ref = rest[-3:]
     tokens = qc_refs[0].shape[0]
     me = lax.axis_index("ctx")
     mine = lax.rem(me, count)
     base = me - mine
     acc_ref[...] = acc_in_ref[...]
-    late = [late_ref.at[m] for m in range(TOGETHER)]
+    late = [late_ref.at[m] for m in range(size)]
     far_step(repeat, count, first, (glob_ref, owner_ref, local_ref), kv_ref, qc_refs, acc_ref, late)
     for j in range(count):
         out_ref[base + j, :tokens, :] = near_ref[j]
@@ -266,7 +268,7 @@
     devices = lax.axis_size("ctx")
     repeat = max(1, devices // heads)
     count = devices // 2
-    params = pltpu.CompilerParams(vmem_limit_bytes=48 << 20)
+    params = pltpu.CompilerParams(vmem_limit_bytes=24 << 20)
     roomy = pltpu.CompilerParams(vmem_limit_bytes=60 << 20)
     tile = jax.ShapeDtypeStruct((tokens, PAIR), jnp.bfloat16)
 
@@ -320,25 +322,27 @@
         cost_estimate=pl.CostEstimate(flops=7 * 10**9, bytes_accessed=4 << 20, transcendentals=0),
     )(*tables, keys, *near_qc)
     done = []
-    for first in range(0, count - TOGETHER, TOGETHER):
+    *sizes, size = [count * part // sum(PARTS) for part in PARTS]
+    first = 0
+    for some in sizes:
         acc, *outs = pl.pallas_call(
-            functools.partial(far_kernel, repeat, count, first),
-            out_shape=[total] + [tile] * TOGETHER,
-            in_specs=[SMEM] * 3 + [VMEM] * (2 + TOGETHER),
-            out_specs=[VMEM] * (1 + TOGETHER),
+            functools.partial(far_kernel, repeat, count, first, some),
+            out_shape=[total] + [tile] * some,
+            in_specs=[SMEM] * 3 + [VMEM] * (2 + some),
+            out_specs=[VMEM] * (1 + some),
             compiler_params=params,
-            cost_estimate=pl.CostEstimate(flops=2 * 10**9, bytes_accessed=4 << 20, transcendentals=0),
-        )(*tables, keys, acc, *far_qc[first : first + TOGETHER])
+            cost_estimate=pl.CostEstimate(flops=some * 10**9, bytes_accessed=4 << 20, transcendentals=0),
+        )(*tables, keys, acc, *far_qc[first : first + some])
         done += outs
-    first = count - TOGETHER
+        first += some
     grads = pl.pallas_call(
-        functools.partial(last_kernel, repeat, count, first),
+        functools.partial(last_kernel, repeat, count, first, size),
         out_shape=jax.ShapeDtypeStruct((devices, 2 * tokens, PAIR), jnp.bfloat16),
         in_specs=[SMEM] * 3 + [VMEM] * (3 + count),
         out_specs=VMEM,
         scratch_shapes=[
             pltpu.VMEM((devices * tokens, PAIR), jnp.float32),
-            pltpu.VMEM((TOGETHER, tokens, PAIR), jnp.bfloat16),
+            pltpu.VMEM((size, tokens, PAIR), jnp.bfloat16),
         ],
         compiler_params=params,
     )(*tables, keys, acc, *far_qc[first:], near_out, *done)

time: 118 us -> 115 us (0.975)
  waiting for transfers between devices: 8.2 us -> 10.7 us
  blocking collectives: 53.9 us -> 51.5 us
  Pallas kernels: 23 us -> 21 us
  local copies, waits for them, and re-layouts: 1.36 us -> 0.03 us
    ppermute x15, waiting for transfers between devices: 8.2 us -> 10.7 us  [swap(): return lax.ppermute(array, 'ctx', [(i, i ^ mask) for i in range(devices)])]
    all_to_all x1, blocking collectives: 53.9 us -> 51.5 us  [per_device(): back = lax.all_to_all(grads, 'ctx', 0, 0, tiled=True)]
    pallas_call x4 -> x3, Pallas kernels: 10.1 us -> 8.17 us  [the longest x2 5.61 us: per_device(): pl.pallas_call(functools.partial(far_kernel, repeat, count, first, some),...]
    unnamed x12 -> x10, local copies, waits for them, and re-layouts: 1.36 us -> 0.03 us
  transfers between devices with their start and end apart: 16 -> 16, of which waited for: 5 -> 6; matrix products, arithmetic and copies ran while one was open for 0% -> 0% of each run, Pallas kernels for 13% -> 13%
where the time goes in v5:
time: 115 us; the launch traced here: 114 us
  blocking collectives  51.5 us (45%)
  starting transfers between devices  29.9 us (26%)
  Pallas kernels  21 us (18%)
  waiting for transfers between devices  10.7 us (9%)
    all_to_all x1, blocking collectives, per_device(): back = lax.all_to_all(grads, 'ctx', 0, 0, tiled=True)  51.5 us
    ppermute x15, starting transfers between devices, swap(): return lax.ppermute(array, 'ctx', [(i, i ^ mask) for i in range(devices)])  23.1 us
    ppermute x15, waiting for transfers between devices, swap(): return lax.ppermute(array, 'ctx', [(i, i ^ mask) for i in range(devices)])  10.7 us
    all_to_all x1, starting transfers between devices, per_device(): lax.all_to_all(packed, 'ctx', 0, 0, tiled=True)  6.75 us
    pallas_call x1, Pallas kernels, per_device(): pl.pallas_call(functools.partial(near_kernel, repeat, count), out_shape=[...  6.71 us
    pallas_call x2, Pallas kernels, per_device(): pl.pallas_call(functools.partial(far_kernel, repeat, count, first, some),...  5.61 us
    pallas_call x1, Pallas kernels, per_device(): pl.pallas_call(functools.partial(last_kernel, repeat, count, first, size)...  2.56 us
    pallas_call x1, Pallas kernels, per_device(): pl.pallas_call(functools.partial(pack_keys_kernel, repeat), out_shape=jax...  2.42 us
  transfers between devices with their start and end apart: 16, of which 6 were waited for; matrix products, arithmetic and copies ran while one was open for 0% of the time, Pallas kernels for 13%

profile of v5, /device:TPU:9, one launch (start us, length us, event | category | flops | bytes accessed | tf_op | source)
XLA Modules:
  0.0 113.8 jit_solution(4216951529757375505)
XLA Ops:
  0.7 2.4 %shard_map.102 = bf16[16,256,128]{2,1,0:T(8,128)(2,1)} custom-call(bf16[256,1024]{1,0:T(8,128)(2,1)} %k_ref.1, bf16[256,1024]{1,0:T(8,128)(2,1)} %v_ref.1), custom_call_target="tpu_custom_call" | custom-call | tf_op jit(solution)/shard_map/pallas_call | solution.py:275
  3.1 6.8 %all-to-all-start = ((bf16[16,256,128]{2,1,0:T(8,128)(2,1)}), bf16[16,256,128]{2,1,0:T(8,128)(2,1)S(1)}, u32[]{:S(2)}, u32[]{:S(2)}) async-start(bf16[16,256,128]{2,1,0:T(8,128)(2,1)} %shard_map.102), calls=%async_computation | async-start | bytes 2097152 | tf_op jit(solution)/shard_map/all_to_all | solution.py:288
  9.9 1.0 shard_map.103
  11.4 1.2 %collective-permute-start.1 = (bf16[256,128]{1,0:T(8,128)(2,1)S(1)}, bf16[256,128]{1,0:T(8,128)(2,1)S(1)}, u32[]{:S(2)}, u32[]{:S(2)}) collective-permute-start(bf16[256,128]{1,0:T(8,128)(2,1)S(1)} %get-tuple-element.32), channel_id=1, source_target_pairs={{0,2},{1,3},{2,0},{3,1},{4,6},{5,7},{6,4},{7,5},{8,10},{9,11},{10,... | collective-permute-start | bytes 196616 | tf_op jit(solution)/shard_map/ppermute | solution.py:291
  13.2 1.6 %collective-permute-start.4 = (bf16[256,128]{1,0:T(8,128)(2,1)S(1)}, bf16[256,128]{1,0:T(8,128)(2,1)S(1)}, u32[]{:S(2)}, u32[]{:S(2)}) collective-permute-start(bf16[256,128]{1,0:T(8,128)(2,1)S(1)} %get-tuple-element.35), channel_id=1, source_target_pairs={{0,5},{1,4},{2,7},{3,6},{4,1},{5,0},{6,3},{7,2},{8,13},{9,12},{10,... | collective-permute-start | bytes 196616 | tf_op jit(solution)/shard_map/ppermute | solution.py:291
  14.9 1.2 %collective-permute-start.5 = (bf16[256,128]{1,0:T(8,128)(2,1)S(1)}, bf16[256,128]{1,0:T(8,128)(2,1)S(1)}, u32[]{:S(2)}, u32[]{:S(2)}) collective-permute-start(bf16[256,128]{1,0:T(8,128)(2,1)S(1)} %get-tuple-element.36), channel_id=1, source_target_pairs={{0,6},{1,7},{2,4},{3,5},{4,2},{5,3},{6,0},{7,1},{8,14},{9,15},{10,... | collective-permute-start | bytes 196616 | tf_op jit(solution)/shard_map/ppermute | solution.py:291
  16.0 1.5 %collective-permute-done.1.rest_2_ = bf16[256,128]{1,0:T(8,128)(2,1)S(1)} collective-permute-done((bf16[256,128]{1,0:T(8,128)(2,1)S(1)}, bf16[256,128]{1,0:T(8,128)(2,1)S(1)}, u32[]{:S(2)}, u32[]{:S(2)}) %collective-permute-start.1) | collective-permute-done | bytes 65568 | tf_op jit(solution)/shard_map/ppermute | solution.py:291
  17.5 2.9 %collective-permute-start.6 = (bf16[256,128]{1,0:T(8,128)(2,1)S(1)}, bf16[256,128]{1,0:T(8,128)(2,1)S(1)}, u32[]{:S(2)}, u32[]{:S(2)}) collective-permute-start(bf16[256,128]{1,0:T(8,128)(2,1)S(1)} %get-tuple-element.37), channel_id=1, source_target_pairs={{0,7},{1,6},{2,5},{3,4},{4,3},{5,2},{6,1},{7,0},{8,15},{9,14},{10,... | collective-permute-start | bytes 196616 | tf_op jit(solution)/shard_map/ppermute | solution.py:291
  21.4 4.1 %collective-permute-start.7 = (bf16[256,128]{1,0:T(8,128)(2,1)S(1)}, bf16[256,128]{1,0:T(8,128)(2,1)S(1)}, u32[]{:S(2)}, u32[]{:S(2)}) collective-permute-start(bf16[256,128]{1,0:T(8,128)(2,1)S(1)} %get-tuple-element.39), channel_id=1, source_target_pairs={{0,8},{1,9},{2,10},{3,11},{4,12},{5,13},{6,14},{7,15},{8,0},{9,1},... | collective-permute-start | bytes 196616 | tf_op jit(solution)/shard_map/ppermute | solution.py:291
  25.5 4.2 %collective-permute-done.3.rest_4_ = bf16[256,128]{1,0:T(8,128)(2,1)S(1)} collective-permute-done((bf16[256,128]{1,0:T(8,128)(2,1)S(1)}, bf16[256,128]{1,0:T(8,128)(2,1)S(1)}, u32[]{:S(2)}, u32[]{:S(2)}) %collective-permute-start.3) | collective-permute-done | bytes 65568 | tf_op jit(solution)/shard_map/ppermute | solution.py:291
  29.7 2.1 %collective-permute-start.8 = (bf16[256,128]{1,0:T(8,128)(2,1)S(1)}, bf16[256,128]{1,0:T(8,128)(2,1)S(1)}, u32[]{:S(2)}, u32[]{:S(2)}) collective-permute-start(bf16[256,128]{1,0:T(8,128)(2,1)S(1)} %get-tuple-element.40), channel_id=1, source_target_pairs={{0,9},{1,8},{2,11},{3,10},{4,13},{5,12},{6,15},{7,14},{8,1},{9,0},... | collective-permute-start | bytes 196616 | tf_op jit(solution)/shard_map/ppermute | solution.py:291
  31.8 2.1 %collective-permute-start.9 = (bf16[256,128]{1,0:T(8,128)(2,1)S(1)}, bf16[256,128]{1,0:T(8,128)(2,1)S(1)}, u32[]{:S(2)}, u32[]{:S(2)}) collective-permute-start(bf16[256,128]{1,0:T(8,128)(2,1)S(1)} %get-tuple-element.41), channel_id=1, source_target_pairs={{0,10},{1,11},{2,8},{3,9},{4,14},{5,15},{6,12},{7,13},{8,2},{9,3},... | collective-permute-start | bytes 196616 | tf_op jit(solution)/shard_map/ppermute | solution.py:291
  34.0 1.7 %collective-permute-start.10 = (bf16[256,128]{1,0:T(8,128)(2,1)S(1)}, bf16[256,128]{1,0:T(8,128)(2,1)S(1)}, u32[]{:S(2)}, u32[]{:S(2)}) collective-permute-start(bf16[256,128]{1,0:T(8,128)(2,1)S(1)} %get-tuple-element.42), channel_id=1, source_target_pairs={{0,11},{1,10},{2,9},{3,8},{4,15},{5,14},{6,13},{7,12},{8,3},{9,2},... | collective-permute-start | bytes 196616 | tf_op jit(solution)/shard_map/ppermute | solution.py:291
  36.2 1.9 %collective-permute-start.11 = (bf16[256,128]{1,0:T(8,128)(2,1)S(1)}, bf16[256,128]{1,0:T(8,128)(2,1)S(1)}, u32[]{:S(2)}, u32[]{:S(2)}) collective-permute-start(bf16[256,128]{1,0:T(8,128)(2,1)S(1)} %get-tuple-element.44), channel_id=1, source_target_pairs={{0,12},{1,13},{2,14},{3,15},{4,8},{5,9},{6,10},{7,11},{8,4},{9,5},... | collective-permute-start | bytes 196616 | tf_op jit(solution)/shard_map/ppermute | solution.py:291
  38.1 6.7 %shard_map.104 = (f32[4096,128]{1,0:T(8,128)S(1)}, bf16[8,256,128]{2,1,0:T(8,128)(2,1)S(1)}) custom-call(s32[2]{0:T(128)S(1)} %copy-done.4, s32[6,64]{1,0:T(8,128)S(1)} %bitcast.7, s32[6,64]{1,0:T(8,128)S(1)} %bitcast.11, bf16[4096,128]{1,0:T(8,128)(2,1)S(1)} %bitcast.3, bf16[256,128]{1,0:T(8,128)(2,1)S(1)} %get-tuple-element.30.rest_0_, ...), custom_call_target="tpu_custom_call" | custom-call | flops 7000000000 | bytes 4194304 | tf_op jit(solution)/shard_map/pallas_call | solution.py:315
  45.0 2.0 %collective-permute-start.13 = (bf16[256,128]{1,0:T(8,128)(2,1)S(1)}, bf16[256,128]{1,0:T(8,128)(2,1)S(1)}, u32[]{:S(2)}, u32[]{:S(2)}) collective-permute-start(bf16[256,128]{1,0:T(8,128)(2,1)S(1)} %get-tuple-element.47), channel_id=1, source_target_pairs={{0,14},{1,15},{2,12},{3,13},{4,10},{5,11},{6,8},{7,9},{8,6},{9,7},... | collective-permute-start | bytes 196616 | tf_op jit(solution)/shard_map/ppermute | solution.py:291
  48.0 3.4 %shard_map.106 = (f32[4096,128]{1,0:T(8,128)S(1)}, bf16[256,128]{1,0:T(8,128)(2,1)S(1)}, bf16[256,128]{1,0:T(8,128)(2,1)S(1)}, bf16[256,128]{1,0:T(8,128)(2,1)S(1)}, bf16[256,128]{1,0:T(8,128)(2,1)S(1)}) custom-call(s32[2]{0:T(128)S(1)} %copy-done.4, s32[6,64]{1,0:T(8,128)S(1)} %bitcast.8, s32[6,64]{1,0:T(8,128)S(1)} %bitcast.12, ...), custom_call_target="tpu_custom_call" | custom-call | flops 4000000000 | bytes 4194304 | tf_op jit(solution)/shard_map/pallas_call | solution.py:328
  51.4 1.4 %collective-permute-done.12.rest_1_ = bf16[256,128]{1,0:T(8,128)(2,1)S(1)} collective-permute-done((bf16[256,128]{1,0:T(8,128)(2,1)S(1)}, bf16[256,128]{1,0:T(8,128)(2,1)S(1)}, u32[]{:S(2)}, u32[]{:S(2)}) %collective-permute-start.12) | collective-permute-done | bytes 65568 | tf_op jit(solution)/shard_map/ppermute | solution.py:291
  52.8 2.2 %shard_map.107 = (f32[4096,128]{1,0:T(8,128)S(1)}, bf16[256,128]{1,0:T(8,128)(2,1)S(1)}, bf16[256,128]{1,0:T(8,128)(2,1)S(1)}) custom-call(s32[2]{0:T(128)S(1)} %copy-done.4, s32[6,64]{1,0:T(8,128)S(1)} %bitcast.9, s32[6,64]{1,0:T(8,128)S(1)} %bitcast.13, bf16[4096,128]{1,0:T(8,128)(2,1)S(1)} %bitcast.5, f32[4096,128]{1,0:T(8,128)S(1)} %get-tuple-element.43.acc_in_ref, ...), custom_call_target="tpu_custom_call" | custom-call | flops 2000000000 | bytes 4194304 | tf_op jit(solution)/shard_map/pallas_call | solution.py:328
  55.0 1.5 %collective-permute-done.13.rest_0_ = bf16[256,128]{1,0:T(8,128)(2,1)S(1)} collective-permute-done((bf16[256,128]{1,0:T(8,128)(2,1)S(1)}, bf16[256,128]{1,0:T(8,128)(2,1)S(1)}, u32[]{:S(2)}, u32[]{:S(2)}) %collective-permute-start.13) | collective-permute-done | bytes 65568 | tf_op jit(solution)/shard_map/ppermute | solution.py:291
  56.6 1.6 %collective-permute-done.14.rest_1_ = bf16[256,128]{1,0:T(8,128)(2,1)S(1)} collective-permute-done((bf16[256,128]{1,0:T(8,128)(2,1)S(1)}, bf16[256,128]{1,0:T(8,128)(2,1)S(1)}, u32[]{:S(2)}, u32[]{:S(2)}) %collective-permute-start.14) | collective-permute-done | bytes 65568 | tf_op jit(solution)/shard_map/ppermute | solution.py:291
  58.2 2.6 %shard_map.108 = bf16[16,512,128]{2,1,0:T(8,128)(2,1)S(1)} custom-call(s32[2]{0:T(128)S(1)} %copy-done.4, s32[6,64]{1,0:T(8,128)S(1)} %bitcast.10, s32[6,64]{1,0:T(8,128)S(1)} %bitcast.14, bf16[4096,128]{1,0:T(8,128)(2,1)S(1)} %bitcast.6, f32[4096,128]{1,0:T(8,128)S(1)} %get-tuple-element.46.acc_in_ref, ...), custom_call_target="tpu_custom_call" | custom-call | tf_op jit(solution)/shard_map/pallas_call | solution.py:338
  60.7 51.5 %all_to_all.10.in_ref = bf16[16,512,128]{2,1,0:T(8,128)(2,1)S(1)} all-to-all(bf16[16,512,128]{2,1,0:T(8,128)(2,1)S(1)} %shard_map.108), channel_id=1, replica_groups=mesh['groups'=2,'ctx'=16] {'ctx'}, dimensions={0} | all-to-all | bytes 4194304 | tf_op jit(solution)/shard_map/all_to_all | solution.py:349
  112.2 1.7 %shard_map.109 = (bf16[256,1024]{1,0:T(8,128)(2,1)}, bf16[256,1024]{1,0:T(8,128)(2,1)}, bf16[256,1024]{1,0:T(8,128)(2,1)}, bf16[256,1024]{1,0:T(8,128)(2,1)}) custom-call(bf16[16,512,128]{2,1,0:T(8,128)(2,1)S(1)} %all_to_all.10.in_ref), custom_call_target="tpu_custom_call" | custom-call | tf_op jit(solution)/shard_map/pallas_call | solution.py:350
  (27 shorter events, 3.8 us)
Async XLA Ops:
  0.6 9.2 %copy-start.1 = (bf16[256,1024]{1,0:T(8,128)(2,1)S(1)}, bf16[256,1024]{1,0:T(8,128)(2,1)}, u32[]{:S(2)}) copy-start(bf16[256,1024]{1,0:T(8,128)(2,1)} %c_ref.3) | copy-start | bytes 1572868
  0.6 9.2 %copy-start = (bf16[256,1024]{1,0:T(8,128)(2,1)S(1)}, bf16[256,1024]{1,0:T(8,128)(2,1)}, u32[]{:S(2)}) copy-start(bf16[256,1024]{1,0:T(8,128)(2,1)} %q_ref.3) | copy-start | bytes 1572868
  3.1 35.0 %copy-start.2 = (s32[64,6]{0,1:T(8,128)S(1)}, s32[64,6]{0,1:T(8,128)}, u32[]{:S(2)}) copy-start(s32[64,6]{0,1:T(8,128)} %param.12) | copy-start | bytes 4612
  3.1 35.0 %copy-start.3 = (s32[64,6]{0,1:T(8,128)S(1)}, s32[64,6]{0,1:T(8,128)}, u32[]{:S(2)}) copy-start(s32[64,6]{0,1:T(8,128)} %param.13) | copy-start | bytes 4612
  3.1 35.0 %copy-start.4 = (s32[2]{0:T(128)S(1)}, s32[2]{0:T(128)}, u32[]{:S(2)}) copy-start(s32[2]{0:T(128)} %glob_ref.7) | copy-start | bytes 28
  3.1 35.0 %all-to-all-start = ((bf16[16,256,128]{2,1,0:T(8,128)(2,1)}), bf16[16,256,128]{2,1,0:T(8,128)(2,1)S(1)}, u32[]{:S(2)}, u32[]{:S(2)}) async-start(bf16[16,256,128]{2,1,0:T(8,128)(2,1)} %shard_map.102), calls=%async_computation | async-start | bytes 2097152 | tf_op jit(solution)/shard_map/all_to_all | solution.py:288
  10.9 3.9 %collective-permute-start = (bf16[256,128]{1,0:T(8,128)(2,1)S(1)}, bf16[256,128]{1,0:T(8,128)(2,1)S(1)}, u32[]{:S(2)}, u32[]{:S(2)}) collective-permute-start(bf16[256,128]{1,0:T(8,128)(2,1)S(1)} %get-tuple-element.31), channel_id=1, source_target_pairs={{0,1},{1,0},{2,3},{3,2},{4,5},{5,4},{6,7},{7,6},{8,9},{9,8},{10,11... | collective-permute-start | bytes 196616 | tf_op jit(solution)/shard_map/ppermute | solution.py:291
  11.4 6.2 %collective-permute-start.1 = (bf16[256,128]{1,0:T(8,128)(2,1)S(1)}, bf16[256,128]{1,0:T(8,128)(2,1)S(1)}, u32[]{:S(2)}, u32[]{:S(2)}) collective-permute-start(bf16[256,128]{1,0:T(8,128)(2,1)S(1)} %get-tuple-element.32), channel_id=1, source_target_pairs={{0,2},{1,3},{2,0},{3,1},{4,6},{5,7},{6,4},{7,5},{8,10},{9,11},{10,... | collective-permute-start | bytes 196616 | tf_op jit(solution)/shard_map/ppermute | solution.py:291
  12.5 8.9 %collective-permute-start.2 = (bf16[256,128]{1,0:T(8,128)(2,1)S(1)}, bf16[256,128]{1,0:T(8,128)(2,1)S(1)}, u32[]{:S(2)}, u32[]{:S(2)}) collective-permute-start(bf16[256,128]{1,0:T(8,128)(2,1)S(1)} %get-tuple-element.33), channel_id=1, source_target_pairs={{0,3},{1,2},{2,1},{3,0},{4,7},{5,6},{6,5},{7,4},{8,11},{9,10},{10,... | collective-permute-start | bytes 196616 | tf_op jit(solution)/shard_map/ppermute | solution.py:291
  13.2 16.6 %collective-permute-start.3 = (bf16[256,128]{1,0:T(8,128)(2,1)S(1)}, bf16[256,128]{1,0:T(8,128)(2,1)S(1)}, u32[]{:S(2)}, u32[]{:S(2)}) collective-permute-start(bf16[256,128]{1,0:T(8,128)(2,1)S(1)} %get-tuple-element.34), channel_id=1, source_target_pairs={{0,4},{1,5},{2,6},{3,7},{4,0},{5,1},{6,2},{7,3},{8,12},{9,13},{10,... | collective-permute-start | bytes 196616 | tf_op jit(solution)/shard_map/ppermute | solution.py:291
  13.2 18.6 %collective-permute-start.4 = (bf16[256,128]{1,0:T(8,128)(2,1)S(1)}, bf16[256,128]{1,0:T(8,128)(2,1)S(1)}, u32[]{:S(2)}, u32[]{:S(2)}) collective-permute-start(bf16[256,128]{1,0:T(8,128)(2,1)S(1)} %get-tuple-element.35), channel_id=1, source_target_pairs={{0,5},{1,4},{2,7},{3,6},{4,1},{5,0},{6,3},{7,2},{8,13},{9,12},{10,... | collective-permute-start | bytes 196616 | tf_op jit(solution)/shard_map/ppermute | solution.py:291
  14.9 19.1 %collective-permute-start.5 = (bf16[256,128]{1,0:T(8,128)(2,1)S(1)}, bf16[256,128]{1,0:T(8,128)(2,1)S(1)}, u32[]{:S(2)}, u32[]{:S(2)}) collective-permute-start(bf16[256,128]{1,0:T(8,128)(2,1)S(1)} %get-tuple-element.36), channel_id=1, source_target_pairs={{0,6},{1,7},{2,4},{3,5},{4,2},{5,3},{6,0},{7,1},{8,14},{9,15},{10,... | collective-permute-start | bytes 196616 | tf_op jit(solution)/shard_map/ppermute | solution.py:291
  17.5 18.6 %collective-permute-start.6 = (bf16[256,128]{1,0:T(8,128)(2,1)S(1)}, bf16[256,128]{1,0:T(8,128)(2,1)S(1)}, u32[]{:S(2)}, u32[]{:S(2)}) collective-permute-start(bf16[256,128]{1,0:T(8,128)(2,1)S(1)} %get-tuple-element.37), channel_id=1, source_target_pairs={{0,7},{1,6},{2,5},{3,4},{4,3},{5,2},{6,1},{7,0},{8,15},{9,14},{10,... | collective-permute-start | bytes 196616 | tf_op jit(solution)/shard_map/ppermute | solution.py:291
  21.4 23.4 %collective-permute-start.7 = (bf16[256,128]{1,0:T(8,128)(2,1)S(1)}, bf16[256,128]{1,0:T(8,128)(2,1)S(1)}, u32[]{:S(2)}, u32[]{:S(2)}) collective-permute-start(bf16[256,128]{1,0:T(8,128)(2,1)S(1)} %get-tuple-element.39), channel_id=1, source_target_pairs={{0,8},{1,9},{2,10},{3,11},{4,12},{5,13},{6,14},{7,15},{8,0},{9,1},... | collective-permute-start | bytes 196616 | tf_op jit(solution)/shard_map/ppermute | solution.py:291
  29.7 15.3 %collective-permute-start.8 = (bf16[256,128]{1,0:T(8,128)(2,1)S(1)}, bf16[256,128]{1,0:T(8,128)(2,1)S(1)}, u32[]{:S(2)}, u32[]{:S(2)}) collective-permute-start(bf16[256,128]{1,0:T(8,128)(2,1)S(1)} %get-tuple-element.40), channel_id=1, source_target_pairs={{0,9},{1,8},{2,11},{3,10},{4,13},{5,12},{6,15},{7,14},{8,1},{9,0},... | collective-permute-start | bytes 196616 | tf_op jit(solution)/shard_map/ppermute | solution.py:291
  31.8 15.2 %collective-permute-start.9 = (bf16[256,128]{1,0:T(8,128)(2,1)S(1)}, bf16[256,128]{1,0:T(8,128)(2,1)S(1)}, u32[]{:S(2)}, u32[]{:S(2)}) collective-permute-start(bf16[256,128]{1,0:T(8,128)(2,1)S(1)} %get-tuple-element.41), channel_id=1, source_target_pairs={{0,10},{1,11},{2,8},{3,9},{4,14},{5,15},{6,12},{7,13},{8,2},{9,3},... | collective-permute-start | bytes 196616 | tf_op jit(solution)/shard_map/ppermute | solution.py:291
  34.0 14.0 %collective-permute-start.10 = (bf16[256,128]{1,0:T(8,128)(2,1)S(1)}, bf16[256,128]{1,0:T(8,128)(2,1)S(1)}, u32[]{:S(2)}, u32[]{:S(2)}) collective-permute-start(bf16[256,128]{1,0:T(8,128)(2,1)S(1)} %get-tuple-element.42), channel_id=1, source_target_pairs={{0,11},{1,10},{2,9},{3,8},{4,15},{5,14},{6,13},{7,12},{8,3},{9,2},... | collective-permute-start | bytes 196616 | tf_op jit(solution)/shard_map/ppermute | solution.py:291
  36.2 15.3 %collective-permute-start.11 = (bf16[256,128]{1,0:T(8,128)(2,1)S(1)}, bf16[256,128]{1,0:T(8,128)(2,1)S(1)}, u32[]{:S(2)}, u32[]{:S(2)}) collective-permute-start(bf16[256,128]{1,0:T(8,128)(2,1)S(1)} %get-tuple-element.44), channel_id=1, source_target_pairs={{0,12},{1,13},{2,14},{3,15},{4,8},{5,9},{6,10},{7,11},{8,4},{9,5},... | collective-permute-start | bytes 196616 | tf_op jit(solution)/shard_map/ppermute | solution.py:291
  44.8 8.0 %collective-permute-start.12 = (bf16[256,128]{1,0:T(8,128)(2,1)S(1)}, bf16[256,128]{1,0:T(8,128)(2,1)S(1)}, u32[]{:S(2)}, u32[]{:S(2)}) collective-permute-start(bf16[256,128]{1,0:T(8,128)(2,1)S(1)} %get-tuple-element.45), channel_id=1, source_target_pairs={{0,13},{1,12},{2,15},{3,14},{4,9},{5,8},{6,11},{7,10},{8,5},{9,4},... | collective-permute-start | bytes 196616 | tf_op jit(solution)/shard_map/ppermute | solution.py:291
  45.0 11.6 %collective-permute-start.13 = (bf16[256,128]{1,0:T(8,128)(2,1)S(1)}, bf16[256,128]{1,0:T(8,128)(2,1)S(1)}, u32[]{:S(2)}, u32[]{:S(2)}) collective-permute-start(bf16[256,128]{1,0:T(8,128)(2,1)S(1)} %get-tuple-element.47), channel_id=1, source_target_pairs={{0,14},{1,15},{2,12},{3,13},{4,10},{5,11},{6,8},{7,9},{8,6},{9,7},... | collective-permute-start | bytes 196616 | tf_op jit(solution)/shard_map/ppermute | solution.py:291
  47.0 11.2 %collective-permute-start.14 = (bf16[256,128]{1,0:T(8,128)(2,1)S(1)}, bf16[256,128]{1,0:T(8,128)(2,1)S(1)}, u32[]{:S(2)}, u32[]{:S(2)}) collective-permute-start(bf16[256,128]{1,0:T(8,128)(2,1)S(1)} %get-tuple-element.48), channel_id=1, source_target_pairs={{0,15},{1,14},{2,13},{3,12},{4,11},{5,10},{6,9},{7,8},{8,7},{9,6},... | collective-permute-start | bytes 196616 | tf_op jit(solution)/shard_map/ppermute | solution.py:291

commit v6 on v5

--- a/solution.py
+++ b/solution.py
@@ -19,7 +19,7 @@
 NEG_FILL = -1e30
 UNROLL = 8
 CHUNKS = 4
-PARTS = (4, 2, 2)
+PARTS = (8, 4, 2, 2)
 SCALE = HEAD_DIM ** -0.5
 EXP_SCALE = SCALE * math.log2(math.e)
 VMEM = pl.BlockSpec(memory_space=pltpu.VMEM)
@@ -119,18 +119,17 @@
         copy.wait()
 
 
-def attend(tables, kv_ref, acc_ref, blocks, group, items):
-    glob_ref, owner_ref, local_ref = tables
-    per_device = kv_ref.shape[0] // BLOCK // lax.axis_size("ctx")
+def attend(table_ref, kv_ref, acc_ref, repeat, items):
+    blocks = kv_ref.shape[0] // BLOCK
+    group = lax.axis_index("ctx") // (repeat * GROUP_HEADS)
+    globals_at = table_ref.shape[0] - GLOBALS
     low = lax.broadcasted_iota(jnp.int32, (BLOCK, PAIR), 1) < HEAD_DIM
     place = lax.broadcasted_iota(jnp.int32, (1, SPAN), 1)
 
     def load(i, qc):
         ids = [jnp.maximum(i - 1, 0), i, jnp.minimum(i + 1, blocks - 1)]
-        ids += [glob_ref[n] for n in range(GLOBALS)]
-        for n in range(ROUNDS):
-            entry = group * ROUNDS + n
-            ids.append(owner_ref[entry, i] * per_device + local_ref[entry, i])
+        ids += [table_ref[globals_at + n] for n in range(GLOBALS)]
+        ids += [table_ref[(group * ROUNDS + n) * blocks + i] for n in range(ROUNDS)]
         rows = [pl.ds(pl.multiple_of(one * BLOCK, BLOCK), BLOCK) for one in ids]
         kv = jnp.concatenate([kv_ref[r, :] for r in rows], axis=0)
         zero = jnp.zeros_like(qc)
@@ -182,45 +181,11 @@
             acc_ref[r, :] += term[n * BLOCK : (n + 1) * BLOCK]
 
 
-def my_group(repeat):
-    return lax.axis_index("ctx") // (repeat * GROUP_HEADS)
-
-
-def near_kernel(repeat, count, glob_ref, owner_ref, local_ref, kv_ref, *rest):
-    qc_refs, (acc_ref, out_ref, near_ref) = rest[:count], rest[count:]
-    tokens = qc_refs[0].shape[0]
-    mine = lax.rem(lax.axis_index("ctx"), count)
-    base = lax.axis_index("ctx") - mine
-    blocks = kv_ref.shape[0] // BLOCK
-    per_device = tokens // BLOCK
-    acc_ref[...] = jnp.zeros_like(acc_ref)
-    for m, ref in enumerate(qc_refs):
-        near_ref[mine ^ m] = ref[...]
-
-    def step(j):
-        items = []
-        for u in range(UNROLL):
-            place = j * UNROLL + u
-            device, local = lax.div(place, per_device), lax.rem(place, per_device)
-            rows = pl.ds(pl.multiple_of(local * BLOCK, BLOCK), BLOCK)
-
-            def put(value, device=device, rows=rows):
-                out_ref[device, rows, :] = value
-
-            items.append((base * per_device + place, near_ref[device, rows, :], put))
-        attend((glob_ref, owner_ref, local_ref), kv_ref, acc_ref, blocks, my_group(repeat), items)
-
-    pl.loop(0, count * per_device // UNROLL)(step)
-
-
-def far_step(repeat, count, first, tables, kv_ref, qc_refs, acc_ref, out_refs):
-    me = lax.axis_index("ctx")
-    mine = lax.rem(me, count)
-    base = me - mine
+def attend_tiles(repeat, first, table_ref, kv_ref, acc_ref, qc_refs, out_refs):
+    per_device = qc_refs[0].shape[0] // BLOCK
     items = []
     for m, (qc_ref, out_ref) in enumerate(zip(qc_refs, out_refs)):
-        source = (count - base) + (mine ^ (first + m))
-        per_device = qc_ref.shape[0] // BLOCK
+        source = lax.axis_index("ctx") ^ (first + m)
         for local in range(per_device):
             rows = pl.ds(local * BLOCK, BLOCK)
 
@@ -230,36 +195,31 @@
             items.append((source * per_device + local, qc_ref, rows, put))
     for start in range(0, len(items), UNROLL):
         now = [(i, ref[rows, :], put) for i, ref, rows, put in items[start : start + UNROLL]]
-        attend(tables, kv_ref, acc_ref, kv_ref.shape[0] // BLOCK, my_group(repeat), now)
-
-
-def far_kernel(repeat, count, first, size, glob_ref, owner_ref, local_ref, kv_ref, acc_in_ref, *rest):
+        attend(table_ref, kv_ref, acc_ref, repeat, now)
+
+
+def part_kernel(repeat, first, size, table_ref, kv_ref, *rest):
+    acc_in_refs, rest = rest[: first > 0], rest[first > 0 :]
     qc_refs, acc_ref, out_refs = rest[:size], rest[size], rest[size + 1 :]
-    acc_ref[...] = acc_in_ref[...]
-    far_step(repeat, count, first, (glob_ref, owner_ref, local_ref), kv_ref, qc_refs, acc_ref, out_refs)
-
-
-def last_kernel(repeat, count, first, size, glob_ref, owner_ref, local_ref, kv_ref, acc_in_ref, *rest):
-    qc_refs, near_ref, done_refs = rest[:size], rest[size], rest[size + 1 : -3]
-    out_ref, acc_ref, late_ref = rest[-3:]
+    acc_ref[...] = acc_in_refs[0][...] if first else jnp.zeros_like(acc_ref)
+    attend_tiles(repeat, first, table_ref, kv_ref, acc_ref, qc_refs, out_refs)
+
+
+def last_kernel(repeat, first, size, table_ref, kv_ref, acc_in_ref, *rest):
+    qc_refs, done_refs, (out_ref, acc_ref, late_ref) = rest[:size], rest[size:-3], rest[-3:]
     tokens = qc_refs[0].shape[0]
-    me = lax.axis_index("ctx")
-    mine = lax.rem(me, count)
-    base = me - mine
     acc_ref[...] = acc_in_ref[...]
     late = [late_ref.at[m] for m in range(size)]
-    far_step(repeat, count, first, (glob_ref, owner_ref, local_ref), kv_ref, qc_refs, acc_ref, late)
-    for j in range(count):
-        out_ref[base + j, :tokens, :] = near_ref[j]
+    attend_tiles(repeat, first, table_ref, kv_ref, acc_ref, qc_refs, late)
     for m, ref in enumerate(list(done_refs) + late):
-        out_ref[(count - base) + (mine ^ m), :tokens, :] = ref[...]
+        out_ref[lax.axis_index("ctx") ^ m, :tokens, :] = ref[...]
 
     def finish(d):
         acc = acc_ref[pl.ds(pl.multiple_of(d * tokens, tokens), tokens), :]
         left = lax.broadcasted_iota(jnp.int32, acc.shape, 1) < HEAD_DIM
         out_ref[d, tokens:, :] = jnp.where(left, acc * SCALE, acc).astype(jnp.bfloat16)
 
-    pl.loop(0, 2 * count)(finish)
+    pl.loop(0, out_ref.shape[0])(finish)
 
 
 def per_device(query, key, value, cotangent, global_ids, rand_owner, rand_local):
@@ -310,42 +270,36 @@
     far_qc = pack_queries(1, [])
     far_qc = [swap(one, count + m) for m, one in enumerate(far_qc)]
 
-    tables = (global_ids, rand_owner.T, rand_local.T)
+    picked = (rand_owner * (tokens // BLOCK) + rand_local).T.reshape(-1)
+    table = jnp.concatenate((picked, global_ids))
     total = jax.ShapeDtypeStruct((devices * tokens, PAIR), jnp.float32)
-    acc, near_out = pl.pallas_call(
-        functools.partial(near_kernel, repeat, count),
-        out_shape=[total, jax.ShapeDtypeStruct((count, tokens, PAIR), jnp.bfloat16)],
-        in_specs=[SMEM] * 3 + [VMEM] * (1 + count),
-        out_specs=[VMEM] * 2,
-        scratch_shapes=[pltpu.VMEM((count, tokens, PAIR), jnp.bfloat16)],
-        compiler_params=params,
-        cost_estimate=pl.CostEstimate(flops=7 * 10**9, bytes_accessed=4 << 20, transcendentals=0),
-    )(*tables, keys, *near_qc)
-    done = []
-    *sizes, size = [count * part // sum(PARTS) for part in PARTS]
-    first = 0
-    for some in sizes:
-        acc, *outs = pl.pallas_call(
-            functools.partial(far_kernel, repeat, count, first, some),
-            out_shape=[total] + [tile] * some,
-            in_specs=[SMEM] * 3 + [VMEM] * (2 + some),
-            out_specs=[VMEM] * (1 + some),
+    *sizes, last = [devices * part // sum(PARTS) for part in PARTS]
+    qc = near_qc + far_qc
+    acc, done = [], []
+    for size in sizes:
+        first = len(done)
+        outs = pl.pallas_call(
+            functools.partial(part_kernel, repeat, first, size),
+            out_shape=[total] + [tile] * size,
+            in_specs=[SMEM] + [VMEM] * (1 + len(acc) + size),
+            out_specs=[VMEM] * (1 + size),
             compiler_params=params,
-            cost_estimate=pl.CostEstimate(flops=some * 10**9, bytes_accessed=4 << 20, transcendentals=0),
-        )(*tables, keys, acc, *far_qc[first : first + some])
-        done += outs
-        first += some
+            cost_estimate=pl.CostEstimate(flops=size * 10**9, bytes_accessed=4 << 20, transcendentals=0),
+        )(table, keys, *acc, *qc[first : first + size])
+        acc = [outs[0]]
+        done += outs[1:]
+    first = len(done)
     grads = pl.pallas_call(
-        functools.partial(last_kernel, repeat, count, first, size),
+        functools.partial(last_kernel, repeat, first, last),
         out_shape=jax.ShapeDtypeStruct((devices, 2 * tokens, PAIR), jnp.bfloat16),
-        in_specs=[SMEM] * 3 + [VMEM] * (3 + count),
+        in_specs=[SMEM] + [VMEM] * (2 + devices),
         out_specs=VMEM,
         scratch_shapes=[
             pltpu.VMEM((devices * tokens, PAIR), jnp.float32),
-            pltpu.VMEM((size, tokens, PAIR), jnp.bfloat16),
+            pltpu.VMEM((last, tokens, PAIR), jnp.bfloat16),
         ],
         compiler_params=params,
-    )(*tables, keys, acc, *far_qc[first:], near_out, *done)
+    )(table, keys, *acc, *qc[first:], *done)
     back = lax.all_to_all(grads, "ctx", 0, 0, tiled=True)
     return pl.pallas_call(
         functools.partial(unpack_kernel, repeat),

time: 115 us -> 114 us (level)
  Pallas kernels: 21 us -> 19.2 us
  starting transfers between devices: 29.9 us -> 31.5 us
    pallas_call x4, Pallas kernels: 14.9 us -> 13.1 us  [the longest x3 10.7 us: per_device(): pl.pallas_call(functools.partial(part_kernel, repeat, first, size), out_s...]
    ppermute x15, starting transfers between devices: 23.1 us -> 24.7 us  [swap(): return lax.ppermute(array, 'ctx', [(i, i ^ mask) for i in range(devices)])]
  transfers between devices with their start and end apart: 16 -> 16, of which waited for: 6 -> 5; matrix products, arithmetic and copies ran while one was open for 0% -> 0% of each run, Pallas kernels for 13% -> 11%
where the time goes in v6:
time: 114 us; the launch traced here: 113 us
  blocking collectives  50.8 us (45%)
  starting transfers between devices  31.5 us (28%)
  Pallas kernels  19.2 us (17%)
  waiting for transfers between devices  10.6 us (9%)
    all_to_all x1, blocking collectives, per_device(): back = lax.all_to_all(grads, 'ctx', 0, 0, tiled=True)  50.8 us
    ppermute x15, starting transfers between devices, swap(): return lax.ppermute(array, 'ctx', [(i, i ^ mask) for i in range(devices)])  24.7 us
    pallas_call x3, Pallas kernels, per_device(): pl.pallas_call(functools.partial(part_kernel, repeat, first, size), out_s...  10.7 us
    ppermute x15, waiting for transfers between devices, swap(): return lax.ppermute(array, 'ctx', [(i, i ^ mask) for i in range(devices)])  10.6 us
    all_to_all x1, starting transfers between devices, per_device(): lax.all_to_all(packed, 'ctx', 0, 0, tiled=True)  6.75 us
    pallas_call x1, Pallas kernels, per_device(): pl.pallas_call(functools.partial(pack_keys_kernel, repeat), out_shape=jax...  2.42 us
    pallas_call x1, Pallas kernels, per_device(): pl.pallas_call(functools.partial(last_kernel, repeat, first, last), out_s...  2.39 us
  transfers between devices with their start and end apart: 16, of which 5 were waited for; matrix products, arithmetic and copies ran while one was open for 0% of the time, Pallas kernels for 11%

profile of v6, /device:TPU:9, one launch (start us, length us, event | category | flops | bytes accessed | tf_op | source)
XLA Modules:
  0.0 113.0 jit_solution(14942646211566824523)
XLA Ops:
  0.7 2.4 %shard_map.102 = bf16[16,256,128]{2,1,0:T(8,128)(2,1)} custom-call(bf16[256,1024]{1,0:T(8,128)(2,1)} %k_ref.1, bf16[256,1024]{1,0:T(8,128)(2,1)} %v_ref.1), custom_call_target="tpu_custom_call" | custom-call | tf_op jit(solution)/shard_map/pallas_call | solution.py:235
  3.1 6.8 %all-to-all-start = ((bf16[16,256,128]{2,1,0:T(8,128)(2,1)}), bf16[16,256,128]{2,1,0:T(8,128)(2,1)S(1)}, u32[]{:S(2)}, u32[]{:S(2)}) async-start(bf16[16,256,128]{2,1,0:T(8,128)(2,1)} %shard_map.102), calls=%async_computation | async-start | bytes 2097152 | tf_op jit(solution)/shard_map/all_to_all | solution.py:248
  9.9 1.0 shard_map.103
  11.4 1.2 %collective-permute-start.1 = (bf16[256,128]{1,0:T(8,128)(2,1)S(1)}, bf16[256,128]{1,0:T(8,128)(2,1)S(1)}, u32[]{:S(2)}, u32[]{:S(2)}) collective-permute-start(bf16[256,128]{1,0:T(8,128)(2,1)S(1)} %get-tuple-element.39), channel_id=1, source_target_pairs={{0,2},{1,3},{2,0},{3,1},{4,6},{5,7},{6,4},{7,5},{8,10},{9,11},{10,... | collective-permute-start | bytes 196616 | tf_op jit(solution)/shard_map/ppermute | solution.py:251
  13.2 1.6 %collective-permute-start.4 = (bf16[256,128]{1,0:T(8,128)(2,1)S(1)}, bf16[256,128]{1,0:T(8,128)(2,1)S(1)}, u32[]{:S(2)}, u32[]{:S(2)}) collective-permute-start(bf16[256,128]{1,0:T(8,128)(2,1)S(1)} %get-tuple-element.42), channel_id=1, source_target_pairs={{0,5},{1,4},{2,7},{3,6},{4,1},{5,0},{6,3},{7,2},{8,13},{9,12},{10,... | collective-permute-start | bytes 196616 | tf_op jit(solution)/shard_map/ppermute | solution.py:251
  14.9 1.0 shard_map.105
  16.0 1.2 %collective-permute-start.5 = (bf16[256,128]{1,0:T(8,128)(2,1)S(1)}, bf16[256,128]{1,0:T(8,128)(2,1)S(1)}, u32[]{:S(2)}, u32[]{:S(2)}) collective-permute-start(bf16[256,128]{1,0:T(8,128)(2,1)S(1)} %get-tuple-element.43), channel_id=1, source_target_pairs={{0,6},{1,7},{2,4},{3,5},{4,2},{5,3},{6,0},{7,1},{8,14},{9,15},{10,... | collective-permute-start | bytes 196616 | tf_op jit(solution)/shard_map/ppermute | solution.py:251
  17.5 2.9 %collective-permute-start.6 = (bf16[256,128]{1,0:T(8,128)(2,1)S(1)}, bf16[256,128]{1,0:T(8,128)(2,1)S(1)}, u32[]{:S(2)}, u32[]{:S(2)}) collective-permute-start(bf16[256,128]{1,0:T(8,128)(2,1)S(1)} %get-tuple-element.44), channel_id=1, source_target_pairs={{0,7},{1,6},{2,5},{3,4},{4,3},{5,2},{6,1},{7,0},{8,15},{9,14},{10,... | collective-permute-start | bytes 196616 | tf_op jit(solution)/shard_map/ppermute | solution.py:251
  20.4 5.1 %collective-permute-start.7 = (bf16[256,128]{1,0:T(8,128)(2,1)S(1)}, bf16[256,128]{1,0:T(8,128)(2,1)S(1)}, u32[]{:S(2)}, u32[]{:S(2)}) collective-permute-start(bf16[256,128]{1,0:T(8,128)(2,1)S(1)} %get-tuple-element.46), channel_id=1, source_target_pairs={{0,8},{1,9},{2,10},{3,11},{4,12},{5,13},{6,14},{7,15},{8,0},{9,1},... | collective-permute-start | bytes 196616 | tf_op jit(solution)/shard_map/ppermute | solution.py:251
  25.5 4.2 %collective-permute-done.3.rest_4_ = bf16[256,128]{1,0:T(8,128)(2,1)S(1)} collective-permute-done((bf16[256,128]{1,0:T(8,128)(2,1)S(1)}, bf16[256,128]{1,0:T(8,128)(2,1)S(1)}, u32[]{:S(2)}, u32[]{:S(2)}) %collective-permute-start.3) | collective-permute-done | bytes 65568 | tf_op jit(solution)/shard_map/ppermute | solution.py:251
  29.7 2.1 %collective-permute-start.8 = (bf16[256,128]{1,0:T(8,128)(2,1)S(1)}, bf16[256,128]{1,0:T(8,128)(2,1)S(1)}, u32[]{:S(2)}, u32[]{:S(2)}) collective-permute-start(bf16[256,128]{1,0:T(8,128)(2,1)S(1)} %get-tuple-element.47), channel_id=1, source_target_pairs={{0,9},{1,8},{2,11},{3,10},{4,13},{5,12},{6,15},{7,14},{8,1},{9,0},... | collective-permute-start | bytes 196616 | tf_op jit(solution)/shard_map/ppermute | solution.py:251
  31.8 2.1 %collective-permute-start.9 = (bf16[256,128]{1,0:T(8,128)(2,1)S(1)}, bf16[256,128]{1,0:T(8,128)(2,1)S(1)}, u32[]{:S(2)}, u32[]{:S(2)}) collective-permute-start(bf16[256,128]{1,0:T(8,128)(2,1)S(1)} %get-tuple-element.48), channel_id=1, source_target_pairs={{0,10},{1,11},{2,8},{3,9},{4,14},{5,15},{6,12},{7,13},{8,2},{9,3},... | collective-permute-start | bytes 196616 | tf_op jit(solution)/shard_map/ppermute | solution.py:251
  34.0 1.7 %collective-permute-start.10 = (bf16[256,128]{1,0:T(8,128)(2,1)S(1)}, bf16[256,128]{1,0:T(8,128)(2,1)S(1)}, u32[]{:S(2)}, u32[]{:S(2)}) collective-permute-start(bf16[256,128]{1,0:T(8,128)(2,1)S(1)} %get-tuple-element.49), channel_id=1, source_target_pairs={{0,11},{1,10},{2,9},{3,8},{4,15},{5,14},{6,13},{7,12},{8,3},{9,2},... | collective-permute-start | bytes 196616 | tf_op jit(solution)/shard_map/ppermute | solution.py:251
  36.2 1.9 %collective-permute-start.11 = (bf16[256,128]{1,0:T(8,128)(2,1)S(1)}, bf16[256,128]{1,0:T(8,128)(2,1)S(1)}, u32[]{:S(2)}, u32[]{:S(2)}) collective-permute-start(bf16[256,128]{1,0:T(8,128)(2,1)S(1)} %get-tuple-element.51), channel_id=1, source_target_pairs={{0,12},{1,13},{2,14},{3,15},{4,8},{5,9},{6,10},{7,11},{8,4},{9,5},... | collective-permute-start | bytes 196616 | tf_op jit(solution)/shard_map/ppermute | solution.py:251
  38.1 5.4 %shard_map.104 = (f32[4096,128]{1,0:T(8,128)S(1)}, bf16[256,128]{1,0:T(8,128)(2,1)S(1)}, bf16[256,128]{1,0:T(8,128)(2,1)S(1)}, bf16[256,128]{1,0:T(8,128)(2,1)S(...) custom-call(s32[386]{0:T(512)S(1)} %constant_dynamic-update-slice_fu, ...), custom_call_target="tpu_custom_call" | custom-call | flops 8000000000 | bytes 4194304 | tf_op jit(solution)/shard_map/pallas_call | solution.py:281
  43.7 2.0 %collective-permute-start.13 = (bf16[256,128]{1,0:T(8,128)(2,1)S(1)}, bf16[256,128]{1,0:T(8,128)(2,1)S(1)}, u32[]{:S(2)}, u32[]{:S(2)}) collective-permute-start(bf16[256,128]{1,0:T(8,128)(2,1)S(1)} %get-tuple-element.54), channel_id=1, source_target_pairs={{0,14},{1,15},{2,12},{3,13},{4,10},{5,11},{6,8},{7,9},{8,6},{9,7},... | collective-permute-start | bytes 196616 | tf_op jit(solution)/shard_map/ppermute | solution.py:251
  45.7 1.5 %collective-permute-start.14 = (bf16[256,128]{1,0:T(8,128)(2,1)S(1)}, bf16[256,128]{1,0:T(8,128)(2,1)S(1)}, u32[]{:S(2)}, u32[]{:S(2)}) collective-permute-start(bf16[256,128]{1,0:T(8,128)(2,1)S(1)} %get-tuple-element.55), channel_id=1, source_target_pairs={{0,15},{1,14},{2,13},{3,12},{4,11},{5,10},{6,9},{7,8},{8,7},{9,6},... | collective-permute-start | bytes 196616 | tf_op jit(solution)/shard_map/ppermute | solution.py:251
  47.2 3.2 %shard_map.106 = (f32[4096,128]{1,0:T(8,128)S(1)}, bf16[256,128]{1,0:T(8,128)(2,1)S(1)}, bf16[256,128]{1,0:T(8,128)(2,1)S(1)}, bf16[256,128]{1,0:T(8,128)(2,1)S(1)}, bf16[256,128]{1,0:T(8,128)(2,1)S(1)}) custom-call(s32[386]{0:T(512)S(1)} %constant_dynamic-update-slice_fusion.table_ref, bf16[4096,128]{1,0:T(8,128)(2,1)S(1)} %bitcast.4, ...), custom_call_target="tpu_custom_call" | custom-call | flops 4000000000 | bytes 4194304 | tf_op jit(solution)/shard_map/pallas_call | solution.py:281
  50.4 4.5 %collective-permute-done.12.rest_2_ = bf16[256,128]{1,0:T(8,128)(2,1)S(1)} collective-permute-done((bf16[256,128]{1,0:T(8,128)(2,1)S(1)}, bf16[256,128]{1,0:T(8,128)(2,1)S(1)}, u32[]{:S(2)}, u32[]{:S(2)}) %collective-permute-start.12) | collective-permute-done | bytes 65568 | tf_op jit(solution)/shard_map/ppermute | solution.py:251
  54.9 2.0 %shard_map.107 = (f32[4096,128]{1,0:T(8,128)S(1)}, bf16[256,128]{1,0:T(8,128)(2,1)S(1)}, bf16[256,128]{1,0:T(8,128)(2,1)S(1)}) custom-call(s32[386]{0:T(512)S(1)} %constant_dynamic-update-slice_fusion.table_ref, bf16[4096,128]{1,0:T(8,128)(2,1)S(1)} %bitcast.5, f32[4096,128]{1,0:T(8,128)S(1)} %get-tuple-element.50.rest_0_, ...), custom_call_target="tpu_custom_call" | custom-call | flops 2000000000 | bytes 4194304 | tf_op jit(solution)/shard_map/pallas_call | solution.py:281
  57.0 1.2 %collective-permute-done.14.rest_1_ = bf16[256,128]{1,0:T(8,128)(2,1)S(1)} collective-permute-done((bf16[256,128]{1,0:T(8,128)(2,1)S(1)}, bf16[256,128]{1,0:T(8,128)(2,1)S(1)}, u32[]{:S(2)}, u32[]{:S(2)}) %collective-permute-start.14) | collective-permute-done | bytes 65568 | tf_op jit(solution)/shard_map/ppermute | solution.py:251
  58.2 2.4 %shard_map.108 = bf16[16,512,128]{2,1,0:T(8,128)(2,1)S(1)} custom-call(s32[386]{0:T(512)S(1)} %constant_dynamic-update-slice_fusion.table_ref, bf16[4096,128]{1,0:T(8,128)(2,1)S(1)} %bitcast.6, f32[4096,128]{1,0:T(8,128)S(1)} %get-tuple-element.53.acc_in_ref, bf16[256,128]{1,0:T(8,128)(2,1)S(1)} %collective-permute-done.13.rest_0_, ...), custom_call_target="tpu_custom_call" | custom-call | tf_op jit(solution)/shard_map/pallas_call | solution.py:292
  60.6 50.8 %all_to_all.10.in_ref = bf16[16,512,128]{2,1,0:T(8,128)(2,1)S(1)} all-to-all(bf16[16,512,128]{2,1,0:T(8,128)(2,1)S(1)} %shard_map.108), channel_id=1, replica_groups=mesh['groups'=2,'ctx'=16] {'ctx'}, dimensions={0} | all-to-all | bytes 4194304 | tf_op jit(solution)/shard_map/all_to_all | solution.py:303
  111.4 1.7 %shard_map.109 = (bf16[256,1024]{1,0:T(8,128)(2,1)}, bf16[256,1024]{1,0:T(8,128)(2,1)}, bf16[256,1024]{1,0:T(8,128)(2,1)}, bf16[256,1024]{1,0:T(8,128)(2,1)}) custom-call(bf16[16,512,128]{2,1,0:T(8,128)(2,1)S(1)} %all_to_all.10.in_ref), custom_call_target="tpu_custom_call" | custom-call | tf_op jit(solution)/shard_map/pallas_call | solution.py:304
  (32 shorter events, 2.2 us)
Async XLA Ops:
  0.6 9.2 %copy-start.1 = (bf16[256,1024]{1,0:T(8,128)(2,1)S(1)}, bf16[256,1024]{1,0:T(8,128)(2,1)}, u32[]{:S(2)}) copy-start(bf16[256,1024]{1,0:T(8,128)(2,1)} %c_ref.3) | copy-start | bytes 1572868
  0.6 9.2 %copy-start = (bf16[256,1024]{1,0:T(8,128)(2,1)S(1)}, bf16[256,1024]{1,0:T(8,128)(2,1)}, u32[]{:S(2)}) copy-start(bf16[256,1024]{1,0:T(8,128)(2,1)} %q_ref.3) | copy-start | bytes 1572868
  3.1 12.8 %copy-start.2 = (s32[64,6]{0,1:T(8,128)S(1)}, s32[64,6]{0,1:T(8,128)}, u32[]{:S(2)}) copy-start(s32[64,6]{0,1:T(8,128)} %param.13) | copy-start | bytes 4612
  3.1 12.8 %copy-start.3 = (s32[64,6]{0,1:T(8,128)S(1)}, s32[64,6]{0,1:T(8,128)}, u32[]{:S(2)}) copy-start(s32[64,6]{0,1:T(8,128)} %param.12) | copy-start | bytes 4612
  3.1 17.3 %copy-start.4 = (s32[2]{0:T(128)S(1)}, s32[2]{0:T(128)}, u32[]{:S(2)}) copy-start(s32[2]{0:T(128)} %param.11) | copy-start | bytes 28
  3.1 35.0 %all-to-all-start = ((bf16[16,256,128]{2,1,0:T(8,128)(2,1)}), bf16[16,256,128]{2,1,0:T(8,128)(2,1)S(1)}, u32[]{:S(2)}, u32[]{:S(2)}) async-start(bf16[16,256,128]{2,1,0:T(8,128)(2,1)} %shard_map.102), calls=%async_computation | async-start | bytes 2097152 | tf_op jit(solution)/shard_map/all_to_all | solution.py:248
  10.9 5.1 %collective-permute-start = (bf16[256,128]{1,0:T(8,128)(2,1)S(1)}, bf16[256,128]{1,0:T(8,128)(2,1)S(1)}, u32[]{:S(2)}, u32[]{:S(2)}) collective-permute-start(bf16[256,128]{1,0:T(8,128)(2,1)S(1)} %get-tuple-element.38), channel_id=1, source_target_pairs={{0,1},{1,0},{2,3},{3,2},{4,5},{5,4},{6,7},{7,6},{8,9},{9,8},{10,11... | collective-permute-start | bytes 196616 | tf_op jit(solution)/shard_map/ppermute | solution.py:251
  11.4 6.2 %collective-permute-start.1 = (bf16[256,128]{1,0:T(8,128)(2,1)S(1)}, bf16[256,128]{1,0:T(8,128)(2,1)S(1)}, u32[]{:S(2)}, u32[]{:S(2)}) collective-permute-start(bf16[256,128]{1,0:T(8,128)(2,1)S(1)} %get-tuple-element.39), channel_id=1, source_target_pairs={{0,2},{1,3},{2,0},{3,1},{4,6},{5,7},{6,4},{7,5},{8,10},{9,11},{10,... | collective-permute-start | bytes 196616 | tf_op jit(solution)/shard_map/ppermute | solution.py:251
  12.5 7.9 %collective-permute-start.2 = (bf16[256,128]{1,0:T(8,128)(2,1)S(1)}, bf16[256,128]{1,0:T(8,128)(2,1)S(1)}, u32[]{:S(2)}, u32[]{:S(2)}) collective-permute-start(bf16[256,128]{1,0:T(8,128)(2,1)S(1)} %get-tuple-element.40), channel_id=1, source_target_pairs={{0,3},{1,2},{2,1},{3,0},{4,7},{5,6},{6,5},{7,4},{8,11},{9,10},{10,... | collective-permute-start | bytes 196616 | tf_op jit(solution)/shard_map/ppermute | solution.py:251
  13.2 16.6 %collective-permute-start.3 = (bf16[256,128]{1,0:T(8,128)(2,1)S(1)}, bf16[256,128]{1,0:T(8,128)(2,1)S(1)}, u32[]{:S(2)}, u32[]{:S(2)}) collective-permute-start(bf16[256,128]{1,0:T(8,128)(2,1)S(1)} %get-tuple-element.41), channel_id=1, source_target_pairs={{0,4},{1,5},{2,6},{3,7},{4,0},{5,1},{6,2},{7,3},{8,12},{9,13},{10,... | collective-permute-start | bytes 196616 | tf_op jit(solution)/shard_map/ppermute | solution.py:251
  13.2 18.6 %collective-permute-start.4 = (bf16[256,128]{1,0:T(8,128)(2,1)S(1)}, bf16[256,128]{1,0:T(8,128)(2,1)S(1)}, u32[]{:S(2)}, u32[]{:S(2)}) collective-permute-start(bf16[256,128]{1,0:T(8,128)(2,1)S(1)} %get-tuple-element.42), channel_id=1, source_target_pairs={{0,5},{1,4},{2,7},{3,6},{4,1},{5,0},{6,3},{7,2},{8,13},{9,12},{10,... | collective-permute-start | bytes 196616 | tf_op jit(solution)/shard_map/ppermute | solution.py:251
  16.0 18.0 %collective-permute-start.5 = (bf16[256,128]{1,0:T(8,128)(2,1)S(1)}, bf16[256,128]{1,0:T(8,128)(2,1)S(1)}, u32[]{:S(2)}, u32[]{:S(2)}) collective-permute-start(bf16[256,128]{1,0:T(8,128)(2,1)S(1)} %get-tuple-element.43), channel_id=1, source_target_pairs={{0,6},{1,7},{2,4},{3,5},{4,2},{5,3},{6,0},{7,1},{8,14},{9,15},{10,... | collective-permute-start | bytes 196616 | tf_op jit(solution)/shard_map/ppermute | solution.py:251
  17.5 18.6 %collective-permute-start.6 = (bf16[256,128]{1,0:T(8,128)(2,1)S(1)}, bf16[256,128]{1,0:T(8,128)(2,1)S(1)}, u32[]{:S(2)}, u32[]{:S(2)}) collective-permute-start(bf16[256,128]{1,0:T(8,128)(2,1)S(1)} %get-tuple-element.44), channel_id=1, source_target_pairs={{0,7},{1,6},{2,5},{3,4},{4,3},{5,2},{6,1},{7,0},{8,15},{9,14},{10,... | collective-permute-start | bytes 196616 | tf_op jit(solution)/shard_map/ppermute | solution.py:251
  20.4 23.1 %collective-permute-start.7 = (bf16[256,128]{1,0:T(8,128)(2,1)S(1)}, bf16[256,128]{1,0:T(8,128)(2,1)S(1)}, u32[]{:S(2)}, u32[]{:S(2)}) collective-permute-start(bf16[256,128]{1,0:T(8,128)(2,1)S(1)} %get-tuple-element.46), channel_id=1, source_target_pairs={{0,8},{1,9},{2,10},{3,11},{4,12},{5,13},{6,14},{7,15},{8,0},{9,1},... | collective-permute-start | bytes 196616 | tf_op jit(solution)/shard_map/ppermute | solution.py:251
  29.7 14.0 %collective-permute-start.8 = (bf16[256,128]{1,0:T(8,128)(2,1)S(1)}, bf16[256,128]{1,0:T(8,128)(2,1)S(1)}, u32[]{:S(2)}, u32[]{:S(2)}) collective-permute-start(bf16[256,128]{1,0:T(8,128)(2,1)S(1)} %get-tuple-element.47), channel_id=1, source_target_pairs={{0,9},{1,8},{2,11},{3,10},{4,13},{5,12},{6,15},{7,14},{8,1},{9,0},... | collective-permute-start | bytes 196616 | tf_op jit(solution)/shard_map/ppermute | solution.py:251
  31.8 13.9 %collective-permute-start.9 = (bf16[256,128]{1,0:T(8,128)(2,1)S(1)}, bf16[256,128]{1,0:T(8,128)(2,1)S(1)}, u32[]{:S(2)}, u32[]{:S(2)}) collective-permute-start(bf16[256,128]{1,0:T(8,128)(2,1)S(1)} %get-tuple-element.48), channel_id=1, source_target_pairs={{0,10},{1,11},{2,8},{3,9},{4,14},{5,15},{6,12},{7,13},{8,2},{9,3},... | collective-permute-start | bytes 196616 | tf_op jit(solution)/shard_map/ppermute | solution.py:251
  34.0 13.3 %collective-permute-start.10 = (bf16[256,128]{1,0:T(8,128)(2,1)S(1)}, bf16[256,128]{1,0:T(8,128)(2,1)S(1)}, u32[]{:S(2)}, u32[]{:S(2)}) collective-permute-start(bf16[256,128]{1,0:T(8,128)(2,1)S(1)} %get-tuple-element.49), channel_id=1, source_target_pairs={{0,11},{1,10},{2,9},{3,8},{4,15},{5,14},{6,13},{7,12},{8,3},{9,2},... | collective-permute-start | bytes 196616 | tf_op jit(solution)/shard_map/ppermute | solution.py:251
  36.2 14.3 %collective-permute-start.11 = (bf16[256,128]{1,0:T(8,128)(2,1)S(1)}, bf16[256,128]{1,0:T(8,128)(2,1)S(1)}, u32[]{:S(2)}, u32[]{:S(2)}) collective-permute-start(bf16[256,128]{1,0:T(8,128)(2,1)S(1)} %get-tuple-element.51), channel_id=1, source_target_pairs={{0,12},{1,13},{2,14},{3,15},{4,8},{5,9},{6,10},{7,11},{8,4},{9,5},... | collective-permute-start | bytes 196616 | tf_op jit(solution)/shard_map/ppermute | solution.py:251
  43.6 11.3 %collective-permute-start.12 = (bf16[256,128]{1,0:T(8,128)(2,1)S(1)}, bf16[256,128]{1,0:T(8,128)(2,1)S(1)}, u32[]{:S(2)}, u32[]{:S(2)}) collective-permute-start(bf16[256,128]{1,0:T(8,128)(2,1)S(1)} %get-tuple-element.52), channel_id=1, source_target_pairs={{0,13},{1,12},{2,15},{3,14},{4,9},{5,8},{6,11},{7,10},{8,5},{9,4},... | collective-permute-start | bytes 196616 | tf_op jit(solution)/shard_map/ppermute | solution.py:251
  43.7 13.2 %collective-permute-start.13 = (bf16[256,128]{1,0:T(8,128)(2,1)S(1)}, bf16[256,128]{1,0:T(8,128)(2,1)S(1)}, u32[]{:S(2)}, u32[]{:S(2)}) collective-permute-start(bf16[256,128]{1,0:T(8,128)(2,1)S(1)} %get-tuple-element.54), channel_id=1, source_target_pairs={{0,14},{1,15},{2,12},{3,13},{4,10},{5,11},{6,8},{7,9},{8,6},{9,7},... | collective-permute-start | bytes 196616 | tf_op jit(solution)/shard_map/ppermute | solution.py:251
  45.7 12.4 %collective-permute-start.14 = (bf16[256,128]{1,0:T(8,128)(2,1)S(1)}, bf16[256,128]{1,0:T(8,128)(2,1)S(1)}, u32[]{:S(2)}, u32[]{:S(2)}) collective-permute-start(bf16[256,128]{1,0:T(8,128)(2,1)S(1)} %get-tuple-element.55), channel_id=1, source_target_pairs={{0,15},{1,14},{2,13},{3,12},{4,11},{5,10},{6,9},{7,8},{8,7},{9,6},... | collective-permute-start | bytes 196616 | tf_op jit(solution)/shard_map/ppermute | solution.py:251

commit v7 on v6

--- a/solution.py
+++ b/solution.py
@@ -19,6 +19,7 @@
 NEG_FILL = -1e30
 UNROLL = 8
 CHUNKS = 4
+EARLY = 4
 PARTS = (8, 4, 2, 2)
 SCALE = HEAD_DIM ** -0.5
 EXP_SCALE = SCALE * math.log2(math.e)
@@ -94,27 +95,37 @@
         copy.wait()
 
 
-def unpack_kernel(repeat, in_ref, att_ref, dq_ref, dk_ref, dv_ref, buf_ref, sems):
+def hold_kernel(count, *refs):
+    for source, ref in zip(refs[:count], refs[-count:]):
+        ref[...] = source[...]
+
+
+def unpack_kernel(repeat, keys_ref, *rest):
+    tile_refs, rest = rest[:-7], rest[-7:]
+    (att_ref, dq_ref, dk_ref, dv_ref), (tiles_ref, buf_ref, sems) = rest[:4], rest[4:]
     tokens, features = att_ref.shape
     size = tokens // CHUNKS
+    me = lax.axis_index("ctx")
     copies = []
-    for t in range(CHUNKS):
-        rows = pl.ds(t * size, size)
-        for half in range(2):
-            place = pl.ds(half * tokens + t * size, size)
+
+    def write(in_ref, first, refs):
+        for t in range(CHUNKS):
+            rows = pl.ds(t * size, size)
             for pair in range(features // PAIR):
                 cols = pl.ds(pair * PAIR, PAIR)
-                even = in_ref[2 * pair * repeat, place, :]
-                odd = in_ref[(2 * pair + 1) * repeat, place, :]
-                buf_ref[2 * half, rows, cols] = jnp.concatenate(
-                    (even[:, :HEAD_DIM], odd[:, :HEAD_DIM]), axis=1
+                low, high = halves(in_ref[2 * pair * repeat, rows, :], in_ref[(2 * pair + 1) * repeat, rows, :])
+                buf_ref[first, rows, cols] = low
+                buf_ref[first + 1, rows, cols] = high
+            for n, ref in enumerate(refs):
+                copies.append(
+                    pltpu.make_async_copy(buf_ref.at[first + n, rows], ref.at[rows], sems.at[first + n, t])
                 )
-                buf_ref[2 * half + 1, rows, cols] = jnp.concatenate(
-                    (even[:, HEAD_DIM:], odd[:, HEAD_DIM:]), axis=1
-                )
-        for n, ref in enumerate((dq_ref, att_ref, dk_ref, dv_ref)):
-            copies.append(pltpu.make_async_copy(buf_ref.at[n, rows], ref.at[rows], sems.at[n, t]))
-            copies[-1].start()
+                copies[-1].start()
+
+    write(keys_ref, 0, (dk_ref, dv_ref))
+    for m, ref in enumerate(tile_refs):
+        tiles_ref[me ^ m] = ref[...]
+    write(tiles_ref, 2, (dq_ref, att_ref))
     for copy in copies:
         copy.wait()
 
@@ -206,20 +217,17 @@
 
 
 def last_kernel(repeat, first, size, table_ref, kv_ref, acc_in_ref, *rest):
-    qc_refs, done_refs, (out_ref, acc_ref, late_ref) = rest[:size], rest[size:-3], rest[-3:]
+    qc_refs, keys_ref, out_refs, acc_ref = rest[:size], rest[size], rest[size + 1 : -1], rest[-1]
     tokens = qc_refs[0].shape[0]
     acc_ref[...] = acc_in_ref[...]
-    late = [late_ref.at[m] for m in range(size)]
-    attend_tiles(repeat, first, table_ref, kv_ref, acc_ref, qc_refs, late)
-    for m, ref in enumerate(list(done_refs) + late):
-        out_ref[lax.axis_index("ctx") ^ m, :tokens, :] = ref[...]
+    attend_tiles(repeat, first, table_ref, kv_ref, acc_ref, qc_refs, out_refs)
 
     def finish(d):
         acc = acc_ref[pl.ds(pl.multiple_of(d * tokens, tokens), tokens), :]
         left = lax.broadcasted_iota(jnp.int32, acc.shape, 1) < HEAD_DIM
-        out_ref[d, tokens:, :] = jnp.where(left, acc * SCALE, acc).astype(jnp.bfloat16)
-
-    pl.loop(0, out_ref.shape[0])(finish)
+        keys_ref[d] = jnp.where(left, acc * SCALE, acc).astype(jnp.bfloat16)
+
+    pl.loop(0, keys_ref.shape[0])(finish)
 
 
 def per_device(query, key, value, cotangent, global_ids, rand_owner, rand_local):
@@ -289,29 +297,41 @@
         acc = [outs[0]]
         done += outs[1:]
     first = len(done)
-    grads = pl.pallas_call(
+    keys_out, *outs = pl.pallas_call(
         functools.partial(last_kernel, repeat, first, last),
-        out_shape=jax.ShapeDtypeStruct((devices, 2 * tokens, PAIR), jnp.bfloat16),
-        in_specs=[SMEM] + [VMEM] * (2 + devices),
-        out_specs=VMEM,
-        scratch_shapes=[
-            pltpu.VMEM((devices * tokens, PAIR), jnp.float32),
-            pltpu.VMEM((last, tokens, PAIR), jnp.bfloat16),
-        ],
+        out_shape=[jax.ShapeDtypeStruct((devices, tokens, PAIR), jnp.bfloat16)] + [tile] * last,
+        in_specs=[SMEM] + [VMEM] * (2 + last),
+        out_specs=[VMEM] * (1 + last),
+        scratch_shapes=[pltpu.VMEM((devices * tokens, PAIR), jnp.float32)],
         compiler_params=params,
-    )(table, keys, *acc, *qc[first:], *done)
-    back = lax.all_to_all(grads, "ctx", 0, 0, tiled=True)
+    )(table, keys, *acc, *qc[first:])
+    back = lax.all_to_all(keys_out, "ctx", 0, 0, tiled=True)
+    split = count + EARLY * devices // sum(PARTS)
+    early = [swap(one, count + m) for m, one in enumerate(done[count:split])]
+    held = done[1:count] + done[split:] + outs
+    held = pl.pallas_call(
+        functools.partial(hold_kernel, len(held)),
+        out_shape=[tile] * len(held),
+        in_specs=[VMEM] * len(held) + [pl.BlockSpec(memory_space=pl.ANY)] * len(early),
+        out_specs=[VMEM] * len(held),
+        compiler_params=params,
+        cost_estimate=pl.CostEstimate(flops=10**11, bytes_accessed=1 << 20, transcendentals=0),
+    )(*held, *early)
+    masks = list(range(1, count)) + list(range(split, devices))
+    held = [swap(one, mask) for one, mask in zip(held, masks)]
+    tiles = done[:1] + held[: count - 1] + early + held[count - 1 :]
     return pl.pallas_call(
         functools.partial(unpack_kernel, repeat),
         out_shape=[jax.ShapeDtypeStruct((tokens, features), jnp.bfloat16)] * 4,
-        in_specs=[VMEM],
+        in_specs=[VMEM] * (1 + devices),
         out_specs=[HBM] * 4,
         scratch_shapes=[
+            pltpu.VMEM((devices, tokens, PAIR), jnp.bfloat16),
             pltpu.VMEM((4, tokens, features), jnp.bfloat16),
             pltpu.SemaphoreType.DMA((4, CHUNKS)),
         ],
         compiler_params=params,
-    )(back)
+    )(back, *tiles)
 
 
 def solution(mesh):

time: 114 us -> 110 us (0.965)
  blocking collectives: 50.8 us -> 0 us
  starting transfers between devices: 31.5 us -> 61.9 us
  waiting for transfers between devices: 10.6 us -> 26.1 us
  Pallas kernels: 19.2 us -> 20.4 us
    all_to_all x1 -> x0, blocking collectives: 50.8 us -> none  [per_device(): back = lax.all_to_all(grads, 'ctx', 0, 0, tiled=True)]
    ppermute x15 -> x30, starting transfers between devices: 24.7 us -> 50.6 us  [swap(): return lax.ppermute(array, 'ctx', [(i, i ^ mask) for i in range(devices)])]
    ppermute x15 -> x30, waiting for transfers between devices: 10.6 us -> 26.1 us  [swap(): return lax.ppermute(array, 'ctx', [(i, i ^ mask) for i in range(devices)])]
    all_to_all x0 -> x1, starting transfers between devices: none -> 4.51 us  [per_device(): back = lax.all_to_all(keys_out, 'ctx', 0, 0, tiled=True)]
  transfers between devices with their start and end apart: 16 -> 32, of which waited for: 5 -> 10; matrix products, arithmetic and copies ran while one was open for 0% -> 0% of each run, Pallas kernels for 11% -> 15%
where the time goes in v7:
time: 110 us; the launch traced here: 109 us
  starting transfers between devices  61.9 us (56%)
  waiting for transfers between devices  26.1 us (24%)
  Pallas kernels  20.4 us (19%)
    ppermute x30, starting transfers between devices, swap(): return lax.ppermute(array, 'ctx', [(i, i ^ mask) for i in range(devices)])  50.6 us
    ppermute x30, waiting for transfers between devices, swap(): return lax.ppermute(array, 'ctx', [(i, i ^ mask) for i in range(devices)])  26.1 us
    pallas_call x3, Pallas kernels, per_device(): pl.pallas_call(functools.partial(part_kernel, repeat, first, size), out_s...  10.9 us
    all_to_all x1, starting transfers between devices, per_device(): lax.all_to_all(packed, 'ctx', 0, 0, tiled=True)  6.75 us
    all_to_all x1, starting transfers between devices, per_device(): back = lax.all_to_all(keys_out, 'ctx', 0, 0, tiled=True)  4.51 us
    pallas_call x1, Pallas kernels, per_device(): pl.pallas_call(functools.partial(last_kernel, repeat, first, last), out_s...  3.35 us
    pallas_call x1, Pallas kernels, per_device(): pl.pallas_call(functools.partial(pack_keys_kernel, repeat), out_shape=jax...  2.42 us
  transfers between devices with their start and end apart: 32, of which 10 were waited for; matrix products, arithmetic and copies ran while one was open for 0% of the time, Pallas kernels for 15%

profile of v7, /device:TPU:9, one launch (start us, length us, event | category | flops | bytes accessed | tf_op | source)
XLA Modules:
  0.0 109.4 jit_solution(17862956181151356397)
XLA Ops:
  0.7 2.4 %shard_map.102 = bf16[16,256,128]{2,1,0:T(8,128)(2,1)} custom-call(bf16[256,1024]{1,0:T(8,128)(2,1)} %k_ref.1, bf16[256,1024]{1,0:T(8,128)(2,1)} %v_ref.1), custom_call_target="tpu_custom_call" | custom-call | tf_op jit(solution)/shard_map/pallas_call | solution.py:243
  3.1 6.8 %all-to-all-start = ((bf16[16,256,128]{2,1,0:T(8,128)(2,1)}), bf16[16,256,128]{2,1,0:T(8,128)(2,1)S(1)}, u32[]{:S(2)}, u32[]{:S(2)}) async-start(bf16[16,256,128]{2,1,0:T(8,128)(2,1)} %shard_map.102), calls=%async_computation | async-start | bytes 2097152 | tf_op jit(solution)/shard_map/all_to_all | solution.py:256
  17.5 2.9 %collective-permute-start.6 = (bf16[256,128]{1,0:T(8,128)(2,1)S(1)}, bf16[256,128]{1,0:T(8,128)(2,1)S(1)}, u32[]{:S(2)}, u32[]{:S(2)}) collective-permute-start(bf16[256,128]{1,0:T(8,128)(2,1)S(1)} %get-tuple-element.58), channel_id=1, source_target_pairs={{0,7},{1,6},{2,5},{3,4},{4,3},{5,2},{6,1},{7,0},{8,15},{9,14},{10,... | collective-permute-start | bytes 196616 | tf_op jit(solution)/shard_map/ppermute | solution.py:259
  20.4 5.1 %collective-permute-start.7 = (bf16[256,128]{1,0:T(8,128)(2,1)S(1)}, bf16[256,128]{1,0:T(8,128)(2,1)S(1)}, u32[]{:S(2)}, u32[]{:S(2)}) collective-permute-start(bf16[256,128]{1,0:T(8,128)(2,1)S(1)} %get-tuple-element.60), channel_id=1, source_target_pairs={{0,8},{1,9},{2,10},{3,11},{4,12},{5,13},{6,14},{7,15},{8,0},{9,1},... | collective-permute-start | bytes 196616 | tf_op jit(solution)/shard_map/ppermute | solution.py:259
  25.5 4.2 %collective-permute-done.3.rest_4_ = bf16[256,128]{1,0:T(8,128)(2,1)S(1)} collective-permute-done((bf16[256,128]{1,0:T(8,128)(2,1)S(1)}, bf16[256,128]{1,0:T(8,128)(2,1)S(1)}, u32[]{:S(2)}, u32[]{:S(2)}) %collective-permute-start.3) | collective-permute-done | bytes 65568 | tf_op jit(solution)/shard_map/ppermute | solution.py:259
  29.7 2.1 %collective-permute-start.8 = (bf16[256,128]{1,0:T(8,128)(2,1)S(1)}, bf16[256,128]{1,0:T(8,128)(2,1)S(1)}, u32[]{:S(2)}, u32[]{:S(2)}) collective-permute-start(bf16[256,128]{1,0:T(8,128)(2,1)S(1)} %get-tuple-element.61), channel_id=1, source_target_pairs={{0,9},{1,8},{2,11},{3,10},{4,13},{5,12},{6,15},{7,14},{8,1},{9,0},... | collective-permute-start | bytes 196616 | tf_op jit(solution)/shard_map/ppermute | solution.py:259
  31.8 2.1 %collective-permute-start.9 = (bf16[256,128]{1,0:T(8,128)(2,1)S(1)}, bf16[256,128]{1,0:T(8,128)(2,1)S(1)}, u32[]{:S(2)}, u32[]{:S(2)}) collective-permute-start(bf16[256,128]{1,0:T(8,128)(2,1)S(1)} %get-tuple-element.62), channel_id=1, source_target_pairs={{0,10},{1,11},{2,8},{3,9},{4,14},{5,15},{6,12},{7,13},{8,2},{9,3},... | collective-permute-start | bytes 196616 | tf_op jit(solution)/shard_map/ppermute | solution.py:259
  36.2 1.9 %collective-permute-start.11 = (bf16[256,128]{1,0:T(8,128)(2,1)S(1)}, bf16[256,128]{1,0:T(8,128)(2,1)S(1)}, u32[]{:S(2)}, u32[]{:S(2)}) collective-permute-start(bf16[256,128]{1,0:T(8,128)(2,1)S(1)} %get-tuple-element.65), channel_id=1, source_target_pairs={{0,12},{1,13},{2,14},{3,15},{4,8},{5,9},{6,10},{7,11},{8,4},{9,5},... | collective-permute-start | bytes 196616 | tf_op jit(solution)/shard_map/ppermute | solution.py:259
  38.1 5.6 %shard_map.104 = (f32[4096,128]{1,0:T(8,128)S(1)}, bf16[256,128]{1,0:T(8,128)(2,1)S(1)}, bf16[256,128]{1,0:T(8,128)(2,1)S(1)}, bf16[256,128]{1,0:T(8,128)(2,1)S(...) custom-call(s32[386]{0:T(512)S(1)} %constant_dynamic-update-slice_fu, ...), custom_call_target="tpu_custom_call" | custom-call | flops 8000000000 | bytes 4194304 | tf_op jit(solution)/shard_map/pallas_call | solution.py:289
  43.8 2.0 %collective-permute-start.13 = (bf16[256,128]{1,0:T(8,128)(2,1)S(1)}, bf16[256,128]{1,0:T(8,128)(2,1)S(1)}, u32[]{:S(2)}, u32[]{:S(2)}) collective-permute-start(bf16[256,128]{1,0:T(8,128)(2,1)S(1)} %get-tuple-element.68), channel_id=1, source_target_pairs={{0,14},{1,15},{2,12},{3,13},{4,10},{5,11},{6,8},{7,9},{8,6},{9,7},... | collective-permute-start | bytes 196616 | tf_op jit(solution)/shard_map/ppermute | solution.py:259
  47.2 3.2 %shard_map.106 = (f32[4096,128]{1,0:T(8,128)S(1)}, bf16[256,128]{1,0:T(8,128)(2,1)S(1)}, bf16[256,128]{1,0:T(8,128)(2,1)S(1)}, bf16[256,128]{1,0:T(8,128)(2,1)S(1)}, bf16[256,128]{1,0:T(8,128)(2,1)S(1)}) custom-call(s32[386]{0:T(512)S(1)} %constant_dynamic-update-slice_fusion.table_ref, bf16[4096,128]{1,0:T(8,128)(2,1)S(1)} %bitcast.4, ...), custom_call_target="tpu_custom_call" | custom-call | flops 4000000000 | bytes 4194304 | tf_op jit(solution)/shard_map/pallas_call | solution.py:289
  50.5 4.0 %collective-permute-start.15 = (bf16[256,128]{1,0:T(8,128)(2,1)S(1)}, bf16[256,128]{1,0:T(8,128)(2,1)S(1)}, u32[]{:S(2)}, u32[]{:S(2)}) collective-permute-start(bf16[256,128]{1,0:T(8,128)(2,1)S(1)} %get-tuple-element.83), channel_id=1, source_target_pairs={{0,8},{1,9},{2,10},{3,11},{4,12},{5,13},{6,14},{7,15},{8,0},{9,1},... | collective-permute-start | bytes 196616 | tf_op jit(solution)/shard_map/ppermute | solution.py:259
  55.4 3.5 %collective-permute-start.17 = (bf16[256,128]{1,0:T(8,128)(2,1)S(1)}, bf16[256,128]{1,0:T(8,128)(2,1)S(1)}, u32[]{:S(2)}, u32[]{:S(2)}) collective-permute-start(bf16[256,128]{1,0:T(8,128)(2,1)S(1)} %get-tuple-element.85), channel_id=1, source_target_pairs={{0,10},{1,11},{2,8},{3,9},{4,14},{5,15},{6,12},{7,13},{8,2},{9,3},... | collective-permute-start | bytes 196616 | tf_op jit(solution)/shard_map/ppermute | solution.py:259
  59.2 2.1 %shard_map.107 = (f32[4096,128]{1,0:T(8,128)S(1)}, bf16[256,128]{1,0:T(8,128)(2,1)S(1)}, bf16[256,128]{1,0:T(8,128)(2,1)S(1)}) custom-call(s32[386]{0:T(512)S(1)} %constant_dynamic-update-slice_fusion.table_ref, bf16[4096,128]{1,0:T(8,128)(2,1)S(1)} %bitcast.5, f32[4096,128]{1,0:T(8,128)S(1)} %get-tuple-element.64.rest_0_, ...), custom_call_target="tpu_custom_call" | custom-call | flops 2000000000 | bytes 4194304 | tf_op jit(solution)/shard_map/pallas_call | solution.py:289
  62.8 3.3 %shard_map.108 = (bf16[16,256,128]{2,1,0:T(8,128)(2,1)}, bf16[256,128]{1,0:T(8,128)(2,1)S(1)}, bf16[256,128]{1,0:T(8,128)(2,1)S(1)}) custom-call(s32[386]{0:T(512)S(1)} %constant_dynamic-update-slice_fusion.table_ref, bf16[4096,128]{1,0:T(8,128)(2,1)S(1)} %bitcast.6, f32[4096,128]{1,0:T(8,128)S(1)} %get-tuple-element.67.acc_in_ref, ...), custom_call_target="tpu_custom_call" | custom-call | tf_op jit(solution)/shard_map/pallas_call | solution.py:300
  66.2 4.5 %all-to-all-start.1 = ((bf16[16,256,128]{2,1,0:T(8,128)(2,1)}), bf16[16,256,128]{2,1,0:T(8,128)(2,1)S(1)}, u32[]{:S(2)}, u32[]{:S(2)}) async-start(bf16[16,256,128]{2,1,0:T(8,128)(2,1)} %get-tuple-element.70), calls=%async_computation.1 | async-start | bytes 2097152 | tf_op jit(solution)/shard_map/all_to_all | solution.py:308
  75.9 2.4 %collective-permute-done.20.rest_2_ = bf16[256,128]{1,0:T(8,128)(2,1)S(1)} collective-permute-done((bf16[256,128]{1,0:T(8,128)(2,1)S(1)}, bf16[256,128]{1,0:T(8,128)(2,1)S(1)}, u32[]{:S(2)}, u32[]{:S(2)}) %collective-permute-start.20) | collective-permute-done | bytes 65568 | tf_op jit(solution)/shard_map/ppermute | solution.py:259
  78.4 2.9 %collective-permute-start.25 = (bf16[256,128]{1,0:T(8,128)(2,1)S(1)}, bf16[256,128]{1,0:T(8,128)(2,1)S(1)}, u32[]{:S(2)}, u32[]{:S(2)}) collective-permute-start(bf16[256,128]{1,0:T(8,128)(2,1)S(1)} %get-tuple-element.93), channel_id=1, source_target_pairs={{0,7},{1,6},{2,5},{3,4},{4,3},{5,2},{6,1},{7,0},{8,15},{9,14},{10,... | collective-permute-start | bytes 196616 | tf_op jit(solution)/shard_map/ppermute | solution.py:259
  81.2 2.6 %collective-permute-start.26 = (bf16[256,128]{1,0:T(8,128)(2,1)S(1)}, bf16[256,128]{1,0:T(8,128)(2,1)S(1)}, u32[]{:S(2)}, u32[]{:S(2)}) collective-permute-start(bf16[256,128]{1,0:T(8,128)(2,1)S(1)} %get-tuple-element.94), channel_id=1, source_target_pairs={{0,12},{1,13},{2,14},{3,15},{4,8},{5,9},{6,10},{7,11},{8,4},{9,5},... | collective-permute-start | bytes 196616 | tf_op jit(solution)/shard_map/ppermute | solution.py:259
  83.8 6.7 %collective-permute-done.22.rest_4_ = bf16[256,128]{1,0:T(8,128)(2,1)S(1)} collective-permute-done((bf16[256,128]{1,0:T(8,128)(2,1)S(1)}, bf16[256,128]{1,0:T(8,128)(2,1)S(1)}, u32[]{:S(2)}, u32[]{:S(2)}) %collective-permute-start.22) | collective-permute-done | bytes 65568 | tf_op jit(solution)/shard_map/ppermute | solution.py:259
  90.6 3.1 %collective-permute-start.27 = (bf16[256,128]{1,0:T(8,128)(2,1)S(1)}, bf16[256,128]{1,0:T(8,128)(2,1)S(1)}, u32[]{:S(2)}, u32[]{:S(2)}) collective-permute-start(bf16[256,128]{1,0:T(8,128)(2,1)S(1)} %get-tuple-element.95), channel_id=1, source_target_pairs={{0,13},{1,12},{2,15},{3,14},{4,9},{5,8},{6,11},{7,10},{8,5},{9,4},... | collective-permute-start | bytes 196616 | tf_op jit(solution)/shard_map/ppermute | solution.py:259
  93.7 2.0 %collective-permute-start.28 = (bf16[256,128]{1,0:T(8,128)(2,1)S(1)}, bf16[256,128]{1,0:T(8,128)(2,1)S(1)}, u32[]{:S(2)}, u32[]{:S(2)}) collective-permute-start(bf16[256,128]{1,0:T(8,128)(2,1)S(1)} %get-tuple-element.96), channel_id=1, source_target_pairs={{0,14},{1,15},{2,12},{3,13},{4,10},{5,11},{6,8},{7,9},{8,6},{9,7},... | collective-permute-start | bytes 196616 | tf_op jit(solution)/shard_map/ppermute | solution.py:259
  97.4 3.2 %collective-permute-done.26.rest_12_ = bf16[256,128]{1,0:T(8,128)(2,1)S(1)} collective-permute-done((bf16[256,128]{1,0:T(8,128)(2,1)S(1)}, bf16[256,128]{1,0:T(8,128)(2,1)S(1)}, u32[]{:S(2)}, u32[]{:S(2)}) %collective-permute-start.26) | collective-permute-done | bytes 65568 | tf_op jit(solution)/shard_map/ppermute | solution.py:259
  100.6 3.9 %collective-permute-done.27.rest_13_ = bf16[256,128]{1,0:T(8,128)(2,1)S(1)} collective-permute-done((bf16[256,128]{1,0:T(8,128)(2,1)S(1)}, bf16[256,128]{1,0:T(8,128)(2,1)S(1)}, u32[]{:S(2)}, u32[]{:S(2)}) %collective-permute-start.27) | collective-permute-done | bytes 65568 | tf_op jit(solution)/shard_map/ppermute | solution.py:259
  (64 shorter events, 25.8 us)
Async XLA Ops:
  3.1 35.0 %all-to-all-start = ((bf16[16,256,128]{2,1,0:T(8,128)(2,1)}), bf16[16,256,128]{2,1,0:T(8,128)(2,1)S(1)}, u32[]{:S(2)}, u32[]{:S(2)}) async-start(bf16[16,256,128]{2,1,0:T(8,128)(2,1)} %shard_map.102), calls=%async_computation | async-start | bytes 2097152 | tf_op jit(solution)/shard_map/all_to_all | solution.py:256
  13.1 16.6 %collective-permute-start.3 = (bf16[256,128]{1,0:T(8,128)(2,1)S(1)}, bf16[256,128]{1,0:T(8,128)(2,1)S(1)}, u32[]{:S(2)}, u32[]{:S(2)}) collective-permute-start(bf16[256,128]{1,0:T(8,128)(2,1)S(1)} %get-tuple-element.55), channel_id=1, source_target_pairs={{0,4},{1,5},{2,6},{3,7},{4,0},{5,1},{6,2},{7,3},{8,12},{9,13},{10,... | collective-permute-start | bytes 196616 | tf_op jit(solution)/shard_map/ppermute | solution.py:259
  13.2 18.6 %collective-permute-start.4 = (bf16[256,128]{1,0:T(8,128)(2,1)S(1)}, bf16[256,128]{1,0:T(8,128)(2,1)S(1)}, u32[]{:S(2)}, u32[]{:S(2)}) collective-permute-start(bf16[256,128]{1,0:T(8,128)(2,1)S(1)} %get-tuple-element.56), channel_id=1, source_target_pairs={{0,5},{1,4},{2,7},{3,6},{4,1},{5,0},{6,3},{7,2},{8,13},{9,12},{10,... | collective-permute-start | bytes 196616 | tf_op jit(solution)/shard_map/ppermute | solution.py:259
  16.0 18.0 %collective-permute-start.5 = (bf16[256,128]{1,0:T(8,128)(2,1)S(1)}, bf16[256,128]{1,0:T(8,128)(2,1)S(1)}, u32[]{:S(2)}, u32[]{:S(2)}) collective-permute-start(bf16[256,128]{1,0:T(8,128)(2,1)S(1)} %get-tuple-element.57), channel_id=1, source_target_pairs={{0,6},{1,7},{2,4},{3,5},{4,2},{5,3},{6,0},{7,1},{8,14},{9,15},{10,... | collective-permute-start | bytes 196616 | tf_op jit(solution)/shard_map/ppermute | solution.py:259
  17.5 18.6 %collective-permute-start.6 = (bf16[256,128]{1,0:T(8,128)(2,1)S(1)}, bf16[256,128]{1,0:T(8,128)(2,1)S(1)}, u32[]{:S(2)}, u32[]{:S(2)}) collective-permute-start(bf16[256,128]{1,0:T(8,128)(2,1)S(1)} %get-tuple-element.58), channel_id=1, source_target_pairs={{0,7},{1,6},{2,5},{3,4},{4,3},{5,2},{6,1},{7,0},{8,15},{9,14},{10,... | collective-permute-start | bytes 196616 | tf_op jit(solution)/shard_map/ppermute | solution.py:259
  20.4 23.3 %collective-permute-start.7 = (bf16[256,128]{1,0:T(8,128)(2,1)S(1)}, bf16[256,128]{1,0:T(8,128)(2,1)S(1)}, u32[]{:S(2)}, u32[]{:S(2)}) collective-permute-start(bf16[256,128]{1,0:T(8,128)(2,1)S(1)} %get-tuple-element.60), channel_id=1, source_target_pairs={{0,8},{1,9},{2,10},{3,11},{4,12},{5,13},{6,14},{7,15},{8,0},{9,1},... | collective-permute-start | bytes 196616 | tf_op jit(solution)/shard_map/ppermute | solution.py:259
  29.7 14.1 %collective-permute-start.8 = (bf16[256,128]{1,0:T(8,128)(2,1)S(1)}, bf16[256,128]{1,0:T(8,128)(2,1)S(1)}, u32[]{:S(2)}, u32[]{:S(2)}) collective-permute-start(bf16[256,128]{1,0:T(8,128)(2,1)S(1)} %get-tuple-element.61), channel_id=1, source_target_pairs={{0,9},{1,8},{2,11},{3,10},{4,13},{5,12},{6,15},{7,14},{8,1},{9,0},... | collective-permute-start | bytes 196616 | tf_op jit(solution)/shard_map/ppermute | solution.py:259
  31.8 14.0 %collective-permute-start.9 = (bf16[256,128]{1,0:T(8,128)(2,1)S(1)}, bf16[256,128]{1,0:T(8,128)(2,1)S(1)}, u32[]{:S(2)}, u32[]{:S(2)}) collective-permute-start(bf16[256,128]{1,0:T(8,128)(2,1)S(1)} %get-tuple-element.62), channel_id=1, source_target_pairs={{0,10},{1,11},{2,8},{3,9},{4,14},{5,15},{6,12},{7,13},{8,2},{9,3},... | collective-permute-start | bytes 196616 | tf_op jit(solution)/shard_map/ppermute | solution.py:259
  34.0 13.3 %collective-permute-start.10 = (bf16[256,128]{1,0:T(8,128)(2,1)S(1)}, bf16[256,128]{1,0:T(8,128)(2,1)S(1)}, u32[]{:S(2)}, u32[]{:S(2)}) collective-permute-start(bf16[256,128]{1,0:T(8,128)(2,1)S(1)} %get-tuple-element.63), channel_id=1, source_target_pairs={{0,11},{1,10},{2,9},{3,8},{4,15},{5,14},{6,13},{7,12},{8,3},{9,2},... | collective-permute-start | bytes 196616 | tf_op jit(solution)/shard_map/ppermute | solution.py:259
  36.2 18.4 %collective-permute-start.11 = (bf16[256,128]{1,0:T(8,128)(2,1)S(1)}, bf16[256,128]{1,0:T(8,128)(2,1)S(1)}, u32[]{:S(2)}, u32[]{:S(2)}) collective-permute-start(bf16[256,128]{1,0:T(8,128)(2,1)S(1)} %get-tuple-element.65), channel_id=1, source_target_pairs={{0,12},{1,13},{2,14},{3,15},{4,8},{5,9},{6,10},{7,11},{8,4},{9,5},... | collective-permute-start | bytes 196616 | tf_op jit(solution)/shard_map/ppermute | solution.py:259
  43.8 15.0 %collective-permute-start.13 = (bf16[256,128]{1,0:T(8,128)(2,1)S(1)}, bf16[256,128]{1,0:T(8,128)(2,1)S(1)}, u32[]{:S(2)}, u32[]{:S(2)}) collective-permute-start(bf16[256,128]{1,0:T(8,128)(2,1)S(1)} %get-tuple-element.68), channel_id=1, source_target_pairs={{0,14},{1,15},{2,12},{3,13},{4,10},{5,11},{6,8},{7,9},{8,6},{9,7},... | collective-permute-start | bytes 196616 | tf_op jit(solution)/shard_map/ppermute | solution.py:259
  45.9 17.0 %collective-permute-start.14 = (bf16[256,128]{1,0:T(8,128)(2,1)S(1)}, bf16[256,128]{1,0:T(8,128)(2,1)S(1)}, u32[]{:S(2)}, u32[]{:S(2)}) collective-permute-start(bf16[256,128]{1,0:T(8,128)(2,1)S(1)} %get-tuple-element.69), channel_id=1, source_target_pairs={{0,15},{1,14},{2,13},{3,12},{4,11},{5,10},{6,9},{7,8},{8,7},{9,6},... | collective-permute-start | bytes 196616 | tf_op jit(solution)/shard_map/ppermute | solution.py:259
  50.5 20.2 %collective-permute-start.15 = (bf16[256,128]{1,0:T(8,128)(2,1)S(1)}, bf16[256,128]{1,0:T(8,128)(2,1)S(1)}, u32[]{:S(2)}, u32[]{:S(2)}) collective-permute-start(bf16[256,128]{1,0:T(8,128)(2,1)S(1)} %get-tuple-element.83), channel_id=1, source_target_pairs={{0,8},{1,9},{2,10},{3,11},{4,12},{5,13},{6,14},{7,15},{8,0},{9,1},... | collective-permute-start | bytes 196616 | tf_op jit(solution)/shard_map/ppermute | solution.py:259
  54.5 16.2 %collective-permute-start.16 = (bf16[256,128]{1,0:T(8,128)(2,1)S(1)}, bf16[256,128]{1,0:T(8,128)(2,1)S(1)}, u32[]{:S(2)}, u32[]{:S(2)}) collective-permute-start(bf16[256,128]{1,0:T(8,128)(2,1)S(1)} %get-tuple-element.84), channel_id=1, source_target_pairs={{0,9},{1,8},{2,11},{3,10},{4,13},{5,12},{6,15},{7,14},{8,1},{9,0},... | collective-permute-start | bytes 196616 | tf_op jit(solution)/shard_map/ppermute | solution.py:259
  55.4 15.4 %collective-permute-start.17 = (bf16[256,128]{1,0:T(8,128)(2,1)S(1)}, bf16[256,128]{1,0:T(8,128)(2,1)S(1)}, u32[]{:S(2)}, u32[]{:S(2)}) collective-permute-start(bf16[256,128]{1,0:T(8,128)(2,1)S(1)} %get-tuple-element.85), channel_id=1, source_target_pairs={{0,10},{1,11},{2,8},{3,9},{4,14},{5,15},{6,12},{7,13},{8,2},{9,3},... | collective-permute-start | bytes 196616 | tf_op jit(solution)/shard_map/ppermute | solution.py:259
  66.2 41.6 %all-to-all-start.1 = ((bf16[16,256,128]{2,1,0:T(8,128)(2,1)}), bf16[16,256,128]{2,1,0:T(8,128)(2,1)S(1)}, u32[]{:S(2)}, u32[]{:S(2)}) async-start(bf16[16,256,128]{2,1,0:T(8,128)(2,1)} %get-tuple-element.70), calls=%async_computation.1 | async-start | bytes 2097152 | tf_op jit(solution)/shard_map/all_to_all | solution.py:308
  73.0 17.5 %collective-permute-start.22 = (bf16[256,128]{1,0:T(8,128)(2,1)S(1)}, bf16[256,128]{1,0:T(8,128)(2,1)S(1)}, u32[]{:S(2)}, u32[]{:S(2)}) collective-permute-start(bf16[256,128]{1,0:T(8,128)(2,1)S(1)} %get-tuple-element.90), channel_id=1, source_target_pairs={{0,4},{1,5},{2,6},{3,7},{4,0},{5,1},{6,2},{7,3},{8,12},{9,13},{10,... | collective-permute-start | bytes 196616 | tf_op jit(solution)/shard_map/ppermute | solution.py:259
  73.1 20.6 %collective-permute-start.23 = (bf16[256,128]{1,0:T(8,128)(2,1)S(1)}, bf16[256,128]{1,0:T(8,128)(2,1)S(1)}, u32[]{:S(2)}, u32[]{:S(2)}) collective-permute-start(bf16[256,128]{1,0:T(8,128)(2,1)S(1)} %get-tuple-element.91), channel_id=1, source_target_pairs={{0,5},{1,4},{2,7},{3,6},{4,1},{5,0},{6,3},{7,2},{8,13},{9,12},{10,... | collective-permute-start | bytes 196616 | tf_op jit(solution)/shard_map/ppermute | solution.py:259
  74.7 21.0 %collective-permute-start.24 = (bf16[256,128]{1,0:T(8,128)(2,1)S(1)}, bf16[256,128]{1,0:T(8,128)(2,1)S(1)}, u32[]{:S(2)}, u32[]{:S(2)}) collective-permute-start(bf16[256,128]{1,0:T(8,128)(2,1)S(1)} %get-tuple-element.92), channel_id=1, source_target_pairs={{0,6},{1,7},{2,4},{3,5},{4,2},{5,3},{6,0},{7,1},{8,14},{9,15},{10,... | collective-permute-start | bytes 196616 | tf_op jit(solution)/shard_map/ppermute | solution.py:259
  78.4 19.0 %collective-permute-start.25 = (bf16[256,128]{1,0:T(8,128)(2,1)S(1)}, bf16[256,128]{1,0:T(8,128)(2,1)S(1)}, u32[]{:S(2)}, u32[]{:S(2)}) collective-permute-start(bf16[256,128]{1,0:T(8,128)(2,1)S(1)} %get-tuple-element.93), channel_id=1, source_target_pairs={{0,7},{1,6},{2,5},{3,4},{4,3},{5,2},{6,1},{7,0},{8,15},{9,14},{10,... | collective-permute-start | bytes 196616 | tf_op jit(solution)/shard_map/ppermute | solution.py:259
  81.2 19.3 %collective-permute-start.26 = (bf16[256,128]{1,0:T(8,128)(2,1)S(1)}, bf16[256,128]{1,0:T(8,128)(2,1)S(1)}, u32[]{:S(2)}, u32[]{:S(2)}) collective-permute-start(bf16[256,128]{1,0:T(8,128)(2,1)S(1)} %get-tuple-element.94), channel_id=1, source_target_pairs={{0,12},{1,13},{2,14},{3,15},{4,8},{5,9},{6,10},{7,11},{8,4},{9,5},... | collective-permute-start | bytes 196616 | tf_op jit(solution)/shard_map/ppermute | solution.py:259
  90.6 13.9 %collective-permute-start.27 = (bf16[256,128]{1,0:T(8,128)(2,1)S(1)}, bf16[256,128]{1,0:T(8,128)(2,1)S(1)}, u32[]{:S(2)}, u32[]{:S(2)}) collective-permute-start(bf16[256,128]{1,0:T(8,128)(2,1)S(1)} %get-tuple-element.95), channel_id=1, source_target_pairs={{0,13},{1,12},{2,15},{3,14},{4,9},{5,8},{6,11},{7,10},{8,5},{9,4},... | collective-permute-start | bytes 196616 | tf_op jit(solution)/shard_map/ppermute | solution.py:259
  93.7 12.5 %collective-permute-start.28 = (bf16[256,128]{1,0:T(8,128)(2,1)S(1)}, bf16[256,128]{1,0:T(8,128)(2,1)S(1)}, u32[]{:S(2)}, u32[]{:S(2)}) collective-permute-start(bf16[256,128]{1,0:T(8,128)(2,1)S(1)} %get-tuple-element.96), channel_id=1, source_target_pairs={{0,14},{1,15},{2,12},{3,13},{4,10},{5,11},{6,8},{7,9},{8,6},{9,7},... | collective-permute-start | bytes 196616 | tf_op jit(solution)/shard_map/ppermute | solution.py:259
  95.7 12.0 %collective-permute-start.29 = (bf16[256,128]{1,0:T(8,128)(2,1)S(1)}, bf16[256,128]{1,0:T(8,128)(2,1)S(1)}, u32[]{:S(2)}, u32[]{:S(2)}) collective-permute-start(bf16[256,128]{1,0:T(8,128)(2,1)S(1)} %get-tuple-element.97), channel_id=1, source_target_pairs={{0,15},{1,14},{2,13},{3,12},{4,11},{5,10},{6,9},{7,8},{8,7},{9,6},... | collective-permute-start | bytes 196616 | tf_op jit(solution)/shard_map/ppermute | solution.py:259
  (13 other events, 123.9 us)

commit v8 on v7

--- a/solution.py
+++ b/solution.py
@@ -19,8 +19,8 @@
 NEG_FILL = -1e30
 UNROLL = 8
 CHUNKS = 4
-EARLY = 4
-PARTS = (8, 4, 2, 2)
+EARLY = 5
+PARTS = (8, 5, 3)
 SCALE = HEAD_DIM ** -0.5
 EXP_SCALE = SCALE * math.log2(math.e)
 VMEM = pl.BlockSpec(memory_space=pltpu.VMEM)
@@ -217,17 +217,21 @@
 
 
 def last_kernel(repeat, first, size, table_ref, kv_ref, acc_in_ref, *rest):
-    qc_refs, keys_ref, out_refs, acc_ref = rest[:size], rest[size], rest[size + 1 : -1], rest[-1]
+    qc_refs, keys_ref, out_refs = rest[:size], rest[size], rest[size + 1 : -3]
+    acc_ref, tile_ref, sems = rest[-3:]
     tokens = qc_refs[0].shape[0]
     acc_ref[...] = acc_in_ref[...]
     attend_tiles(repeat, first, table_ref, kv_ref, acc_ref, qc_refs, out_refs)
 
-    def finish(d):
-        acc = acc_ref[pl.ds(pl.multiple_of(d * tokens, tokens), tokens), :]
+    copies = []
+    for d in range(keys_ref.shape[0]):
+        acc = acc_ref[pl.ds(d * tokens, tokens), :]
         left = lax.broadcasted_iota(jnp.int32, acc.shape, 1) < HEAD_DIM
-        keys_ref[d] = jnp.where(left, acc * SCALE, acc).astype(jnp.bfloat16)
-
-    pl.loop(0, keys_ref.shape[0])(finish)
+        tile_ref[d] = jnp.where(left, acc * SCALE, acc).astype(jnp.bfloat16)
+        copies.append(pltpu.make_async_copy(tile_ref.at[d], keys_ref.at[d], sems.at[d]))
+        copies[-1].start()
+    for copy in copies:
+        copy.wait()
 
 
 def per_device(query, key, value, cotangent, global_ids, rand_owner, rand_local):
@@ -301,8 +305,12 @@
         functools.partial(last_kernel, repeat, first, last),
         out_shape=[jax.ShapeDtypeStruct((devices, tokens, PAIR), jnp.bfloat16)] + [tile] * last,
         in_specs=[SMEM] + [VMEM] * (2 + last),
-        out_specs=[VMEM] * (1 + last),
-        scratch_shapes=[pltpu.VMEM((devices * tokens, PAIR), jnp.float32)],
+        out_specs=[HBM] + [VMEM] * last,
+        scratch_shapes=[
+            pltpu.VMEM((devices * tokens, PAIR), jnp.float32),
+            pltpu.VMEM((devices, tokens, PAIR), jnp.bfloat16),
+            pltpu.SemaphoreType.DMA((devices,)),
+        ],
         compiler_params=params,
     )(table, keys, *acc, *qc[first:])
     back = lax.all_to_all(keys_out, "ctx", 0, 0, tiled=True)

time: 110 us -> 108 us (0.982)
  starting transfers between devices: 61.9 us -> 59.8 us
  waiting for transfers between devices: 26.1 us -> 28 us
    ppermute x30, starting transfers between devices: 50.6 us -> 45.7 us  [swap(): return lax.ppermute(array, 'ctx', [(i, i ^ mask) for i in range(devices)])]
    all_to_all x1, starting transfers between devices: 4.51 us -> 7.29 us  [per_device(): back = lax.all_to_all(keys_out, 'ctx', 0, 0, tiled=True)]
    ppermute x30, waiting for transfers between devices: 26.1 us -> 27.9 us  [swap(): return lax.ppermute(array, 'ctx', [(i, i ^ mask) for i in range(devices)])]
    pallas_call x3 -> x2, Pallas kernels: 10.9 us -> 9.27 us  [per_device(): pl.pallas_call(functools.partial(part_kernel, repeat, first, size), out_s...]
  transfers between devices with their start and end apart: 32 -> 32, of which waited for: 10 -> 10; matrix products, arithmetic and copies ran while one was open for 0% -> 0% of each run, Pallas kernels for 15% -> 14%
where the time goes in v8:
time: 108 us
  starting transfers between devices  59.8 us (55%)
  waiting for transfers between devices  28 us (26%)
  Pallas kernels  19.3 us (18%)
    ppermute x30, starting transfers between devices, swap(): return lax.ppermute(array, 'ctx', [(i, i ^ mask) for i in range(devices)])  45.7 us
    ppermute x30, waiting for transfers between devices, swap(): return lax.ppermute(array, 'ctx', [(i, i ^ mask) for i in range(devices)])  27.9 us
    pallas_call x2, Pallas kernels, per_device(): pl.pallas_call(functools.partial(part_kernel, repeat, first, size), out_s...  9.27 us
    all_to_all x1, starting transfers between devices, per_device(): back = lax.all_to_all(keys_out, 'ctx', 0, 0, tiled=True)  7.29 us
    all_to_all x1, starting transfers between devices, per_device(): lax.all_to_all(packed, 'ctx', 0, 0, tiled=True)  6.75 us
    pallas_call x1, Pallas kernels, per_device(): pl.pallas_call(functools.partial(last_kernel, repeat, first, last), out_s...  3.87 us
    pallas_call x1, Pallas kernels, per_device(): pl.pallas_call(functools.partial(pack_keys_kernel, repeat), out_shape=jax...  2.44 us
  transfers between devices with their start and end apart: 32, of which 10 were waited for; matrix products, arithmetic and copies ran while one was open for 0% of the time, Pallas kernels for 14%

profile of v8, /device:TPU:9, one launch (start us, length us, event | category | flops | bytes accessed | tf_op | source)
XLA Modules:
  0.0 108.0 jit_solution(11346236140142928707)
XLA Ops:
  0.7 2.4 %shard_map.102 = bf16[16,256,128]{2,1,0:T(8,128)(2,1)} custom-call(bf16[256,1024]{1,0:T(8,128)(2,1)} %k_ref.1, bf16[256,1024]{1,0:T(8,128)(2,1)} %v_ref.1), custom_call_target="tpu_custom_call" | custom-call | tf_op jit(solution)/shard_map/pallas_call | solution.py:247
  3.1 6.8 %all-to-all-start = ((bf16[16,256,128]{2,1,0:T(8,128)(2,1)}), bf16[16,256,128]{2,1,0:T(8,128)(2,1)S(1)}, u32[]{:S(2)}, u32[]{:S(2)}) async-start(bf16[16,256,128]{2,1,0:T(8,128)(2,1)} %shard_map.102), calls=%async_computation | async-start | bytes 2097152 | tf_op jit(solution)/shard_map/all_to_all | solution.py:260
  17.5 2.9 %collective-permute-start.6 = (bf16[256,128]{1,0:T(8,128)(2,1)S(1)}, bf16[256,128]{1,0:T(8,128)(2,1)S(1)}, u32[]{:S(2)}, u32[]{:S(2)}) collective-permute-start(bf16[256,128]{1,0:T(8,128)(2,1)S(1)} %get-tuple-element.56), channel_id=1, source_target_pairs={{0,7},{1,6},{2,5},{3,4},{4,3},{5,2},{6,1},{7,0},{8,15},{9,14},{10,... | collective-permute-start | bytes 196616 | tf_op jit(solution)/shard_map/ppermute | solution.py:263
  20.4 5.1 %collective-permute-start.7 = (bf16[256,128]{1,0:T(8,128)(2,1)S(1)}, bf16[256,128]{1,0:T(8,128)(2,1)S(1)}, u32[]{:S(2)}, u32[]{:S(2)}) collective-permute-start(bf16[256,128]{1,0:T(8,128)(2,1)S(1)} %get-tuple-element.58), channel_id=1, source_target_pairs={{0,8},{1,9},{2,10},{3,11},{4,12},{5,13},{6,14},{7,15},{8,0},{9,1},... | collective-permute-start | bytes 196616 | tf_op jit(solution)/shard_map/ppermute | solution.py:263
  25.6 4.2 %collective-permute-done.3.rest_4_ = bf16[256,128]{1,0:T(8,128)(2,1)S(1)} collective-permute-done((bf16[256,128]{1,0:T(8,128)(2,1)S(1)}, bf16[256,128]{1,0:T(8,128)(2,1)S(1)}, u32[]{:S(2)}, u32[]{:S(2)}) %collective-permute-start.3) | collective-permute-done | bytes 65568 | tf_op jit(solution)/shard_map/ppermute | solution.py:263
  29.8 2.1 %collective-permute-start.8 = (bf16[256,128]{1,0:T(8,128)(2,1)S(1)}, bf16[256,128]{1,0:T(8,128)(2,1)S(1)}, u32[]{:S(2)}, u32[]{:S(2)}) collective-permute-start(bf16[256,128]{1,0:T(8,128)(2,1)S(1)} %get-tuple-element.59), channel_id=1, source_target_pairs={{0,9},{1,8},{2,11},{3,10},{4,13},{5,12},{6,15},{7,14},{8,1},{9,0},... | collective-permute-start | bytes 196616 | tf_op jit(solution)/shard_map/ppermute | solution.py:263
  31.8 2.1 %collective-permute-start.9 = (bf16[256,128]{1,0:T(8,128)(2,1)S(1)}, bf16[256,128]{1,0:T(8,128)(2,1)S(1)}, u32[]{:S(2)}, u32[]{:S(2)}) collective-permute-start(bf16[256,128]{1,0:T(8,128)(2,1)S(1)} %get-tuple-element.60), channel_id=1, source_target_pairs={{0,10},{1,11},{2,8},{3,9},{4,14},{5,15},{6,12},{7,13},{8,2},{9,3},... | collective-permute-start | bytes 196616 | tf_op jit(solution)/shard_map/ppermute | solution.py:263
  34.0 1.7 %collective-permute-start.10 = (bf16[256,128]{1,0:T(8,128)(2,1)S(1)}, bf16[256,128]{1,0:T(8,128)(2,1)S(1)}, u32[]{:S(2)}, u32[]{:S(2)}) collective-permute-start(bf16[256,128]{1,0:T(8,128)(2,1)S(1)} %get-tuple-element.61), channel_id=1, source_target_pairs={{0,11},{1,10},{2,9},{3,8},{4,15},{5,14},{6,13},{7,12},{8,3},{9,2},... | collective-permute-start | bytes 196616 | tf_op jit(solution)/shard_map/ppermute | solution.py:263
  36.2 1.9 %collective-permute-start.11 = (bf16[256,128]{1,0:T(8,128)(2,1)S(1)}, bf16[256,128]{1,0:T(8,128)(2,1)S(1)}, u32[]{:S(2)}, u32[]{:S(2)}) collective-permute-start(bf16[256,128]{1,0:T(8,128)(2,1)S(1)} %get-tuple-element.62), channel_id=1, source_target_pairs={{0,12},{1,13},{2,14},{3,15},{4,8},{5,9},{6,10},{7,11},{8,4},{9,5},... | collective-permute-start | bytes 196616 | tf_op jit(solution)/shard_map/ppermute | solution.py:263
  38.1 5.5 %shard_map.104 = (f32[4096,128]{1,0:T(8,128)S(1)}, bf16[256,128]{1,0:T(8,128)(2,1)S(1)}, bf16[256,128]{1,0:T(8,128)(2,1)S(1)}, bf16[256,128]{1,0:T(8,128)(2,1)S(...) custom-call(s32[386]{0:T(512)S(1)} %constant_dynamic-update-slice_fu, ...), custom_call_target="tpu_custom_call" | custom-call | flops 8000000000 | bytes 4194304 | tf_op jit(solution)/shard_map/pallas_call | solution.py:293
  43.8 2.0 %collective-permute-start.13 = (bf16[256,128]{1,0:T(8,128)(2,1)S(1)}, bf16[256,128]{1,0:T(8,128)(2,1)S(1)}, u32[]{:S(2)}, u32[]{:S(2)}) collective-permute-start(bf16[256,128]{1,0:T(8,128)(2,1)S(1)} %get-tuple-element.65), channel_id=1, source_target_pairs={{0,14},{1,15},{2,12},{3,13},{4,10},{5,11},{6,8},{7,9},{8,6},{9,7},... | collective-permute-start | bytes 196616 | tf_op jit(solution)/shard_map/ppermute | solution.py:263
  47.3 2.8 %collective-permute-done.11.rest_5_ = bf16[256,128]{1,0:T(8,128)(2,1)S(1)} collective-permute-done((bf16[256,128]{1,0:T(8,128)(2,1)S(1)}, bf16[256,128]{1,0:T(8,128)(2,1)S(1)}, u32[]{:S(2)}, u32[]{:S(2)}) %collective-permute-start.11) | collective-permute-done | bytes 65568 | tf_op jit(solution)/shard_map/ppermute | solution.py:263
  50.1 3.8 %shard_map.106 = (f32[4096,128]{1,0:T(8,128)S(1)}, bf16[256,128]{1,0:T(8,128)(2,1)S(1)}, bf16[256,128]{1,0:T(8,128)(2,1)S(1)}, bf16[256,128]{1,0:T(8,128)(2,1)S(...) custom-call(s32[386]{0:T(512)S(1)} %constant_dynamic-update-slice_fusion.table_ref, ...), custom_call_target="tpu_custom_call" | custom-call | flops 5000000000 | bytes 4194304 | tf_op jit(solution)/shard_map/pallas_call | solution.py:293
  55.1 2.7 %collective-permute-start.16 = (bf16[256,128]{1,0:T(8,128)(2,1)S(1)}, bf16[256,128]{1,0:T(8,128)(2,1)S(1)}, u32[]{:S(2)}, u32[]{:S(2)}) collective-permute-start(bf16[256,128]{1,0:T(8,128)(2,1)S(1)} %get-tuple-element.80), channel_id=1, source_target_pairs={{0,9},{1,8},{2,11},{3,10},{4,13},{5,12},{6,15},{7,14},{8,1},{9,0},... | collective-permute-start | bytes 196616 | tf_op jit(solution)/shard_map/ppermute | solution.py:263
  57.8 2.1 %collective-permute-start.17 = (bf16[256,128]{1,0:T(8,128)(2,1)S(1)}, bf16[256,128]{1,0:T(8,128)(2,1)S(1)}, u32[]{:S(2)}, u32[]{:S(2)}) collective-permute-start(bf16[256,128]{1,0:T(8,128)(2,1)S(1)} %get-tuple-element.81), channel_id=1, source_target_pairs={{0,10},{1,11},{2,8},{3,9},{4,14},{5,15},{6,12},{7,13},{8,2},{9,3},... | collective-permute-start | bytes 196616 | tf_op jit(solution)/shard_map/ppermute | solution.py:263
  61.0 3.9 %shard_map.107 = (bf16[16,256,128]{2,1,0:T(8,128)(2,1)}, bf16[256,128]{1,0:T(8,128)(2,1)S(1)}, bf16[256,128]{1,0:T(8,128)(2,1)S(1)}, bf16[256,128]{1,0:T(8,128)(2,1)S(1)}) custom-call(s32[386]{0:T(512)S(1)} %constant_dynamic-update-slice_fusion.table_ref, bf16[4096,128]{1,0:T(8,128)(2,1)S(1)} %bitcast.5, f32[4096,128]{1,0:T(8,128)S(1)} %get-tuple-element.63.acc_in_ref, ...), custom_call_target="tpu_custom_call" | custom-call | tf_op jit(solution)/shard_map/pallas_call | solution.py:304
  64.8 7.3 %all-to-all-start.1 = ((bf16[16,256,128]{2,1,0:T(8,128)(2,1)}), bf16[16,256,128]{2,1,0:T(8,128)(2,1)S(1)}, u32[]{:S(2)}, u32[]{:S(2)}) async-start(bf16[16,256,128]{2,1,0:T(8,128)(2,1)} %get-tuple-element.67), calls=%async_computation.1 | async-start | bytes 2097152 | tf_op jit(solution)/shard_map/all_to_all | solution.py:316
  77.3 2.4 %collective-permute-done.21.rest_2_ = bf16[256,128]{1,0:T(8,128)(2,1)S(1)} collective-permute-done((bf16[256,128]{1,0:T(8,128)(2,1)S(1)}, bf16[256,128]{1,0:T(8,128)(2,1)S(1)}, u32[]{:S(2)}, u32[]{:S(2)}) %collective-permute-start.21) | collective-permute-done | bytes 65568 | tf_op jit(solution)/shard_map/ppermute | solution.py:263
  79.8 2.9 %collective-permute-start.26 = (bf16[256,128]{1,0:T(8,128)(2,1)S(1)}, bf16[256,128]{1,0:T(8,128)(2,1)S(1)}, u32[]{:S(2)}, u32[]{:S(2)}) collective-permute-start(bf16[256,128]{1,0:T(8,128)(2,1)S(1)} %get-tuple-element.90), channel_id=1, source_target_pairs={{0,7},{1,6},{2,5},{3,4},{4,3},{5,2},{6,1},{7,0},{8,15},{9,14},{10,... | collective-permute-start | bytes 196616 | tf_op jit(solution)/shard_map/ppermute | solution.py:263
  84.2 7.8 %collective-permute-done.23.rest_4_ = bf16[256,128]{1,0:T(8,128)(2,1)S(1)} collective-permute-done((bf16[256,128]{1,0:T(8,128)(2,1)S(1)}, bf16[256,128]{1,0:T(8,128)(2,1)S(1)}, u32[]{:S(2)}, u32[]{:S(2)}) %collective-permute-start.23) | collective-permute-done | bytes 65568 | tf_op jit(solution)/shard_map/ppermute | solution.py:263
  92.0 2.8 %collective-permute-start.28 = (bf16[256,128]{1,0:T(8,128)(2,1)S(1)}, bf16[256,128]{1,0:T(8,128)(2,1)S(1)}, u32[]{:S(2)}, u32[]{:S(2)}) collective-permute-start(bf16[256,128]{1,0:T(8,128)(2,1)S(1)} %get-tuple-element.92), channel_id=1, source_target_pairs={{0,14},{1,15},{2,12},{3,13},{4,10},{5,11},{6,8},{7,9},{8,6},{9,7},... | collective-permute-start | bytes 196616 | tf_op jit(solution)/shard_map/ppermute | solution.py:263
  94.8 1.7 %collective-permute-start.29 = (bf16[256,128]{1,0:T(8,128)(2,1)S(1)}, bf16[256,128]{1,0:T(8,128)(2,1)S(1)}, u32[]{:S(2)}, u32[]{:S(2)}) collective-permute-start(bf16[256,128]{1,0:T(8,128)(2,1)S(1)} %get-tuple-element.93), channel_id=1, source_target_pairs={{0,15},{1,14},{2,13},{3,12},{4,11},{5,10},{6,9},{7,8},{8,7},{9,6},... | collective-permute-start | bytes 196616 | tf_op jit(solution)/shard_map/ppermute | solution.py:263
  96.5 1.9 %collective-permute-done.26.rest_7_ = bf16[256,128]{1,0:T(8,128)(2,1)S(1)} collective-permute-done((bf16[256,128]{1,0:T(8,128)(2,1)S(1)}, bf16[256,128]{1,0:T(8,128)(2,1)S(1)}, u32[]{:S(2)}, u32[]{:S(2)}) %collective-permute-start.26) | collective-permute-done | bytes 65568 | tf_op jit(solution)/shard_map/ppermute | solution.py:263
  98.4 4.7 %collective-permute-done.27.rest_13_ = bf16[256,128]{1,0:T(8,128)(2,1)S(1)} collective-permute-done((bf16[256,128]{1,0:T(8,128)(2,1)S(1)}, bf16[256,128]{1,0:T(8,128)(2,1)S(1)}, u32[]{:S(2)}, u32[]{:S(2)}) %collective-permute-start.27) | collective-permute-done | bytes 65568 | tf_op jit(solution)/shard_map/ppermute | solution.py:263
  (63 shorter events, 23.6 us)
Async XLA Ops:
  3.1 35.0 %all-to-all-start = ((bf16[16,256,128]{2,1,0:T(8,128)(2,1)}), bf16[16,256,128]{2,1,0:T(8,128)(2,1)S(1)}, u32[]{:S(2)}, u32[]{:S(2)}) async-start(bf16[16,256,128]{2,1,0:T(8,128)(2,1)} %shard_map.102), calls=%async_computation | async-start | bytes 2097152 | tf_op jit(solution)/shard_map/all_to_all | solution.py:260
  13.2 16.6 %collective-permute-start.3 = (bf16[256,128]{1,0:T(8,128)(2,1)S(1)}, bf16[256,128]{1,0:T(8,128)(2,1)S(1)}, u32[]{:S(2)}, u32[]{:S(2)}) collective-permute-start(bf16[256,128]{1,0:T(8,128)(2,1)S(1)} %get-tuple-element.53), channel_id=1, source_target_pairs={{0,4},{1,5},{2,6},{3,7},{4,0},{5,1},{6,2},{7,3},{8,12},{9,13},{10,... | collective-permute-start | bytes 196616 | tf_op jit(solution)/shard_map/ppermute | solution.py:263
  13.2 18.6 %collective-permute-start.4 = (bf16[256,128]{1,0:T(8,128)(2,1)S(1)}, bf16[256,128]{1,0:T(8,128)(2,1)S(1)}, u32[]{:S(2)}, u32[]{:S(2)}) collective-permute-start(bf16[256,128]{1,0:T(8,128)(2,1)S(1)} %get-tuple-element.54), channel_id=1, source_target_pairs={{0,5},{1,4},{2,7},{3,6},{4,1},{5,0},{6,3},{7,2},{8,13},{9,12},{10,... | collective-permute-start | bytes 196616 | tf_op jit(solution)/shard_map/ppermute | solution.py:263
  16.0 18.0 %collective-permute-start.5 = (bf16[256,128]{1,0:T(8,128)(2,1)S(1)}, bf16[256,128]{1,0:T(8,128)(2,1)S(1)}, u32[]{:S(2)}, u32[]{:S(2)}) collective-permute-start(bf16[256,128]{1,0:T(8,128)(2,1)S(1)} %get-tuple-element.55), channel_id=1, source_target_pairs={{0,6},{1,7},{2,4},{3,5},{4,2},{5,3},{6,0},{7,1},{8,14},{9,15},{10,... | collective-permute-start | bytes 196616 | tf_op jit(solution)/shard_map/ppermute | solution.py:263
  17.5 18.6 %collective-permute-start.6 = (bf16[256,128]{1,0:T(8,128)(2,1)S(1)}, bf16[256,128]{1,0:T(8,128)(2,1)S(1)}, u32[]{:S(2)}, u32[]{:S(2)}) collective-permute-start(bf16[256,128]{1,0:T(8,128)(2,1)S(1)} %get-tuple-element.56), channel_id=1, source_target_pairs={{0,7},{1,6},{2,5},{3,4},{4,3},{5,2},{6,1},{7,0},{8,15},{9,14},{10,... | collective-permute-start | bytes 196616 | tf_op jit(solution)/shard_map/ppermute | solution.py:263
  20.4 23.2 %collective-permute-start.7 = (bf16[256,128]{1,0:T(8,128)(2,1)S(1)}, bf16[256,128]{1,0:T(8,128)(2,1)S(1)}, u32[]{:S(2)}, u32[]{:S(2)}) collective-permute-start(bf16[256,128]{1,0:T(8,128)(2,1)S(1)} %get-tuple-element.58), channel_id=1, source_target_pairs={{0,8},{1,9},{2,10},{3,11},{4,12},{5,13},{6,14},{7,15},{8,0},{9,1},... | collective-permute-start | bytes 196616 | tf_op jit(solution)/shard_map/ppermute | solution.py:263
  29.8 14.0 %collective-permute-start.8 = (bf16[256,128]{1,0:T(8,128)(2,1)S(1)}, bf16[256,128]{1,0:T(8,128)(2,1)S(1)}, u32[]{:S(2)}, u32[]{:S(2)}) collective-permute-start(bf16[256,128]{1,0:T(8,128)(2,1)S(1)} %get-tuple-element.59), channel_id=1, source_target_pairs={{0,9},{1,8},{2,11},{3,10},{4,13},{5,12},{6,15},{7,14},{8,1},{9,0},... | collective-permute-start | bytes 196616 | tf_op jit(solution)/shard_map/ppermute | solution.py:263
  31.8 13.9 %collective-permute-start.9 = (bf16[256,128]{1,0:T(8,128)(2,1)S(1)}, bf16[256,128]{1,0:T(8,128)(2,1)S(1)}, u32[]{:S(2)}, u32[]{:S(2)}) collective-permute-start(bf16[256,128]{1,0:T(8,128)(2,1)S(1)} %get-tuple-element.60), channel_id=1, source_target_pairs={{0,10},{1,11},{2,8},{3,9},{4,14},{5,15},{6,12},{7,13},{8,2},{9,3},... | collective-permute-start | bytes 196616 | tf_op jit(solution)/shard_map/ppermute | solution.py:263
  34.0 13.3 %collective-permute-start.10 = (bf16[256,128]{1,0:T(8,128)(2,1)S(1)}, bf16[256,128]{1,0:T(8,128)(2,1)S(1)}, u32[]{:S(2)}, u32[]{:S(2)}) collective-permute-start(bf16[256,128]{1,0:T(8,128)(2,1)S(1)} %get-tuple-element.61), channel_id=1, source_target_pairs={{0,11},{1,10},{2,9},{3,8},{4,15},{5,14},{6,13},{7,12},{8,3},{9,2},... | collective-permute-start | bytes 196616 | tf_op jit(solution)/shard_map/ppermute | solution.py:263
  36.2 13.9 %collective-permute-start.11 = (bf16[256,128]{1,0:T(8,128)(2,1)S(1)}, bf16[256,128]{1,0:T(8,128)(2,1)S(1)}, u32[]{:S(2)}, u32[]{:S(2)}) collective-permute-start(bf16[256,128]{1,0:T(8,128)(2,1)S(1)} %get-tuple-element.62), channel_id=1, source_target_pairs={{0,12},{1,13},{2,14},{3,15},{4,8},{5,9},{6,10},{7,11},{8,4},{9,5},... | collective-permute-start | bytes 196616 | tf_op jit(solution)/shard_map/ppermute | solution.py:263
  43.6 14.2 %collective-permute-start.12 = (bf16[256,128]{1,0:T(8,128)(2,1)S(1)}, bf16[256,128]{1,0:T(8,128)(2,1)S(1)}, u32[]{:S(2)}, u32[]{:S(2)}) collective-permute-start(bf16[256,128]{1,0:T(8,128)(2,1)S(1)} %get-tuple-element.64), channel_id=1, source_target_pairs={{0,13},{1,12},{2,15},{3,14},{4,9},{5,8},{6,11},{7,10},{8,5},{9,4},... | collective-permute-start | bytes 196616 | tf_op jit(solution)/shard_map/ppermute | solution.py:263
  43.8 16.2 %collective-permute-start.13 = (bf16[256,128]{1,0:T(8,128)(2,1)S(1)}, bf16[256,128]{1,0:T(8,128)(2,1)S(1)}, u32[]{:S(2)}, u32[]{:S(2)}) collective-permute-start(bf16[256,128]{1,0:T(8,128)(2,1)S(1)} %get-tuple-element.65), channel_id=1, source_target_pairs={{0,14},{1,15},{2,12},{3,13},{4,10},{5,11},{6,8},{7,9},{8,6},{9,7},... | collective-permute-start | bytes 196616 | tf_op jit(solution)/shard_map/ppermute | solution.py:263
  45.7 14.5 %collective-permute-start.14 = (bf16[256,128]{1,0:T(8,128)(2,1)S(1)}, bf16[256,128]{1,0:T(8,128)(2,1)S(1)}, u32[]{:S(2)}, u32[]{:S(2)}) collective-permute-start(bf16[256,128]{1,0:T(8,128)(2,1)S(1)} %get-tuple-element.66), channel_id=1, source_target_pairs={{0,15},{1,14},{2,13},{3,12},{4,11},{5,10},{6,9},{7,8},{8,7},{9,6},... | collective-permute-start | bytes 196616 | tf_op jit(solution)/shard_map/ppermute | solution.py:263
  53.9 18.2 %collective-permute-start.15 = (bf16[256,128]{1,0:T(8,128)(2,1)S(1)}, bf16[256,128]{1,0:T(8,128)(2,1)S(1)}, u32[]{:S(2)}, u32[]{:S(2)}) collective-permute-start(bf16[256,128]{1,0:T(8,128)(2,1)S(1)} %get-tuple-element.79), channel_id=1, source_target_pairs={{0,8},{1,9},{2,10},{3,11},{4,12},{5,13},{6,14},{7,15},{8,0},{9,1},... | collective-permute-start | bytes 196616 | tf_op jit(solution)/shard_map/ppermute | solution.py:263
  55.1 17.0 %collective-permute-start.16 = (bf16[256,128]{1,0:T(8,128)(2,1)S(1)}, bf16[256,128]{1,0:T(8,128)(2,1)S(1)}, u32[]{:S(2)}, u32[]{:S(2)}) collective-permute-start(bf16[256,128]{1,0:T(8,128)(2,1)S(1)} %get-tuple-element.80), channel_id=1, source_target_pairs={{0,9},{1,8},{2,11},{3,10},{4,13},{5,12},{6,15},{7,14},{8,1},{9,0},... | collective-permute-start | bytes 196616 | tf_op jit(solution)/shard_map/ppermute | solution.py:263
  57.8 14.3 %collective-permute-start.17 = (bf16[256,128]{1,0:T(8,128)(2,1)S(1)}, bf16[256,128]{1,0:T(8,128)(2,1)S(1)}, u32[]{:S(2)}, u32[]{:S(2)}) collective-permute-start(bf16[256,128]{1,0:T(8,128)(2,1)S(1)} %get-tuple-element.81), channel_id=1, source_target_pairs={{0,10},{1,11},{2,8},{3,9},{4,14},{5,15},{6,12},{7,13},{8,2},{9,3},... | collective-permute-start | bytes 196616 | tf_op jit(solution)/shard_map/ppermute | solution.py:263
  59.9 12.2 %collective-permute-start.18 = (bf16[256,128]{1,0:T(8,128)(2,1)S(1)}, bf16[256,128]{1,0:T(8,128)(2,1)S(1)}, u32[]{:S(2)}, u32[]{:S(2)}) collective-permute-start(bf16[256,128]{1,0:T(8,128)(2,1)S(1)} %get-tuple-element.82), channel_id=1, source_target_pairs={{0,11},{1,10},{2,9},{3,8},{4,15},{5,14},{6,13},{7,12},{8,3},{9,2},... | collective-permute-start | bytes 196616 | tf_op jit(solution)/shard_map/ppermute | solution.py:263
  64.8 41.5 %all-to-all-start.1 = ((bf16[16,256,128]{2,1,0:T(8,128)(2,1)}), bf16[16,256,128]{2,1,0:T(8,128)(2,1)S(1)}, u32[]{:S(2)}, u32[]{:S(2)}) async-start(bf16[16,256,128]{2,1,0:T(8,128)(2,1)} %get-tuple-element.67), calls=%async_computation.1 | async-start | bytes 2097152 | tf_op jit(solution)/shard_map/all_to_all | solution.py:316
  74.4 17.5 %collective-permute-start.23 = (bf16[256,128]{1,0:T(8,128)(2,1)S(1)}, bf16[256,128]{1,0:T(8,128)(2,1)S(1)}, u32[]{:S(2)}, u32[]{:S(2)}) collective-permute-start(bf16[256,128]{1,0:T(8,128)(2,1)S(1)} %get-tuple-element.87), channel_id=1, source_target_pairs={{0,4},{1,5},{2,6},{3,7},{4,0},{5,1},{6,2},{7,3},{8,12},{9,13},{10,... | collective-permute-start | bytes 196616 | tf_op jit(solution)/shard_map/ppermute | solution.py:263
  75.3 19.5 %collective-permute-start.24 = (bf16[256,128]{1,0:T(8,128)(2,1)S(1)}, bf16[256,128]{1,0:T(8,128)(2,1)S(1)}, u32[]{:S(2)}, u32[]{:S(2)}) collective-permute-start(bf16[256,128]{1,0:T(8,128)(2,1)S(1)} %get-tuple-element.88), channel_id=1, source_target_pairs={{0,5},{1,4},{2,7},{3,6},{4,1},{5,0},{6,3},{7,2},{8,13},{9,12},{10,... | collective-permute-start | bytes 196616 | tf_op jit(solution)/shard_map/ppermute | solution.py:263
  76.1 20.3 %collective-permute-start.25 = (bf16[256,128]{1,0:T(8,128)(2,1)S(1)}, bf16[256,128]{1,0:T(8,128)(2,1)S(1)}, u32[]{:S(2)}, u32[]{:S(2)}) collective-permute-start(bf16[256,128]{1,0:T(8,128)(2,1)S(1)} %get-tuple-element.89), channel_id=1, source_target_pairs={{0,6},{1,7},{2,4},{3,5},{4,2},{5,3},{6,0},{7,1},{8,14},{9,15},{10,... | collective-permute-start | bytes 196616 | tf_op jit(solution)/shard_map/ppermute | solution.py:263
  79.8 18.6 %collective-permute-start.26 = (bf16[256,128]{1,0:T(8,128)(2,1)S(1)}, bf16[256,128]{1,0:T(8,128)(2,1)S(1)}, u32[]{:S(2)}, u32[]{:S(2)}) collective-permute-start(bf16[256,128]{1,0:T(8,128)(2,1)S(1)} %get-tuple-element.90), channel_id=1, source_target_pairs={{0,7},{1,6},{2,5},{3,4},{4,3},{5,2},{6,1},{7,0},{8,15},{9,14},{10,... | collective-permute-start | bytes 196616 | tf_op jit(solution)/shard_map/ppermute | solution.py:263
  82.6 20.5 %collective-permute-start.27 = (bf16[256,128]{1,0:T(8,128)(2,1)S(1)}, bf16[256,128]{1,0:T(8,128)(2,1)S(1)}, u32[]{:S(2)}, u32[]{:S(2)}) collective-permute-start(bf16[256,128]{1,0:T(8,128)(2,1)S(1)} %get-tuple-element.91), channel_id=1, source_target_pairs={{0,13},{1,12},{2,15},{3,14},{4,9},{5,8},{6,11},{7,10},{8,5},{9,4},... | collective-permute-start | bytes 196616 | tf_op jit(solution)/shard_map/ppermute | solution.py:263
  92.0 12.8 %collective-permute-start.28 = (bf16[256,128]{1,0:T(8,128)(2,1)S(1)}, bf16[256,128]{1,0:T(8,128)(2,1)S(1)}, u32[]{:S(2)}, u32[]{:S(2)}) collective-permute-start(bf16[256,128]{1,0:T(8,128)(2,1)S(1)} %get-tuple-element.92), channel_id=1, source_target_pairs={{0,14},{1,15},{2,12},{3,13},{4,10},{5,11},{6,8},{7,9},{8,6},{9,7},... | collective-permute-start | bytes 196616 | tf_op jit(solution)/shard_map/ppermute | solution.py:263
  (13 other events, 123.8 us)
